TPU v7x, 32 devices: a whole 2x2x4 slice. The times are simulated.
32 devices in a mesh: dp: 16 (over z, y, x), tensor: 2 (over core).
Axes of the slice: x: 2, y: 2, z: 4, core: 2. Of those that a mesh axis runs over, the one named last changes fastest.
Arguments:
- tokens: bfloat16 [2, 128, 197, 512], P(None, 'dp'), may hold values from -6 to 6
- held: int32 [2, 16], P(None, 'dp'), may hold values from 1 to 8, as said below
- routes: int32 [2, 128, 197, 2], P(None, 'dp'), may hold values from 0 to 7, all different within a row; in each aligned block of 1576 rows (0 to 1575, 1576 to 3151, ..., all dimensions but the last counted through in order) at most 630 rows name the same one
- ln1_gain: bfloat16 [512], P('dp'), may hold values from 0.099609375 to 1.8984375
- qkv_weight: bfloat16 [3, 512, 512], P(None, 'dp', 'tensor'), may hold values from -0.25 to 0.25
- out_weight: bfloat16 [512, 512], P('tensor', 'dp'), may hold values from -1 to 1
- ln2_gain: bfloat16 [512], P('dp'), may hold values from 0.099609375 to 1.8984375
- router_weight: bfloat16 [512, 8], P('dp'), may hold values from -0.125 to 0.125
- expert_in: bfloat16 [8, 512, 2048], P(None, 'dp', 'tensor'), may hold values from -0.25 to 0.25
- expert_out: bfloat16 [8, 2048, 512], P(None, 'tensor', 'dp'), may hold values from -0.1875 to 0.1875
- grad_out: bfloat16 [2, 128, 197, 512], P(None, 'dp'), may hold values from -6 to 6
Outputs:
- block_out: bfloat16 [2, 128, 197, 512], P(None, 'dp')
- grad_tokens: bfloat16 [2, 128, 197, 512], P(None, 'dp')
- grad_ln1_gain: float32 [512], P('dp')
- grad_qkv: float32 [3, 512, 512], P(None, 'dp', 'tensor')
- grad_out_weight: float32 [512, 512], P('tensor', 'dp')
- grad_ln2_gain: float32 [512], P('dp')
- grad_router: float32 [512, 8], P('dp')
- grad_expert_in: float32 [8, 512, 2048], P(None, 'dp', 'tensor')
- grad_expert_out: float32 [8, 2048, 512], P(None, 'tensor', 'dp')
Inputs may be any that keep to these rules, and one draw needn't show every extreme that they name: `held`: the live images of a group are its first ones; some group of some micro-batch holds 8 and some holds 1. `routes`: the two experts of a token differ; among the tokens of one index of dp in one micro-batch no expert is named more than 630 times, a bound that some block reaches in some of them.
All inputs are finite; a program needn't handle non-finite values.
Results may differ from a plain program's by a relative error of at most 0.012.
Values may be sent and summed in bfloat16 or wider, within the bound.
No kernel may reach another device: no remote copies, remote signals or barrier semaphores. Data moves between devices by JAX's collectives and lax.ppermute only.
A program may use at most 384 MiB of HBM per device.

v0:
```python
import jax
import jax.numpy as jnp
from jax import lax
from jax.sharding import PartitionSpec as P

HD = 64
CAP = 630


def layer_stats(values):
    centre = values - jnp.mean(values, -1, keepdims=True)
    factor = lax.rsqrt(jnp.mean(centre * centre, -1, keepdims=True) + 1e-06)
    return (centre * factor, factor)


def norm_back(grad_normed, normed, factor):
    return factor * (
        grad_normed
        - jnp.mean(grad_normed, -1, keepdims=True)
        - normed * jnp.mean(grad_normed * normed, -1, keepdims=True)
    )


def gelu_slope(values):
    return (
        0.5 * (1.0 + lax.erf(values * 0.7071067811865476))
        + values * jnp.exp(-0.5 * values * values) * 0.3989422804014327
    )


def route_slots(chosen, experts):
    flat = chosen.reshape(-1)
    onehot = (flat[:, None] == jnp.arange(experts, dtype=jnp.int32)[None, :]).astype(jnp.int32)
    before = jnp.cumsum(onehot, 0) - onehot
    place = jnp.sum(before * onehot, 1)
    owner = (
        jnp.zeros((experts, CAP), jnp.int32)
        .at[flat, place]
        .set(jnp.arange(flat.shape[0], dtype=jnp.int32) // 2)
    )
    return (flat, place, owner)


def body(
    tokens,
    held,
    routes,
    ln1_gain,
    qkv_weight,
    out_weight,
    ln2_gain,
    router_weight,
    expert_in,
    expert_out,
    grad_out,
):
    f32 = jnp.float32
    bf16 = jnp.bfloat16
    gathered = (
        lax.all_gather(ln1_gain, "dp", axis=0, tiled=True),
        lax.all_gather(qkv_weight, "dp", axis=1, tiled=True),
        lax.all_gather(out_weight, "dp", axis=1, tiled=True),
        lax.all_gather(ln2_gain, "dp", axis=0, tiled=True),
        lax.all_gather(router_weight, "dp", axis=0, tiled=True),
        lax.all_gather(expert_in, "dp", axis=1, tiled=True),
        lax.all_gather(expert_out, "dp", axis=2, tiled=True),
    )
    micro, slots, seq, width = tokens.shape
    rows = slots * seq
    local = qkv_weight.shape[2]
    heads_here = local // HD
    experts = expert_in.shape[0]
    factor_scale = HD ** (-0.5)
    gain1 = gathered[0].astype(f32)
    w_qkv = gathered[1]
    w_out = gathered[2]
    gain2 = gathered[3].astype(f32)
    w_router = gathered[4]
    w_in = gathered[5]
    w_back = gathered[6]
    outputs = []
    saved = []
    for step in range(micro):
        live = (jnp.arange(slots, dtype=jnp.int32) < held[step, 0]).astype(f32)
        live_rows = jnp.broadcast_to(live[:, None], (slots, seq)).reshape(rows, 1)
        inputs = tokens[step].reshape(rows, width).astype(f32)
        normed1, factor1 = layer_stats(inputs)
        act1 = (normed1 * gain1).astype(bf16)
        proj = jnp.einsum("rd,jdc->jrc", act1, w_qkv, preferred_element_type=f32).astype(bf16)
        split = proj.reshape(3, slots, seq, heads_here, HD)
        query, key_part, value = (split[0], split[1], split[2])
        scores = factor_scale * jnp.einsum(
            "ishd,ithd->ihst", query, key_part, preferred_element_type=f32
        )
        top = jax.nn.logsumexp(scores, -1, keepdims=True)
        probs = jnp.exp(scores - top).astype(bf16)
        attended = (
            jnp.einsum("ihst,ithd->ishd", probs, value, preferred_element_type=f32)
            .astype(bf16)
            .reshape(rows, local)
        )
        partial_attn = jnp.dot(attended, w_out, preferred_element_type=f32)
        branch = lax.psum(partial_attn, "tensor")
        middle = inputs + branch
        normed2, factor2 = layer_stats(middle)
        act2 = (normed2 * gain2).astype(bf16)
        logits = jnp.dot(act2, w_router, preferred_element_type=f32)
        chosen = routes[step].reshape(rows, 2)
        gates = jax.nn.softmax(jnp.take_along_axis(logits, chosen, 1), -1)
        flat, place, owner = route_slots(chosen, experts)
        expert_rows = act2[owner]
        inner = jnp.einsum("ecd,edf->ecf", expert_rows, w_in, preferred_element_type=f32)
        hidden = jax.nn.gelu(inner, approximate=False).astype(bf16)
        result = jnp.einsum("ecf,efd->ecd", hidden, w_back, preferred_element_type=f32)
        per_route = result[flat, place].reshape(rows, 2, width)
        mixed_part = jnp.sum(gates[:, :, None] * per_route, 1)
        mixed = lax.psum(mixed_part.astype(jnp.bfloat16), "tensor").astype(jnp.float32)
        finished = ((middle + mixed) * live_rows).astype(bf16)
        outputs.append(finished.reshape(slots, seq, width))
        saved.append(
            (
                live_rows,
                normed1,
                factor1,
                act1,
                query,
                key_part,
                value,
                top,
                attended,
                normed2,
                factor2,
                act2,
                chosen,
                gates,
                flat,
                place,
                owner,
                expert_rows,
                inner,
                hidden,
                per_route,
            )
        )
    again = (
        lax.all_gather(ln1_gain, "dp", axis=0, tiled=True),
        lax.all_gather(qkv_weight, "dp", axis=1, tiled=True),
        lax.all_gather(out_weight, "dp", axis=1, tiled=True),
        lax.all_gather(ln2_gain, "dp", axis=0, tiled=True),
        lax.all_gather(router_weight, "dp", axis=0, tiled=True),
        lax.all_gather(expert_in, "dp", axis=1, tiled=True),
        lax.all_gather(expert_out, "dp", axis=2, tiled=True),
    )
    gain1 = again[0].astype(f32)
    w_qkv = again[1]
    w_out = again[2]
    gain2 = again[3].astype(f32)
    router_full = again[4].astype(f32)
    w_in = again[5]
    w_back = again[6]
    totals = None
    grad_inputs = []
    for step in range(micro):
        (
            live_rows,
            normed1,
            factor1,
            act1,
            query,
            key_part,
            value,
            top,
            attended,
            normed2,
            factor2,
            act2,
            chosen,
            gates,
            flat,
            place,
            owner,
            expert_rows,
            inner,
            hidden,
            per_route,
        ) = saved[step]
        incoming = grad_out[step].reshape(rows, width).astype(f32) * live_rows
        gate_table = jnp.zeros((experts, CAP), f32).at[flat, place].set(gates.reshape(-1))
        scaled = (gate_table[:, :, None] * incoming[owner]).astype(bf16)
        grad_back = jnp.einsum("ecf,ecd->efd", hidden, scaled, preferred_element_type=f32)
        grad_hidden = jnp.einsum("ecd,efd->ecf", scaled, w_back, preferred_element_type=f32)
        grad_inner = (grad_hidden * gelu_slope(inner)).astype(bf16)
        grad_in = jnp.einsum("ecd,ecf->edf", expert_rows, grad_inner, preferred_element_type=f32)
        grad_rows = jnp.einsum("ecf,edf->ecd", grad_inner, w_in, preferred_element_type=f32)
        grad_act2_part = jnp.sum(grad_rows[flat, place].reshape(rows, 2, width), 1)
        gate_part = jnp.sum(incoming[:, None, :] * per_route, -1)
        grad_act2_sum, gate_grad = lax.psum((grad_act2_part, gate_part), "tensor")
        grad_picked = gates * (gate_grad - jnp.sum(gates * gate_grad, -1, keepdims=True))
        expert_ids = jnp.arange(experts, dtype=jnp.int32)[None, None, :]
        grad_logits = jnp.sum(
            grad_picked[:, :, None] * (chosen[:, :, None] == expert_ids).astype(f32), 1
        )
        grad_router = jnp.dot(act2.astype(f32).T, grad_logits, precision=lax.Precision.HIGHEST)
        grad_act2 = grad_act2_sum + jnp.dot(
            grad_logits, router_full.T, precision=lax.Precision.HIGHEST
        )
        grad_gain2 = jnp.sum(grad_act2 * normed2, 0)
        grad_middle = incoming + norm_back(grad_act2 * gain2, normed2, factor2)
        grad_branch = grad_middle.astype(bf16)
        grad_wout = jnp.einsum("rc,rd->cd", attended, grad_branch, preferred_element_type=f32)
        grad_att = (
            jnp.einsum("rd,cd->rc", grad_branch, w_out, preferred_element_type=f32)
            .astype(bf16)
            .reshape(slots, seq, heads_here, HD)
        )
        scores = factor_scale * jnp.einsum(
            "ishd,ithd->ihst", query, key_part, preferred_element_type=f32
        )
        probs = jnp.exp(scores - top)
        grad_value = jnp.einsum(
            "ihst,ishd->ithd", probs.astype(bf16), grad_att, preferred_element_type=f32
        ).astype(bf16)
        grad_probs = jnp.einsum("ishd,ithd->ihst", grad_att, value, preferred_element_type=f32)
        grad_scores = (
            probs * (grad_probs - jnp.sum(grad_probs * probs, -1, keepdims=True))
        ).astype(bf16)
        grad_query = (
            factor_scale
            * jnp.einsum("ihst,ithd->ishd", grad_scores, key_part, preferred_element_type=f32)
        ).astype(bf16)
        grad_key = (
            factor_scale
            * jnp.einsum("ihst,ishd->ithd", grad_scores, query, preferred_element_type=f32)
        ).astype(bf16)
        grad_proj = jnp.stack([grad_query, grad_key, grad_value]).reshape(3, rows, local)
        grad_qkv = jnp.einsum("rd,jrc->jdc", act1, grad_proj, preferred_element_type=f32)
        grad_act1_part = jnp.einsum("jrc,jdc->rd", grad_proj, w_qkv, preferred_element_type=f32)
        grad_act1 = lax.psum(grad_act1_part, "tensor")
        grad_gain1 = jnp.sum(grad_act1 * normed1, 0)
        grad_total = grad_middle + norm_back(grad_act1 * gain1, normed1, factor1)
        grad_low = grad_total.astype(bf16)
        grad_inputs.append(grad_low.reshape(slots, seq, width))
        current = (grad_gain1, grad_qkv, grad_wout, grad_gain2, grad_router, grad_in, grad_back)
        if totals is None:
            totals = tuple(current)
        else:
            totals = tuple((a + b for a, b in zip(totals, current)))
    shards = (
        lax.psum_scatter(totals[0], "dp", scatter_dimension=0, tiled=True),
        lax.psum_scatter(totals[1], "dp", scatter_dimension=1, tiled=True),
        lax.psum_scatter(totals[2], "dp", scatter_dimension=1, tiled=True),
        lax.psum_scatter(totals[3], "dp", scatter_dimension=0, tiled=True),
        lax.psum_scatter(totals[4], "dp", scatter_dimension=0, tiled=True),
        lax.psum_scatter(totals[5], "dp", scatter_dimension=1, tiled=True),
        lax.psum_scatter(totals[6], "dp", scatter_dimension=2, tiled=True),
    )
    block_out = jnp.stack(outputs)
    grad_tokens = jnp.stack(grad_inputs)
    return (
        block_out,
        grad_tokens,
        shards[0],
        shards[1],
        shards[2],
        shards[3],
        shards[4],
        shards[5],
        shards[6],
    )


def solution(mesh):
    placed = (
        P(None, "dp", None, None),
        P(None, "dp"),
        P(None, "dp", None, None),
        P("dp"),
        P(None, "dp", "tensor"),
        P("tensor", "dp"),
        P("dp"),
        P("dp", None),
        P(None, "dp", "tensor"),
        P(None, "tensor", "dp"),
        P(None, "dp", None, None),
    )
    return jax.shard_map(
        body,
        mesh=mesh,
        in_specs=placed,
        out_specs=(
            P(None, "dp", None, None),
            P(None, "dp", None, None),
            P("dp"),
            P(None, "dp", "tensor"),
            P("tensor", "dp"),
            P("dp"),
            P("dp", None),
            P(None, "dp", "tensor"),
            P(None, "tensor", "dp"),
        ),
        check_vma=False,
    )
```

profile of v0, /device:TPU:0, one launch (start us, length us, event | category | flops | bytes accessed | tf_op | source)
XLA Modules:
  0.0 2296.4 jit_solution(15278771614918574339)
XLA Ops:
  17.3 44.1 %all-reduce.12 = (bf16[512]{0:T(512)(128)(2,1)S(1)}, bf16[512]{0:T(512)(128)(2,1)}) all-reduce(bf16[512]{0:T(512)(128)(2,1)S(1)} %dynamic-update-slice, bf16[512]{0:T(512)(128)(2,1)S(1)} %dynamic-update-slice.1), channel_id=1, replica_groups=mesh['dp'=16,'tensor'=2] {'dp'}, use_global_device_ids=true, to_apply=%add.2 | all-reduce | flops 1024 | bytes 4096
  61.4 6.1 multiply_reduce_fusion.19
  68.7 37.4 %all_gather.30 = bf16[256,512]{0,1:T(8,128)(2,1)S(1)} all-gather(bf16[256,32]{0,1:T(8,128)(2,1)} %param.18), channel_id=1, replica_groups=mesh['dp'=16,'tensor'=2] {'dp'}, dimensions={1}, use_global_device_ids=true | all-gather | bytes 278528 | tf_op jit(solution)/shard_map/all_gather | solution.py:62
  106.1 44.5 %all_gather.29 = bf16[3,512,256]{2,1,0:T(8,128)(2,1)} all-gather(bf16[3,32,256]{2,1,0:T(8,128)(2,1)} %param.17), channel_id=1, replica_groups=mesh['dp'=16,'tensor'=2] {'dp'}, dimensions={1}, use_global_device_ids=true | all-gather | bytes 835584 | tf_op jit(solution)/shard_map/all_gather | solution.py:61
  150.6 5.5 copy.295
  235.7 36.6 %all-gather = bf16[16,32,8]{1,2,0:T(8,128)(2,1)S(1)} all-gather(bf16[1,32,8]{1,2,0:T(8,128)(2,1)S(1)} %bitcast.168), channel_id=1, replica_groups=mesh['dp'=16,'tensor'=2] {'dp'}, dimensions={0}, use_global_device_ids=true | all-gather | bytes 8704 | tf_op jit(solution)/shard_map/all_gather | solution.py:64
  281.2 15.9 scatter_custom_fusion.1
  297.2 16.0 scatter_custom_fusion
  337.8 21.0 gather_fusion.6
  358.8 10.6 reshape.536
  371.6 21.0 gather_fusion.4
  392.6 10.6 reshape.522
  413.6 21.3 gather_fusion.2
  435.4 30.0 %gather_fusion.9 = f32[3152]{0:T(1024)S(1)} fusion(f32[1576,8]{0,1:T(8,128)S(1)} %fusion.99, s32[3152]{0:T(1024)S(1)} %reshape.609), kind=kCustom, calls=%fused_computation.1.clone | custom fusion | bytes 50432 | tf_op jit(solution)/shard_map/jit(take_along_axis)/gather | solution.py:109
  467.1 23.2 %gather_fusion = bf16[5040,512]{1,0:T(8,128)(2,1)} fusion(bf16[1576,512]{1,0:T(8,128)(2,1)} %get-tuple-element.127, s32[5120]{0:T(1024)S(1)} %copy-done.91), kind=kCustom, calls=%fused_computation.2 | custom fusion | bytes 10342080 | tf_op jit(solution)/shard_map/gather | solution.py:111
  490.8 30.0 %gather_fusion.8 = f32[3152]{0:T(1024)S(1)} fusion(f32[1576,8]{0,1:T(8,128)S(1)} %fusion.96, s32[3152]{0:T(1024)S(1)} %copy-done.12), kind=kCustom, calls=%fused_computation.clone | custom fusion | bytes 50432 | tf_op jit(solution)/shard_map/jit(take_along_axis)/gather | solution.py:109
  526.0 16.4 scatter_custom_fusion.3
  544.0 16.0 scatter_custom_fusion.2
  560.2 4.7 reshape.494
  564.8 4.7 reshape.508
  569.5 20.1 fusion.33
  589.6 19.7 fusion.17
  609.2 13.5 fusion.102
  622.7 13.7 copy.355
  636.4 52.3 %gather_fusion.7 = f32[3152,512]{1,0:T(8,128)} fusion(f32[8,630,512]{2,0,1:T(8,128)} %copy.355, s32[3152]{0:T(1024)S(1)} %copy-done.9), kind=kCustom, calls=%fused_computation.9 | custom fusion | bytes 12935808 | tf_op jit(solution)/shard_map/gather | solution.py:195
  688.7 8.5 reshape.456
  697.2 28.2 %reduce_sum.373 = f32[1576,512]{1,0:T(8,128)} reduce(f32[1576,2,512]{2,1,0:T(2,128)} %reshape.456, f32[]{:T(128)} %constant.51.clone.1), dimensions={1}, to_apply=%region_44.46 | reduce | flops 806912 | bytes 9682948 | tf_op jit(solution)/shard_map/reduce_sum | solution.py:195
  725.4 19.4 fusion.32
  744.7 20.0 fusion.11
  764.8 13.4 fusion.101
  778.1 13.8 copy.337
  792.0 52.4 %gather_fusion.5 = f32[3152,512]{1,0:T(8,128)} fusion(f32[8,630,512]{2,0,1:T(8,128)} %copy.337, s32[3152]{0:T(1024)S(1)} %copy-done.8), kind=kCustom, calls=%fused_computation.7 | custom fusion | bytes 12935808 | tf_op jit(solution)/shard_map/gather | solution.py:195
  844.4 8.3 reshape.453
  852.7 28.2 %reduce_sum.364 = f32[1576,512]{1,0:T(8,128)} reduce(f32[1576,2,512]{2,1,0:T(2,128)} %reshape.453, f32[]{:T(128)} %constant.51.clone.1), dimensions={1}, to_apply=%region_31.33 | reduce | flops 806912 | bytes 9682948 | tf_op jit(solution)/shard_map/reduce_sum | solution.py:195
  881.0 49.6 %fusion.5 = bf16[8,630,1024]{2,1,0:T(8,128)(2,1)} fusion(f32[8,630,1024]{2,1,0:T(8,128)} %get-tuple-element.137, u8[630,1024]{1,0:T(8,128)(4,1)S(1)} %copy-done.74, u8[630,1024]{1,0:T(8,128)(4,1)S(1)} %copy-done.73), kind=kLoop, calls=%fused_computation.23 | loop fusion | flops 361267200 | bytes 32256000 | tf_op jit(solution)/shard_map/convert_element_type | solution.py:113
  930.6 50.0 %fusion.2 = bf16[8,630,1024]{2,1,0:T(8,128)(2,1)} fusion(f32[8,630,1024]{2,1,0:T(8,128)} %get-tuple-element.138, u8[630,1024]{1,0:T(8,128)(4,1)S(1)} %get-tuple-element.56, u8[630,1024]{1,0:T(8,128)(4,1)S(1)} %get-tuple-element.55), kind=kLoop, calls=%fused_computation.20 | loop fusion | flops 361267200 | bytes 32256000 | tf_op jit(solution)/shard_map/convert_element_type | solution.py:113
  980.6 13.4 fusion.100
  994.0 13.7 copy.335
  1007.8 52.4 %gather_fusion.3 = f32[3152,512]{1,0:T(8,128)} fusion(f32[8,630,512]{2,0,1:T(8,128)} %copy.335, s32[3152]{0:T(1024)S(1)} %copy-done.9), kind=kCustom, calls=%fused_computation.5 | custom fusion | bytes 12935808 | tf_op jit(solution)/shard_map/gather | solution.py:115
  1060.2 8.3 reshape.451
  1068.5 13.4 fusion.97
  1081.9 13.7 copy.315
  1095.6 52.3 %gather_fusion.1 = f32[3152,512]{1,0:T(8,128)} fusion(f32[8,630,512]{2,0,1:T(8,128)} %copy.315, s32[3152]{0:T(1024)S(1)} %copy-done.8), kind=kCustom, calls=%fused_computation.3 | custom fusion | bytes 12935808 | tf_op jit(solution)/shard_map/gather | solution.py:115
  1147.9 8.5 reshape.447
  1156.4 21.9 multiply_reduce_fusion.2
  1178.3 19.6 multiply_reduce_fusion.3
  1198.0 8.9 all-reduce.8
  1220.9 7.7 multiply_reduce_fusion.9
  1228.6 11.1 multiply_add_fusion.1
  1247.9 5.7 fusion.43
  1258.1 4.7 multiply_convert_fusion.3
  1278.8 5.7 fusion.44
  1289.0 4.6 multiply_convert_fusion.2
  1358.5 16.8 fusion.38
  1380.4 20.4 convolution_add_fusion
  1400.9 14.6 fusion.104
  1415.5 18.9 convolution_add_fusion.1
  1447.7 26.6 %all-reduce.20.cloned.1.call-done = f32[3,512,256]{2,0,1:T(4,128)} async-done(((f32[3,512,256]{2,0,1:T(4,128)}), f32[3,512,256]{2,0,1:T(4,128)}) %all-reduce.20.cloned.1.call-update) | async-done | bytes 1572880
  1475.9 32.2 %all-reduce.22.cloned.1.call-done = (f32[1576,512]{1,0:T(8,128)}, f32[1576,512]{1,0:T(8,128)}) async-done(((f32[1576,512]{1,0:T(8,128)}, f32[1576,512]{1,0:T(8,128)}), (f32[1576,512]{1,0:T(8,128)}, f32[1576,512]{1,0:T(8,128)})) %all-reduce.22.cloned.1.call-update) | async-done | bytes 6455312 | tf_op jit(solution)/shard_map/psum | solution.py:238
  1512.9 7.1 multiply_reduce_fusion.10
  1520.0 42.3 %all-reduce.7 = (f32[512]{0:T(512)S(1)}, f32[512]{0:T(512)S(1)}) all-reduce(f32[512]{0:T(512)S(1)} %add.243, f32[512]{0:T(512)S(1)} %add.247), channel_id=2, replica_groups=mesh['dp'=16,'tensor'=2] {'dp'}, use_global_device_ids=true, to_apply=%region_58.60.clone | all-reduce | flops 1024 | bytes 8192
  1574.9 13.8 reduce-scatter.7.cloned.1.call-done
  1588.8 345.5 %reduce-scatter.11.cloned.1.call-done = f32[8,1024,32]{1,2,0:T(8,128)} async-done(((f32[8,1024,512]{1,2,0:T(8,128)}), f32[8,1024,32]{1,2,0:T(8,128)}) %reduce-scatter.11.cloned.1.call-update) | async-done | bytes 1048592 | tf_op jit(solution)/shard_map/reduce_scatter | solution.py:255
  1934.2 354.8 %reduce-scatter.9.cloned.1.call-done = f32[8,32,1024]{2,1,0:T(8,128)} async-done(((f32[8,512,1024]{2,1,0:T(8,128)}), f32[8,32,1024]{2,1,0:T(8,128)}) %reduce-scatter.9.cloned.1.call-update) | async-done | bytes 1048592 | tf_op jit(solution)/shard_map/reduce_scatter | solution.py:254
  (513 shorter events, 292.5 us)
Async XLA Ops:
  8.0 395.2 %all-reduce.26.cloned.1.call-start = ((), (), s32[]{:S(2)}) async-start(), calls=%async_computation.13 | async-start | bytes 12910592 | tf_op jit(solution)/shard_map/psum | solution.py:103
  11.7 146.7 %copy-start.100 = (f32[1576]{0:T(1024)}, f32[1576]{0:T(1024)S(1)}, u32[]{:S(2)}) copy-start(f32[1576]{0:T(1024)S(1)} %div.79) | copy-start | bytes 18916
  61.4 128.6 %copy-start.115 = (f32[512]{0:T(512)}, f32[512]{0:T(512)S(1)}, u32[]{:S(2)}) copy-start(f32[512]{0:T(512)S(1)} %convert_element_type.218) | copy-start | bytes 6148
  68.5 89.9 %copy-start.102 = (f32[1576]{0:T(1024)}, f32[1576]{0:T(1024)S(1)}, u32[]{:S(2)}) copy-start(f32[1576]{0:T(1024)S(1)} %rsqrt.39) | copy-start | bytes 18916
  68.7 121.3 %copy-start.110 = (f32[1576]{0:T(1024)}, f32[1576]{0:T(1024)S(1)}, u32[]{:S(2)}) copy-start(f32[1576]{0:T(1024)S(1)} %rsqrt.42) | copy-start | bytes 18916
  106.1 121.4 %copy-start.59 = (bf16[256,512]{0,1:T(8,128)(2,1)}, bf16[256,512]{0,1:T(8,128)(2,1)S(1)}, u32[]{:S(2)}) copy-start(bf16[256,512]{0,1:T(8,128)(2,1)S(1)} %all_gather.30) | copy-start | bytes 786436
  168.9 15.1 copy-start.38
  199.2 12.8 copy-start.42
  229.9 50.4 %copy-start.125 = (s32[2]{0:T(128)S(1)}, s32[2]{0:T(128)}, u32[]{:S(2)}) copy-start(s32[2]{0:T(128)} %constant.149) | copy-start | bytes 28
  229.9 50.5 %copy-start.124 = (s32[2]{0:T(128)S(1)}, s32[2]{0:T(128)}, u32[]{:S(2)}) copy-start(s32[2]{0:T(128)} %constant.152) | copy-start | bytes 28
  229.9 339.6 %all-gather.4.cloned.1.call-start = ((), (), s32[]{:S(2)}) async-start(), calls=%async_computation.4 | async-start | bytes 8912896 | tf_op jit(solution)/shard_map/all_gather | solution.py:65
  230.5 359.1 %all-gather.6.cloned.1.call-start = ((), (), s32[]{:S(2)}) async-start(), calls=%async_computation.5 | async-start | bytes 8912896 | tf_op jit(solution)/shard_map/all_gather | solution.py:66
  231.1 989.7 %all-reduce.24.cloned.1.call-start = ((), (), s32[]{:S(2)}) async-start(), calls=%async_computation.12 | async-start | bytes 12910592 | tf_op jit(solution)/shard_map/psum | solution.py:197
  235.3 176.0 %copy-start.112 = (f32[512]{0:T(512)}, f32[512]{0:T(512)S(1)}, u32[]{:S(2)}) copy-start(f32[512]{0:T(512)S(1)} %convert_element_type.225) | copy-start | bytes 6148
  235.5 100.1 %copy-start.104 = (f32[1576]{0:T(1024)}, f32[1576]{0:T(1024)S(1)}, u32[]{:S(2)}) copy-start(f32[1576]{0:T(1024)S(1)} %mul.439) | copy-start | bytes 18916
  235.6 133.8 %copy-start.106 = (f32[1576]{0:T(1024)}, f32[1576]{0:T(1024)S(1)}, u32[]{:S(2)}) copy-start(f32[1576]{0:T(1024)S(1)} %mul.421) | copy-start | bytes 18916
  272.4 162.5 %copy-start.83 = (bf16[512,8]{0,1:T(8,128)(2,1)}, bf16[512,8]{0,1:T(8,128)(2,1)S(1)}, u32[]{:S(2)}) copy-start(bf16[512,8]{0,1:T(8,128)(2,1)S(1)} %reshape.598) | copy-start | bytes 24580
  272.5 41.3 %copy-start.96 = (s32[1576,2]{0,1:T(2,128)}, s32[1576,2]{0,1:T(2,128)S(1)}, u32[]{:S(2)}) copy-start(s32[1576,2]{0,1:T(2,128)S(1)} %reshape_squeeze.5) | copy-start | bytes 37828
  272.6 40.9 %copy-start.98 = (s32[1576,2]{0,1:T(2,128)}, s32[1576,2]{0,1:T(2,128)S(1)}, u32[]{:S(2)}) copy-start(s32[1576,2]{0,1:T(2,128)S(1)} %reshape_squeeze.4) | copy-start | bytes 37828
  280.6 32.8 %copy-start.117 = (s32[3152]{0:T(1024)}, s32[3152]{0:T(1024)S(1)}, u32[]{:S(2)}) copy-start(s32[3152]{0:T(1024)S(1)} %get-tuple-element.146) | copy-start | bytes 37828
  337.8 21.0 copy-start
  369.4 23.2 %copy-start.90 = (s32[5120]{0:T(1024)}, s32[5120]{0:T(1024)S(1)}, u32[]{:S(2)}) copy-start(s32[5120]{0:T(1024)S(1)} %pad_clamp_fusion.1) | copy-start | bytes 61444
  371.6 21.0 copy-start.2
  411.3 23.6 %copy-start.94 = (f32[1576]{0:T(1024)}, f32[1576]{0:T(1024)S(1)}, u32[]{:S(2)}) copy-start(f32[1576]{0:T(1024)S(1)} %add_rsqrt_fusion.2) | copy-start | bytes 18916
  413.6 21.3 copy-start.4
  435.4 31.7 %copy-start.91 = (s32[5120]{0:T(1024)S(1)}, s32[5120]{0:T(1024)}, u32[]{:S(2)}) copy-start(s32[5120]{0:T(1024)} %copy-done.90) | copy-start | bytes 61444
  467.1 23.2 %copy-start.6 = (bf16[1576,512]{1,0:T(8,128)(2,1)S(1)}, bf16[1576,512]{1,0:T(8,128)(2,1)}, u32[]{:S(2)}) copy-start(bf16[1576,512]{1,0:T(8,128)(2,1)} %get-tuple-element.127) | copy-start | bytes 4841476
  467.1 23.2 %copy-start.84 = (bf16[512,8]{0,1:T(8,128)(2,1)S(1)}, bf16[512,8]{0,1:T(8,128)(2,1)}, u32[]{:S(2)}) copy-start(bf16[512,8]{0,1:T(8,128)(2,1)} %copy-done.83) | copy-start | bytes 24580
  467.1 23.7 %copy-start.12 = (s32[3152]{0:T(1024)S(1)}, s32[3152]{0:T(1024)}, u32[]{:S(2)}) copy-start(s32[3152]{0:T(1024)} %reshape.604) | copy-start | bytes 37828
  490.8 30.8 %copy-start.35 = (s32[1576,2]{1,0:T(8,128)S(1)}, s32[1576,2]{1,0:T(8,128)}, u32[]{:S(2)}) copy-start(s32[1576,2]{1,0:T(8,128)} %copy-done.34) | copy-start | bytes 37828
  490.8 30.8 %copy-start.37 = (s32[1576,2]{1,0:T(8,128)S(1)}, s32[1576,2]{1,0:T(8,128)}, u32[]{:S(2)}) copy-start(s32[1576,2]{1,0:T(8,128)} %copy-done.36) | copy-start | bytes 37828
  525.6 39.2 %copy-start.30 = (f32[1576,2]{1,0:T(8,128)}, f32[1576,2]{1,0:T(8,128)S(1)}, u32[]{:S(2)}) copy-start(f32[1576,2]{1,0:T(8,128)S(1)} %fusion.56) | copy-start | bytes 37828
  542.6 47.0 %copy-start.75 = (f32[8,630]{1,0:T(8,128)}, f32[8,630]{1,0:T(8,128)S(1)}, u32[]{:S(2)}) copy-start(f32[8,630]{1,0:T(8,128)S(1)} %reshape.473) | copy-start | bytes 60484
  543.6 21.2 copy-start.32
  560.2 184.6 %copy-start.77 = (f32[8,630]{1,0:T(8,128)}, f32[8,630]{1,0:T(8,128)S(1)}, u32[]{:S(2)}) copy-start(f32[8,630]{1,0:T(8,128)S(1)} %reshape.469) | copy-start | bytes 60484
  622.7 13.7 copy-start.9
  778.1 13.8 copy-start.8
  852.7 28.2 %copy-start.73 = (u8[630,1024]{1,0:T(8,128)(4,1)S(1)}, u8[630,1024]{1,0:T(8,128)(4,1)}, u32[]{:S(2)}) copy-start(u8[630,1024]{1,0:T(8,128)(4,1)} %get-tuple-element.57) | copy-start | bytes 1935364
  852.7 28.2 %copy-start.74 = (u8[630,1024]{1,0:T(8,128)(4,1)S(1)}, u8[630,1024]{1,0:T(8,128)(4,1)}, u32[]{:S(2)}) copy-start(u8[630,1024]{1,0:T(8,128)(4,1)} %get-tuple-element.58) | copy-start | bytes 1935364
  930.6 298.0 %all-reduce.28.cloned.1.call-start = ((), (), s32[]{:S(2)}) async-start(), calls=%async_computation.14 | async-start | bytes 6455296 | tf_op jit(solution)/shard_map/psum | solution.py:117
  1156.4 21.9 copy-start.3
  1156.4 21.9 copy-start.29
  1156.4 21.9 copy-start.33
  1178.3 19.7 copy-start.63
  1197.9 237.1 %reduce-scatter.13.cloned.1.call-start = ((), (), s32[]{:S(2)}) async-start(), calls=%async_computation.9 | async-start | bytes 278528
  1206.9 11.4 copy-start.99
  1206.9 11.5 copy-start.97
  1206.9 11.5 copy-start.7
  1208.1 11.0 copy-start.5
  1220.7 253.6 %all-reduce.20.cloned.1.call-start = ((), (), s32[]{:S(2)}) async-start(), calls=%async_computation.10 | async-start | bytes 4194304
  1228.6 12.9 copy-start.60
  1242.1 11.5 slice-start.2
  1272.7 11.7 slice-start
  1310.1 12.8 copy-start.24
  1310.1 12.8 copy-start.101
  1310.1 12.8 copy-start.103
  1310.1 12.8 copy-start.116
  1331.1 12.8 copy-start.20
  1331.1 12.8 copy-start.109
  1331.1 12.8 copy-start.111
  1351.4 156.6 %all-reduce.22.cloned.1.call-start = ((), (), s32[]{:S(2)}) async-start(), calls=%async_computation.11 | async-start | bytes 12910592 | tf_op jit(solution)/shard_map/psum | solution.py:238
  1357.8 231.0 %reduce-scatter.7.cloned.1.call-start = ((), (), s32[]{:S(2)}) async-start(), calls=%async_computation.6 | async-start | bytes 557056 | tf_op jit(solution)/shard_map/reduce_scatter | solution.py:251
  1380.4 553.9 %reduce-scatter.11.cloned.1.call-start = ((), (), s32[]{:S(2)}) async-start(), calls=%async_computation.8 | async-start | bytes 17825792 | tf_op jit(solution)/shard_map/reduce_scatter | solution.py:255
  1400.9 888.2 %reduce-scatter.9.cloned.1.call-start = ((), (), s32[]{:S(2)}) async-start(), calls=%async_computation.7 | async-start | bytes 17825792 | tf_op jit(solution)/shard_map/reduce_scatter | solution.py:254
  (79 other events, 406.4 us)
Sparse Core Ops, SparseCore 0:
  230.0 28.8 all-reduce.25
  930.7 29.5 all-reduce.23
  1198.0 20.5 all-reduce.27
Sparse Core Ops, SparseCore 1:
  233.1 108.7 all-gather.3
  344.5 110.5 all-gather.5
  1220.8 73.3 reduce-scatter.12
  1351.5 122.7 all-reduce.19
  1476.9 31.1 all-reduce.21
  1510.9 77.8 reduce-scatter.6
  1591.6 342.6 reduce-scatter.10
  1937.1 351.9 reduce-scatter.8
where the time goes:
time: 2310 us; the launch traced here: 2300 us
  waiting for transfers between devices  774 us (34%)
  local copies, waits for them, and re-layouts  717 us (31%)
  matrix products  290 us (13%)
  other arithmetic  282 us (12%)
  blocking collectives  214 us (9%)
    reduce_scatter x1, waiting for transfers between devices, body(): lax.psum_scatter(totals[5], 'dp', scatter_dimension=1, tiled=True)  355 us
    reduce_scatter x1, waiting for transfers between devices, body(): lax.psum_scatter(totals[6], 'dp', scatter_dimension=2, tiled=True)  345 us
    gather x2, local copies, waits for them, and re-layouts, body(): grad_act2_part = jnp.sum(grad_rows[flat, place].reshape(rows, 2, width), 1)  105 us
    gather x2, local copies, waits for them, and re-layouts, body(): per_route = result[flat, place].reshape(rows, 2, width)  105 us
    convert_element_type x2, other arithmetic, body(): hidden = jax.nn.gelu(inner, approximate=False).astype(bf16)  99.6 us
    unnamed x288, local copies, waits for them, and re-layouts  93.7 us
    unnamed x2, blocking collectives  86.3 us
    gather x6, local copies, waits for them, and re-layouts, body(): gates = jax.nn.softmax(jnp.take_along_axis(logits, chosen, 1), -1)  63.8 us
  transfers between devices with their start and end apart: 11, of which 5 were waited for; matrix products, arithmetic and copies ran while one was open for 37% of the time, Pallas kernels for 0%

commit v1 on v0

v1 whole, which is shorter than its diff:
```python
import functools

import jax
import jax.numpy as jnp
from jax import lax
from jax.experimental import pallas as pl
from jax.experimental.pallas import tpu as pltpu
from jax.sharding import PartitionSpec as P

F32 = jnp.float32
BF16 = jnp.bfloat16
HD = 64
SEQ = 197
ROWS = 208
SLOTS = 1280
SPAN = 1536
WIN = 128
TILE = 256
EXPERTS = 8
LANES = 128
GROUP = 1
VMEM = 58 * 1024 * 1024

LIVE, START, TOTAL, TABLE = 8, 32, 160, 256


def nt(a, b):
    return lax.dot_general(a, b, (((1,), (1,)), ((), ())), preferred_element_type=F32)


def tn(a, b):
    return lax.dot_general(a, b, (((0,), (0,)), ((), ())), preferred_element_type=F32)


def mm(a, b):
    return jnp.dot(a, b, preferred_element_type=F32)


def iota(shape, dim):
    return lax.broadcasted_iota(jnp.int32, shape, dim)


def layer_stats(values):
    centre = values - jnp.mean(values, -1, keepdims=True)
    factor = lax.rsqrt(jnp.mean(centre * centre, -1, keepdims=True) + 1e-06)
    return centre * factor, factor


def norm_back(grad, normed, factor):
    return factor * (
        grad - jnp.mean(grad, -1, keepdims=True) - normed * jnp.mean(grad * normed, -1, keepdims=True)
    )


def gelu_both(u):
    a = jnp.abs(u) * 0.7071067811865476
    t = 1.0 / (1.0 + 0.3275911 * a)
    bell = jnp.exp(-a * a)
    poly = t * (
        0.127414796 + t * (-0.142248368 + t * (0.7107068705 + t * (-0.7265760135 + t * 0.5307027145)))
    )
    tail = poly * bell
    phi = jnp.where(u >= 0.0, 1.0 - tail, tail)
    return u * phi, phi + u * bell * 0.3989422804014327


def split_low(values):
    high = values.astype(BF16).astype(F32)
    return high, values - high


def load_weights(info, parts, weights, sems, rel, rows):
    c, me = info[0], info[1]
    copies = []
    for side, part in enumerate(parts):
        t = c ^ side
        for k, r in enumerate(rel):
            where = pl.multiple_of((me ^ r) * rows, 16)
            copies.append(
                pltpu.make_async_copy(part.at[k], weights.at[t, pl.ds(where, rows), :], sems.at[side, k])
            )
    for copy in copies:
        copy.start()
    for copy in copies:
        copy.wait()


def head_mask(which):
    lane = iota((ROWS, LANES), 1)
    return (lane < HD) if which == 0 else (lane >= HD)


def forward_kernel(rel, rows, info, tok, mask, *refs):
    i = pl.program_id(0)
    w_parts, refs = refs[:-10], refs[-10:]
    src, mid, proj, att, lse, gates, weights, gains, xs, sems = refs
    shares, _, cols = weights.shape
    local = (cols - LANES) // 4
    aux_at = 4 * local

    @pl.when(i == 0)
    def _():
        load_weights(info, w_parts, weights, sems, rel, rows)
        gains[...] = weights[0, :, aux_at:].astype(F32).T[0:16, :]

    @pl.when(info[LIVE + i] == 1)
    def _():
        xs[192:ROWS, :] = jnp.zeros((ROWS - 192, 512), F32)
        xs[0:SEQ, :] = tok[0, 0].astype(F32)
        x = xs[...]
        normed, _ = layer_stats(x)
        act = (normed * gains[8:9, :]).astype(BF16)
        for t in range(shares):
            proj[0, :, t * 3 * local : (t + 1) * 3 * local] = mm(act, weights[t, :, 0 : 3 * local]).astype(BF16)
        key_ok = iota((ROWS, ROWS), 1) < SEQ
        lane = iota((ROWS, LANES), 1)
        saved = jnp.zeros((ROWS, LANES), F32)
        for t in range(shares):
            for p in range(local // LANES):
                at = t * 3 * local + p * LANES
                q = proj[0, :, at : at + LANES]
                k = proj[0, :, at + local : at + local + LANES]
                v = proj[0, :, at + 2 * local : at + 2 * local + LANES]
                halves = []
                for h in range(2):
                    qm = jnp.where(head_mask(h), q.astype(F32), 0.0).astype(BF16)
                    s = jnp.where(key_ok, nt(qm, k) * (HD**-0.5), -1e30)
                    top = jnp.max(s, -1, keepdims=True)
                    e = jnp.exp(s - top)
                    total = jnp.sum(e, -1, keepdims=True)
                    probs = (e * (1.0 / total)).astype(BF16)
                    halves.append(mm(probs, v))
                    saved = jnp.where(lane == (t * local + p * LANES) // HD + h, top + jnp.log(total), saved)
                att[0, :, t * local + p * LANES : t * local + (p + 1) * LANES] = jnp.where(
                    lane < HD, halves[0], halves[1]
                ).astype(BF16)
        lse[0] = saved
        branch = nt(att[0, :, 0:local], weights[0, :, 3 * local : aux_at])
        for t in range(1, shares):
            branch = branch + nt(att[0, :, t * local : (t + 1) * local], weights[t, :, 3 * local : aux_at])
        middle = x + branch
        mid[0] = middle
        normed2, _ = layer_stats(middle)
        act2 = (normed2 * gains[9:10, :]).astype(BF16)
        src[0, :, 0:512] = act2
        chosen = mask[0, 0].astype(F32)
        logits = jnp.where(chosen > 0.0, mm(act2, weights[0, :, aux_at:]), -1e30)
        top = jnp.max(logits, -1, keepdims=True)
        e = jnp.exp(logits - top) * chosen
        gate = e / jnp.maximum(jnp.sum(e, -1, keepdims=True), 0.5)
        gates[0] = gate
        high, low = split_low(gate)
        src[0, :, 512:640] = (high + pltpu.roll(low, 8, 1)).astype(BF16)


def dispatch_kernel(count, info, own, oth, gy, mask, x_hbm, xbuf, tbuf, pbuf, sems):
    i = pl.program_id(0)

    @pl.when(i == 0)
    def _():
        for e in range(EXPERTS):

            @pl.loop(0, SPAN // TILE)
            def _(k):
                xbuf[e, pl.ds(pl.multiple_of(k * TILE, TILE), TILE), :] = jnp.zeros((TILE, 1152), BF16)

        tbuf[...] = jnp.zeros(tbuf.shape, BF16)
        pbuf[...] = jnp.full(pbuf.shape, -4096.0, F32)

    @pl.when(info[LIVE + i] == 1)
    def _():
        @pl.when(i < count)
        def _():
            tbuf[0:ROWS, 0:512] = own[0, :, 0:512]
            tbuf[0:ROWS, 1024:1152] = own[0, :, 512:640]

        @pl.when(i >= count)
        def _():
            tbuf[0:ROWS, 0:512] = oth[0, :, 0:512]
            tbuf[0:ROWS, 1024:1152] = oth[0, :, 512:640]

        tbuf[0:SEQ, 512:1024] = gy[0, 0]
        chosen = mask[0, 0]
        lower = (iota((ROWS, ROWS), 0) > iota((ROWS, ROWS), 1)).astype(F32).astype(BF16)
        pbuf[0:ROWS, :] = jnp.where(chosen.astype(F32) > 0.0, mm(lower, chosen), -4096.0)
        place = pbuf[...].T
        slot = iota((WIN, TILE), 0).astype(F32)

        def window(w):
            picks = []
            for e in range(EXPERTS):
                off = (info[START + i * 8 + e] % 16 - WIN * w).astype(F32)
                picks.append(jnp.where(slot == place[e : e + 1, :] + off, 1.0, 0.0).astype(BF16))
            pick = jnp.concatenate(picks, 0)
            for n in range(3):
                cols = slice(n * 384, (n + 1) * 384)
                part = mm(pick, tbuf[:, cols]).astype(BF16)
                for e in range(EXPERTS):
                    first = pl.multiple_of(info[START + i * 8 + e] // 16 * 16 + WIN * w, 16)
                    rows = pl.ds(first, WIN)
                    xbuf[e, rows, cols] = xbuf[e, rows, cols] + part[e * WIN : (e + 1) * WIN]

        window(0)

        @pl.when(needs_second(info, i))
        def _():
            window(1)

    @pl.when(i == 15)
    def _():
        for start in (True, False):
            for e in range(EXPERTS):
                for k in range(SLOTS // TILE):

                    @pl.when(k * TILE < info[TOTAL + e])
                    def _():
                        rows = pl.ds(k * TILE, TILE)
                        copy = pltpu.make_async_copy(xbuf.at[e, rows, :], x_hbm.at[e, rows, :], sems.at[e, k])
                        if start:
                            copy.start()
                        else:
                            copy.wait()


def window_end(info, i, e):
    begin = info[START + i * 8 + e]
    end = info[START + i * 8 + 8 + e]
    return end - begin // 16 * 16


def needs_second(info, i):
    most = window_end(info, i, 0)
    for e in range(1, EXPERTS):
        most = jnp.maximum(most, window_end(info, i, e))
    return most > WIN


def expert_kernel(
    first, rel_in, rel_out, order_in, order_out, rows, n_in, n_out, info, x, *refs
):
    pieces_in, refs = refs[:n_in], refs[n_in:]
    pieces_out, refs = refs[:n_out], refs[n_out:]
    n_grad = 1 if len(rel_in) == 1 else 2
    y = refs[0]
    grads_in, grads_out = refs[1 : 1 + n_grad], refs[1 + n_grad : 1 + 2 * n_grad]
    w_in, w_out, acc_in, acc_out, sems = refs[1 + 2 * n_grad :]
    e, t = pl.program_id(0), pl.program_id(1)
    expert = first + e
    me = info[1]

    @pl.when(t == 0)
    def _():
        copies = []
        for side, (pieces, rel, buf) in enumerate(((pieces_in, rel_in, w_in), (pieces_out, rel_out, w_out))):
            k = 0
            for piece in pieces:
                for b in range(piece.shape[0]):
                    where = pl.multiple_of((me ^ rel[k]) * rows, 16)
                    copies.append(
                        pltpu.make_async_copy(piece.at[b, e], buf.at[pl.ds(where, rows), :], sems.at[side, k])
                    )
                    k += 1
        for copy in copies:
            copy.start()
        for copy in copies:
            copy.wait()
        acc_in[...] = jnp.zeros(acc_in.shape, F32)
        acc_out[...] = jnp.zeros(acc_out.shape, F32)

    @pl.when(t * TILE < info[TOTAL + expert])
    def _():
        rows_x = x[0, :, 0:512]
        rows_g = x[0, :, 512:1024]
        lane = iota((TILE, LANES), 1)
        mine = (lane == expert) | (lane == expert + 8)
        gate = jnp.sum(jnp.where(mine, x[0, :, 1024:1152].astype(F32), 0.0), -1, keepdims=True)
        inner = mm(rows_x, w_in[...])
        act, slope = gelu_both(inner)
        hid = act.astype(BF16)
        out = nt(hid, w_out[...])
        g = rows_g.astype(F32)
        deo = (gate * g).astype(BF16)
        dinner = (mm(deo, w_out[...]) * slope).astype(BF16)
        dgate = jnp.sum(g * out, -1, keepdims=True)
        high, low = split_low(dgate)
        y[0, :, 0:512] = (gate * out).astype(BF16)
        y[0, :, 512:1024] = nt(dinner, w_in[...]).astype(BF16)
        y[0, :, 1024:1152] = jnp.where(
            lane == expert, high, jnp.where(lane == expert + 8, low, 0.0)
        ).astype(BF16)
        acc_in[...] += tn(rows_x, dinner)
        acc_out[...] += tn(deo, hid)

    @pl.when(t == pl.num_programs(1) - 1)
    def _():
        for acc, outs, order in ((acc_in, grads_in, order_in), (acc_out, grads_out, order_out)):
            half = len(order) // len(outs)
            for k, r in enumerate(order):
                where = pl.multiple_of((me ^ r) * rows, 16)
                outs[k // half][k % half, 0] = acc[pl.ds(where, rows), :].astype(BF16)


def combine_kernel(base, info, y_hbm, mask, out, ybuf, acc, sems):
    i = pl.program_id(0)
    slot = i % 2

    def copies(j, buf, w):
        for e in range(EXPERTS):
            first = pl.multiple_of(info[START + (base + j) * 8 + e] // 16 * 16 + WIN * w, 16)
            yield pltpu.make_async_copy(
                y_hbm.at[e, pl.ds(first, WIN), :],
                ybuf.at[buf, pl.ds(e * WIN, WIN), :],
                sems.at[buf, e],
            )

    def fetch(j, buf):
        @pl.when(info[LIVE + base + j] == 1)
        def _():
            for copy in copies(j, buf, 0):
                copy.start()

    @pl.when(i == 0)
    def _():
        fetch(i, slot)

    @pl.when(i + 1 < pl.num_programs(0))
    def _():
        fetch(i + 1, 1 - slot)

    @pl.when(info[LIVE + base + i] == 1)
    def _():
        for copy in copies(i, slot, 0):
            copy.wait()
        chosen = mask[0, 0]
        lower = (iota((ROWS, ROWS), 0) > iota((ROWS, ROWS), 1)).astype(F32).astype(BF16)
        place = jnp.where(chosen.astype(F32) > 0.0, mm(lower, chosen), -4096.0)
        lane = iota((ROWS, WIN), 1).astype(F32)

        def window(w):
            picks = []
            for e in range(EXPERTS):
                begin = info[START + (base + i) * 8 + e]
                limit = info[TOTAL + e] - begin // 16 * 16 - WIN * w

                @pl.when(limit < WIN)
                def _():
                    part = ybuf[slot, e * WIN : (e + 1) * WIN, :].astype(F32)
                    keep = iota((WIN, 1152), 0) < limit
                    ybuf[slot, e * WIN : (e + 1) * WIN, :] = jnp.where(keep, part, 0.0).astype(BF16)

                off = (begin % 16 - WIN * w).astype(F32)
                picks.append(jnp.where(lane == place[:, e : e + 1] + off, 1.0, 0.0).astype(BF16))
            return mm(jnp.concatenate(picks, 1), ybuf[slot])

        acc[...] = window(0)

        @pl.when(needs_second(info, base + i))
        def _():
            for copy in copies(i, slot, 1):
                copy.start()
            for copy in copies(i, slot, 1):
                copy.wait()
            acc[...] += window(1)

        if out.dtype == F32:
            out[0] = acc[...]
        else:
            out[0, :, 0:1024] = acc[:, 0:1024].astype(BF16)
            aux = acc[:, 1024:1152]
            both = jnp.where(iota((ROWS, LANES), 1) < 8, aux + pltpu.roll(aux, LANES - 8, 1), 0.0)
            high, low = split_low(both)
            out[0, :, 1024:1152] = (high + pltpu.roll(low, 8, 1)).astype(BF16)


def backward_kernel(
    rel,
    order,
    rows,
    info,
    tok,
    gy_ref,
    comb_own,
    comb_oth,
    mid,
    proj,
    att,
    lse,
    gates,
    *refs,
):
    i = pl.program_id(0)
    c, me = info[0], info[1]
    scratch, refs = refs[-11:], refs[:-11]
    weights, gains, twice, xs, gs, dproj, acc_qkv, acc_out, acc_router, acc_gain, sems = scratch
    shares, _, cols = weights.shape
    w_parts, refs = refs[:shares], refs[shares:]
    block_out, grad_tok = refs[:2]
    grads = refs[2:]
    local = (cols - LANES) // 4
    aux_at = 4 * local

    @pl.when(i == 0)
    def _():
        load_weights(info, w_parts, weights, sems, rel, rows)
        aux = weights[0, :, aux_at:].astype(F32)
        gains[...] = aux.T[0:16, :]
        lane = iota((512, LANES), 1)
        router = jnp.where(lane < 8, aux, 0.0)
        twice[...] = (router + pltpu.roll(router, 8, 1)).astype(BF16)
        acc_qkv[...] = jnp.zeros(acc_qkv.shape, F32)
        acc_out[...] = jnp.zeros(acc_out.shape, F32)
        acc_router[...] = jnp.zeros(acc_router.shape, F32)
        acc_gain[...] = jnp.zeros(acc_gain.shape, F32)

    @pl.when(info[LIVE + i] == 0)
    def _():
        block_out[...] = jnp.zeros(block_out.shape, BF16)
        grad_tok[...] = jnp.zeros(grad_tok.shape, BF16)

    @pl.when(info[LIVE + i] == 1)
    def _():
        xs[192:ROWS, :] = jnp.zeros((ROWS - 192, 512), F32)
        xs[0:SEQ, :] = tok[0, 0].astype(F32)
        gs[192:ROWS, :] = jnp.zeros((ROWS - 192, 512), F32)
        gs[0:SEQ, :] = gy_ref[0, 0].astype(F32)
        gy = gs[...]
        lane = iota((ROWS, LANES), 1)
        middle = mid[0]
        mixed = comb_own[0, :, 0:512] + comb_oth[0, :, 0:512].astype(F32)
        block_out[0] = (middle + mixed)[0:SEQ, :].astype(BF16)
        normed2, factor2 = layer_stats(middle)
        act2 = (normed2 * gains[9:10, :]).astype(BF16)
        gate = gates[0]
        aux = comb_own[0, :, 1024:1152] + comb_oth[0, :, 1024:1152].astype(F32)
        dgate = jnp.where(lane < 8, aux + pltpu.roll(aux, LANES - 8, 1), 0.0)
        dlogits = gate * (dgate - jnp.sum(gate * dgate, -1, keepdims=True))
        high, low = split_low(dlogits)
        packed = (high + pltpu.roll(low, 8, 1)).astype(BF16)
        acc_router[...] += tn(act2, packed)
        dact2 = (
            comb_own[0, :, 512:1024] + comb_oth[0, :, 512:1024].astype(F32) + nt(packed, twice[...])
        )
        acc_gain[9:10, :] += jnp.sum(dact2 * normed2, 0, keepdims=True)
        dmiddle = gy + norm_back(dact2 * gains[9:10, :], normed2, factor2)
        gs[...] = dmiddle
        dbranch = dmiddle.astype(BF16)
        x = xs[...]
        normed1, factor1 = layer_stats(x)
        act1 = (normed1 * gains[8:9, :]).astype(BF16)
        key_ok = iota((ROWS, ROWS), 1) < SEQ
        for t in range(shares):
            acc_out[t] += tn(dbranch, att[0, :, t * local : (t + 1) * local])
            datt_t = mm(dbranch, weights[t, :, 3 * local : aux_at]).astype(BF16)
            for p in range(local // LANES):
                at = t * 3 * local + p * LANES
                q = proj[0, :, at : at + LANES]
                k = proj[0, :, at + local : at + local + LANES]
                v = proj[0, :, at + 2 * local : at + 2 * local + LANES]
                datt = datt_t[:, p * LANES : (p + 1) * LANES]
                parts = []
                for h in range(2):
                    qm = jnp.where(head_mask(h), q.astype(F32), 0.0).astype(BF16)
                    dm = jnp.where(head_mask(h), datt.astype(F32), 0.0).astype(BF16)
                    head = (t * local + p * LANES) // HD + h
                    s = nt(qm, k) * (HD**-0.5) - lse[0, :, head : head + 1]
                    probs = jnp.where(key_ok, jnp.exp(jnp.where(key_ok, s, 0.0)), 0.0)
                    dprobs = nt(dm, v)
                    ds = (probs * (dprobs - jnp.sum(dprobs * probs, -1, keepdims=True))).astype(BF16)
                    parts.append((mm(ds, k), tn(ds, q), tn(probs.astype(BF16), datt)))
                for j in range(3):
                    both = jnp.where(lane < HD, parts[0][j], parts[1][j])
                    if j < 2:
                        both = both * (HD**-0.5)
                    dproj[:, at + j * local : at + j * local + LANES] = both.astype(BF16)
        dact1 = jnp.zeros((ROWS, 512), F32)
        for t in range(shares):
            dp = dproj[:, t * 3 * local : (t + 1) * 3 * local]
            acc_qkv[t] += tn(act1, dp)
            dact1 = dact1 + nt(dp, weights[t, :, 0 : 3 * local])
        acc_gain[8:9, :] += jnp.sum(dact1 * normed1, 0, keepdims=True)
        total = gs[...] + norm_back(dact1 * gains[8:9, :], normed1, factor1)
        grad_tok[0] = total[0:SEQ, :].astype(BF16)

    @pl.when(i == pl.num_programs(0) - 1)
    def _():
        lane = iota((512, LANES), 1)
        router = acc_router[...]
        aux = jnp.where(lane < 8, router + pltpu.roll(router, LANES - 8, 1), acc_gain[...].T)
        acc_router[...] = aux
        for k, r in enumerate(order):
            where = pl.ds(pl.multiple_of((me ^ r) * rows, 16), rows)
            for side, out in enumerate(grads):
                out[k, :, 0 : 3 * local] = acc_qkv[c ^ side, where, :].astype(BF16)
                out[k, :, 3 * local : aux_at] = acc_out[c ^ side, where, :].astype(BF16)
                out[k, :, aux_at:] = acc_router[where, :].astype(BF16)


def swap(n, bit):
    return [(i, i ^ bit) for i in range(n)]


def relatives(order):
    rel = [0]
    for bit in order:
        rel = rel + [r ^ (1 << bit) for r in rel]
    return tuple(rel)


def scatter_order(order):
    out = [0]
    for bit in reversed(order):
        out = out + [r ^ (1 << bit) for r in out]
    return tuple(out)


def hyper_gather(shard, order, n):
    pieces = [shard[None]]
    for bit in order:
        send = pieces[0] if len(pieces) == 1 else jnp.concatenate(pieces, 0)
        pieces.append(lax.ppermute(send, "dp", swap(n, 1 << bit)))
    return pieces


def hyper_scatter(keep, send, order, n):
    for step, bit in enumerate(order):
        got = lax.ppermute(send, "dp", swap(n, 1 << bit))
        if step == len(order) - 1:
            return (keep.astype(F32) + got.astype(F32))[0]
        half = keep.shape[0] // 2
        send = keep[half:] + got[half:]
        keep = keep[:half] + got[:half]


def any_spec():
    return pl.BlockSpec(memory_space=pl.ANY)


def params():
    return pltpu.CompilerParams(vmem_limit_bytes=VMEM)


def shape(s, d):
    return jax.ShapeDtypeStruct(s, d)


def body(
    n,
    shares,
    tokens,
    held,
    routes,
    ln1_gain,
    qkv_weight,
    out_weight,
    ln2_gain,
    router_weight,
    expert_in,
    expert_out,
    grad_out,
):
    rows = qkv_weight.shape[1]
    width = expert_in.shape[2]
    local = qkv_weight.shape[2]
    pack = 4 * local + LANES
    mine_count = 16 // shares
    per_micro = 8 // shares
    fast = rows % 16 == 0 and n & (n - 1) == 0
    c = lax.axis_index("tensor")
    me = lax.axis_index("dp")
    bits = n.bit_length() - 1
    if fast:
        order_a = tuple(reversed(range(bits)))
        order_b = order_a[:-2] + (order_a[-1], order_a[-2])
        block = rows
    else:
        order_a = order_b = ()
        block = 512
    rel_a, rel_b = relatives(order_a), relatives(order_b)
    back_a, back_b = tuple(reversed(order_a)), tuple(reversed(order_b))
    scat_a, scat_b = scatter_order(back_a), scatter_order(back_b)
    blocks = len(rel_a)

    aux = jnp.concatenate(
        [router_weight, ln1_gain[:, None], ln2_gain[:, None], jnp.zeros((rows, LANES - 10), BF16)], 1
    )
    small = jnp.concatenate([qkv_weight[0], qkv_weight[1], qkv_weight[2], out_weight.T, aux], 1)
    if fast:
        w_own = jnp.concatenate(hyper_gather(small, order_a, n), 0)
    else:
        w_own = lax.all_gather(small, "dp", axis=0, tiled=True)[None]

    def across(a, r):
        return lax.ppermute(a, "tensor", swap(shares, r))

    w_parts = [w_own] + [across(w_own, r) for r in range(1, shares)]

    weights = []
    back = jnp.swapaxes(expert_out, 1, 2)
    for at in range(0, EXPERTS, GROUP):
        pair = []
        for shard, order in ((expert_in[at : at + GROUP], order_a), (back[at : at + GROUP], order_b)):
            if fast:
                pair.append(hyper_gather(shard, order, n))
            else:
                pair.append([lax.all_gather(shard, "dp", axis=1, tiled=True)[None]])
        weights.append(pair)

    live = jnp.arange(8, dtype=jnp.int32)[None, :] < held
    lane = jnp.arange(LANES, dtype=jnp.int32)
    picked = (routes[..., 0:1] == lane) | (routes[..., 1:2] == lane)
    picked = (picked & live[:, :, None, None]).astype(BF16)
    mask = jnp.pad(picked, ((0, 0), (0, 0), (0, ROWS - SEQ), (0, 0)))
    counts = jnp.sum(
        (routes[..., None] == jnp.arange(EXPERTS, dtype=jnp.int32)).astype(jnp.int32), (2, 3)
    ) * live.astype(jnp.int32)[:, :, None]

    def own_first(a):
        a = a.reshape((2, per_micro, shares) + a.shape[2:])
        out = []
        for r in range(shares):
            part = a[:, :, 0]
            for t in range(1, shares):
                part = jnp.where(c ^ r == t, a[:, :, t], part)
            out.append(part.reshape((mine_count,) + a.shape[3:]))
        return jnp.concatenate(out, 0)

    counts = own_first(counts)
    live_list = own_first(live.astype(jnp.int32))
    ends = jnp.sum(
        jnp.where(jnp.arange(16)[:, None, None] >= jnp.arange(16)[None, :, None], counts[None], 0), 1
    )
    info = jnp.concatenate(
        [
            jnp.stack([c, me]).astype(jnp.int32),
            jnp.zeros((LIVE - 2,), jnp.int32),
            live_list,
            jnp.zeros((START - LIVE - 16,), jnp.int32),
            (ends - counts).reshape(-1),
            ends[15],
            jnp.zeros((TABLE - TOTAL - EXPERTS,), jnp.int32),
        ]
    )

    def image(i, s):
        j = i % mine_count
        return (j // per_micro, shares * (j % per_micro) + (s[0] ^ (i // mine_count)), 0, 0)

    tok_spec = pl.BlockSpec((1, 1, SEQ, 512), image)
    mask_spec = pl.BlockSpec((1, 1, ROWS, LANES), image)

    def row_spec(cols):
        return pl.BlockSpec((1, ROWS, cols), lambda i, s: (i, 0, 0))

    src, mid, proj, att, lse, gates = pl.pallas_call(
        functools.partial(forward_kernel, rel_a, block),
        grid_spec=pltpu.PrefetchScalarGridSpec(
            num_scalar_prefetch=1,
            grid=(mine_count,),
            in_specs=[tok_spec, mask_spec] + [any_spec()] * shares,
            out_specs=[row_spec(640), row_spec(512), row_spec(1536), row_spec(512), row_spec(LANES), row_spec(LANES)],
            scratch_shapes=[
                pltpu.VMEM((shares, 512, pack), BF16),
                pltpu.VMEM((16, 512), F32),
                pltpu.VMEM((ROWS, 512), F32),
                pltpu.SemaphoreType.DMA((shares, blocks)),
            ],
        ),
        out_shape=[
            shape((mine_count, ROWS, 640), BF16),
            shape((mine_count, ROWS, 512), F32),
            shape((mine_count, ROWS, 1536), BF16),
            shape((mine_count, ROWS, 512), BF16),
            shape((mine_count, ROWS, LANES), F32),
            shape((mine_count, ROWS, LANES), F32),
        ],
        compiler_params=params(),
        cost_estimate=pl.CostEstimate(flops=15 * 10**9, bytes_accessed=20 * 10**6, transcendentals=3 * 10**6),
        name="forward",
    )(info, tokens, mask, *w_parts)

    src_oth = [across(src, r) for r in range(1, shares)]
    src_oth = src_oth[0] if shares == 2 else jnp.concatenate(src_oth, 0)

    rows_x = pl.pallas_call(
        functools.partial(dispatch_kernel, mine_count),
        grid_spec=pltpu.PrefetchScalarGridSpec(
            num_scalar_prefetch=1,
            grid=(16,),
            in_specs=[
                pl.BlockSpec((1, ROWS, 640), lambda i, s: (jnp.minimum(i, mine_count - 1), 0, 0)),
                pl.BlockSpec((1, ROWS, 640), lambda i, s: (jnp.maximum(i - mine_count, 0), 0, 0)),
                tok_spec,
                mask_spec,
            ],
            out_specs=any_spec(),
            scratch_shapes=[
                pltpu.VMEM((EXPERTS, SPAN, 1152), BF16),
                pltpu.VMEM((TILE, 1152), BF16),
                pltpu.VMEM((TILE, LANES), F32),
                pltpu.SemaphoreType.DMA((EXPERTS, SLOTS // TILE)),
            ],
        ),
        out_shape=shape((EXPERTS, SLOTS, 1152), BF16),
        compiler_params=params(),
        cost_estimate=pl.CostEstimate(flops=12 * 10**9, bytes_accessed=30 * 10**6, transcendentals=0),
        name="dispatch",
    )(info, src, src_oth, grad_out, mask)

    tiles = SLOTS // TILE
    y_parts = []
    shards_in, shards_out = [], []
    for number, at in enumerate(range(0, EXPERTS, GROUP)):
        pieces_in, pieces_out = weights[number]

        def tile_at(e, t, s, at=at):
            last = jnp.maximum((s[TOTAL + at + e] + TILE - 1) // TILE - 1, 0)
            return jnp.minimum(t, last)

        halves = [blocks // 2] * 2 if blocks > 1 else [1]
        grad_specs = [pl.BlockSpec((h, 1, block, width), lambda e, t, s: (0, e, 0, 0)) for h in halves]
        grad_shapes = [shape((h, GROUP, block, width), BF16) for h in halves]
        got = pl.pallas_call(
            functools.partial(
                expert_kernel, at, rel_a, rel_b, scat_a, scat_b, block, len(pieces_in), len(pieces_out)
            ),
            grid_spec=pltpu.PrefetchScalarGridSpec(
                num_scalar_prefetch=1,
                grid=(GROUP, tiles),
                in_specs=[pl.BlockSpec((1, TILE, 1152), lambda e, t, s, at=at, f=tile_at: (at + e, f(e, t, s), 0))]
                + [any_spec()] * (len(pieces_in) + len(pieces_out)),
                out_specs=[pl.BlockSpec((1, TILE, 1152), lambda e, t, s, f=tile_at: (e, f(e, t, s), 0))]
                + grad_specs
                + grad_specs,
                scratch_shapes=[
                    pltpu.VMEM((512, width), BF16),
                    pltpu.VMEM((512, width), BF16),
                    pltpu.VMEM((512, width), F32),
                    pltpu.VMEM((512, width), F32),
                    pltpu.SemaphoreType.DMA((2, blocks)),
                ],
            ),
            out_shape=[shape((GROUP, SPAN, 1152), BF16)] + grad_shapes + grad_shapes,
            compiler_params=params(),
            cost_estimate=pl.CostEstimate(
                flops=GROUP * 5 * 10**9, bytes_accessed=GROUP * 12 * 10**6, transcendentals=GROUP * 10**6
            ),
            name="expert",
        )(info, rows_x, *pieces_in, *pieces_out)
        y_parts.append(got[0])
        if fast:
            shards_in.append(hyper_scatter(got[1], got[2], back_a, n))
            shards_out.append(hyper_scatter(got[3], got[4], back_b, n))
        else:
            shards_in.append(lax.psum_scatter(got[1][0], "dp", scatter_dimension=1, tiled=True).astype(F32))
            shards_out.append(lax.psum_scatter(got[2][0], "dp", scatter_dimension=1, tiled=True).astype(F32))
    rows_y = jnp.concatenate(y_parts, 0)

    def combine(base, dtype):
        return pl.pallas_call(
            functools.partial(combine_kernel, base),
            grid_spec=pltpu.PrefetchScalarGridSpec(
                num_scalar_prefetch=1,
                grid=(mine_count,),
                in_specs=[
                    any_spec(),
                    pl.BlockSpec((1, 1, ROWS, LANES), lambda i, s: image(i + base, s)),
                ],
                out_specs=row_spec(1152),
                scratch_shapes=[
                    pltpu.VMEM((2, EXPERTS * WIN, 1152), BF16),
                    pltpu.VMEM((ROWS, 1152), F32),
                    pltpu.SemaphoreType.DMA((2, EXPERTS)),
                ],
            ),
            out_shape=shape((mine_count, ROWS, 1152), dtype),
            compiler_params=params(),
            cost_estimate=pl.CostEstimate(flops=5 * 10**9, bytes_accessed=25 * 10**6, transcendentals=0),
            name="combine",
        )(info, rows_y, mask)

    comb_oth = [across(combine(mine_count * r, BF16), r) for r in range(1, shares)]
    comb_oth = comb_oth[0] if shares == 2 else sum(a.astype(F32) for a in comb_oth).astype(BF16)
    comb_own = combine(0, F32)

    small_spec = pl.BlockSpec((blocks, block, pack), lambda i, s: (0, 0, 0))
    tok_out = pl.BlockSpec((1, SEQ, 512), lambda i, s: (i, 0, 0))
    out_own, tok_own, *grads = pl.pallas_call(
        functools.partial(backward_kernel, rel_a, scat_a, block),
        grid_spec=pltpu.PrefetchScalarGridSpec(
            num_scalar_prefetch=1,
            grid=(mine_count,),
            in_specs=[
                tok_spec,
                tok_spec,
                row_spec(1152),
                row_spec(1152),
                row_spec(512),
                row_spec(1536),
                row_spec(512),
                row_spec(LANES),
                row_spec(LANES),
            ]
            + [any_spec()] * shares,
            out_specs=[tok_out, tok_out] + [small_spec] * shares,
            scratch_shapes=[
                pltpu.VMEM((shares, 512, pack), BF16),
                pltpu.VMEM((16, 512), F32),
                pltpu.VMEM((512, LANES), BF16),
                pltpu.VMEM((ROWS, 512), F32),
                pltpu.VMEM((ROWS, 512), F32),
                pltpu.VMEM((ROWS, 1536), BF16),
                pltpu.VMEM((shares, 512, 3 * local), F32),
                pltpu.VMEM((shares, 512, local), F32),
                pltpu.VMEM((512, LANES), F32),
                pltpu.VMEM((LANES, 512), F32),
                pltpu.SemaphoreType.DMA((shares, blocks)),
            ],
        ),
        out_shape=[
            shape((mine_count, SEQ, 512), BF16),
            shape((mine_count, SEQ, 512), BF16),
        ]
        + [shape((blocks, block, pack), BF16)] * shares,
        compiler_params=params(),
        cost_estimate=pl.CostEstimate(flops=25 * 10**9, bytes_accessed=30 * 10**6, transcendentals=3 * 10**6),
        name="backward",
    )(info, tokens, grad_out, comb_own, comb_oth, mid, proj, att, lse, gates, *w_parts)

    both = grads[0].astype(F32)
    for r in range(1, shares):
        both = both + across(grads[r], r).astype(F32)
    both = both.astype(BF16)
    if fast:
        half = blocks // 2
        mine = hyper_scatter(both[:half], both[half:], back_a, n)
    else:
        mine = lax.psum_scatter(both[0], "dp", scatter_dimension=0, tiled=True).astype(F32)

    def whole(own):
        parts = [own] + [across(own, r) for r in range(1, shares)]
        parts = [a.reshape(2, per_micro, 1, SEQ, 512) for a in parts]
        out = []
        for t in range(shares):
            part = parts[0]
            for r in range(1, shares):
                part = jnp.where(c ^ r == t, parts[r], part)
            out.append(part)
        return jnp.concatenate(out, 2).reshape(2, 8, SEQ, 512)

    return (
        whole(out_own),
        whole(tok_own),
        mine[:, 4 * local + 8],
        jnp.stack([mine[:, j * local : (j + 1) * local] for j in range(3)]),
        mine[:, 3 * local : 4 * local].T,
        mine[:, 4 * local + 9],
        mine[:, 4 * local : 4 * local + 8],
        jnp.concatenate(shards_in, 0),
        jnp.swapaxes(jnp.concatenate(shards_out, 0), 1, 2),
    )


def solution(mesh):
    placed = (
        P(None, "dp", None, None),
        P(None, "dp"),
        P(None, "dp", None, None),
        P("dp"),
        P(None, "dp", "tensor"),
        P("tensor", "dp"),
        P("dp"),
        P("dp", None),
        P(None, "dp", "tensor"),
        P(None, "tensor", "dp"),
        P(None, "dp", None, None),
    )
    return jax.shard_map(
        functools.partial(body, mesh.shape["dp"], mesh.shape["tensor"]),
        mesh=mesh,
        in_specs=placed,
        out_specs=(
            P(None, "dp", None, None),
            P(None, "dp", None, None),
            P("dp"),
            P(None, "dp", "tensor"),
            P("tensor", "dp"),
            P("dp"),
            P("dp", None),
            P(None, "dp", "tensor"),
            P(None, "tensor", "dp"),
        ),
        check_vma=False,
    )
```

time: 2310 us -> 810 us (0.35)
  local copies, waits for them, and re-layouts: 717 us -> 54.7 us
  waiting for transfers between devices: 774 us -> 299 us
  matrix products: 290 us -> 0 us
  blocking collectives: 214 us -> 0 us
  starting transfers between devices: 0.47 us -> 158 us
  other arithmetic: 282 us -> 139 us
  Pallas kernels: 0 us -> 142 us
    reduce_scatter x3 -> x0, waiting for transfers between devices: 714 us -> none  [the longest x1 355 us: body(): lax.psum_scatter(totals[5], 'dp', scatter_dimension=1, tiled=True)]
    gather x18 -> x0, local copies, waits for them, and re-layouts: 390 us -> none  [the longest x2 105 us: body(): grad_act2_part = jnp.sum(grad_rows[flat, place].reshape(rows, 2, width), 1)]
    ppermute x0 -> x142, waiting for transfers between devices: none -> 299 us  [the longest x68 169 us: hyper_scatter(): got = lax.ppermute(send, 'dp', swap(n, 1 << bit))]
    dot_general x42 -> x0, matrix products: 290 us -> none  [the longest x2 39.7 us: body(): jnp.einsum('ecd,efd->ecf', scaled, w_back, preferred_element_type=f32)]
    ppermute x0 -> x142, starting transfers between devices: none -> 158 us  [the longest x68 89.7 us: hyper_scatter(): got = lax.ppermute(send, 'dp', swap(n, 1 << bit))]
    pallas_call x0 -> x6, Pallas kernels: none -> 142 us  [the longest x1 42.2 us: body(): pl.pallas_call(functools.partial(backward_kernel, rel_a, scat_a, block),...]
    reduce_sum x22 -> x2, other arithmetic: 132 us -> 1.46 us  [the longest x1 1.11 us: body(): jnp.sum((routes[..., None] == jnp.arange(EXPERTS, dtype=jnp.int32)).astyp...]
    convert_element_type x12 -> x2, other arithmetic: 125 us -> 1 us  [the longest x1 0.72 us: body(): live_list = own_first(live.astype(jnp.int32))]
  transfers between devices with their start and end apart: 11 -> 142, of which waited for: 5 -> 70; matrix products, arithmetic and copies ran while one was open for 37% -> 23% of each run, Pallas kernels for 0% -> 18%
where the time goes in v1:
time: 810 us; the launch traced here: 797 us
  waiting for transfers between devices  299 us (37%)
  starting transfers between devices  158 us (20%)
  Pallas kernels  142 us (18%)
  other arithmetic  139 us (17%)
  local copies, waits for them, and re-layouts  54.7 us (7%)
    ppermute x68, waiting for transfers between devices, hyper_scatter(): got = lax.ppermute(send, 'dp', swap(n, 1 << bit))  169 us
    ppermute x68, waiting for transfers between devices, hyper_gather(): pieces.append(lax.ppermute(send, 'dp', swap(n, 1 << bit)))  130 us
    pallas_call x7, other arithmetic, body(): pl.pallas_call(functools.partial(expert_kernel, at, rel_a, rel_b, scat_a,...  93.1 us
    ppermute x68, starting transfers between devices, hyper_scatter(): got = lax.ppermute(send, 'dp', swap(n, 1 << bit))  89.7 us
    ppermute x68, starting transfers between devices, hyper_gather(): pieces.append(lax.ppermute(send, 'dp', swap(n, 1 << bit)))  68.1 us
    pallas_call x1, Pallas kernels, body(): pl.pallas_call(functools.partial(backward_kernel, rel_a, scat_a, block),...  42.2 us
    pallas_call x2, Pallas kernels, combine(): pl.pallas_call(functools.partial(combine_kernel, base), grid_spec=pltpu.P...  36.2 us
    concatenate x51, other arithmetic, hyper_gather(): send = pieces[0] if len(pieces) == 1 else jnp.concatenate(pieces, 0)  31.3 us
  transfers between devices with their start and end apart: 142, of which 70 were waited for; matrix products, arithmetic and copies ran while one was open for 23% of the time, Pallas kernels for 18%

profile of v1, /device:TPU:0, one launch (start us, length us, event | category | flops | bytes accessed | tf_op | source)
XLA Modules:
  0.0 796.6 jit_solution(2649392449452471035)
XLA Ops:
  4.7 4.1 collective-permute-start
  33.2 4.3 collective-permute-done.6.refs_1_
  37.5 5.3 collective-permute-done.14
  42.8 6.7 collective-permute-done.22
  49.5 7.8 collective-permute-done.30
  67.4 3.4 collective-permute-start.18
  78.3 3.0 collective-permute-start.34
  83.8 3.4 collective-permute-start.42
  98.1 6.3 collective-permute-done.1
  114.9 4.1 collective-permute-done.15
  123.3 5.6 collective-permute-done.3
  136.8 4.2 collective-permute-done.11.refs_7_
  159.6 22.6 %forward.1 = (bf16[8,208,640]{2,1,0:T(8,128)(2,1)}, f32[8,208,512]{2,1,0:T(8,128)}, bf16[8,208,1536]{2,1,0:T(8,128)(2,1)}, bf16[8,208,512]{2,1,0:T(8,128)(2,1)},...) custom-call(s32[256]{0:T(256)} %concatenate.181.info, bf16[2,8,197,512]{3,2,1,0:T(8,128)(2,1)} %copy.75.tok, ...), custom_call_target="tpu_custom_call" | custom-call | flops 15000000512 | bytes 20000000 | tf_op jit(solution)/shard_map/forward/pallas_call | solution.py:654
  186.9 4.7 collective-permute-done.40
  191.6 5.5 collective-permute-done.16
  198.0 4.7 collective-permute-done.24
  212.1 5.6 collective-permute-done.36
  223.3 5.6 collective-permute-done.12.refs_8_
  229.2 5.3 collective-permute-done.60
  234.6 4.1 collective-permute-done.20
  249.4 11.3 %collective-permute-done.29 = bf16[8,1,32,1024]{3,2,1,0:T(8,128)(2,1)} collective-permute-done((bf16[8,1,32,1024]{3,2,1,0:T(8,128)(2,1)S(1)}, bf16[8,1,32,1024]{3,2,1,0:T(8,128)(2,1)}, u32[]{:S(2)}, u32[]{:S(2)}) %collective-permute-start.29) | collective-permute-done | bytes 524320 | tf_op jit(solution)/shard_map/ppermute | solution.py:520
  260.7 11.2 %collective-permute-done.13.refs_9_ = bf16[8,1,32,1024]{3,2,1,0:T(8,128)(2,1)} collective-permute-done((bf16[8,1,32,1024]{3,2,1,0:T(8,128)(2,1)S(1)}, bf16[8,1,32,1024]{3,2,1,0:T(8,128)(2,1)}, u32[]{:S(2)}, u32[]{:S(2)}) %collective-permute-start.13) | collective-permute-done | bytes 524320 | tf_op jit(solution)/shard_map/ppermute | solution.py:520
  274.0 27.9 %dispatch.1.x = bf16[8,1280,1152]{2,1,0:T(8,128)(2,1)} custom-call(s32[256]{0:T(256)} %concatenate.181.info, bf16[8,208,640]{2,1,0:T(8,128)(2,1)} %get-tuple-element.59.own, bf16[8,208,640]{2,1,0:T(8,128)(2,1)} %collective-permute-done.5.oth, bf16[2,8,197,512]{3,2,1,0:T(8,128)(2,1)} %copy.76.gy.gy_ref, bf16[2,8,208,128]{3,2,1,0:T(8,128)(2,1)} %pad_convert_fusion.mask), custom_call_target="tpu_custom_call" | custom-call | flops 12000000000 | bytes 30000000 | tf_op jit(solution)/shard_map/dispatch/pallas_call | solution.py:684
  302.0 13.3 %expert.8 = (bf16[1,1536,1152]{2,1,0:T(8,128)(2,1)}, bf16[8,1,32,1024]{3,2,1,0:T(8,128)(2,1)}, bf16[8,1,32,1024]{3,2,1,0:T(8,128)(2,1)}, bf16[8,1,32,1024]{3,2,1,0:T(8,128)(2,1)}, bf16[8,1,32,1024]{3,2,1,0:T(8,128)(2,1)}) custom-call(s32[256]{0:T(256)} %concatenate.181.info, bf16[8,1280,1152]{2,1,0:T(8,128)(2,1)} %dispatch.1.x, ...), custom_call_target="tpu_custom_call" | custom-call | flops 5000000000 | bytes 12000000 | tf_op jit(solution)/shard_map/expert/pallas_call | solution.py:722
  319.5 4.0 constant_dynamic-update-slice_fusion.12
  323.6 12.0 %expert.15 = (bf16[8,1536,1152]{2,1,0:T(8,128)(2,1)}, bf16[8,1,32,1024]{3,2,1,0:T(8,128)(2,1)S(1)}, bf16[8,1,32,1024]{3,2,1,0:T(8,128)(2,1)}, bf16[8,1,32,1024]{3,2,1,0:T(8,128)(2,1)S(1)}, bf16[8,1,32,1024]{3,2,1,0:T(8,128)(2,1)}) fusion(bf16[8,1536,1152]{2,1,0:T(8,128)(2,1)} %constant_dynamic-update-slice_fusion.12, s32[256]{0:T(256)S(1)} %copy-done.92, ...), kind=kCustom, calls=%fused_computation.213 | custom fusion | flops 5000000000 | bytes 31327232 | tf_op jit(solution)/shard_map/expert/pallas_call | solution.py:722
  335.6 16.4 %expert.14 = (bf16[8,1536,1152]{2,1,0:T(8,128)(2,1)}, bf16[8,1,32,1024]{3,2,1,0:T(8,128)(2,1)S(1)}, bf16[8,1,32,1024]{3,2,1,0:T(8,128)(2,1)}, bf16[8,1,32,1024]{3,2,1,0:T(8,128)(2,1)S(1)}, bf16[8,1,32,1024]{3,2,1,0:T(8,128)(2,1)}) fusion(bf16[8,1536,1152]{2,1,0:T(8,128)(2,1)} %get-tuple-element.272, s32[256]{0:T(256)S(1)} %copy-done.92, ...), kind=kCustom, calls=%fused_computation.212 | custom fusion | flops 5000000000 | bytes 31327232 | tf_op jit(solution)/shard_map/expert/pallas_call | solution.py:722
  352.0 9.1 %expert.13 = (bf16[8,1536,1152]{2,1,0:T(8,128)(2,1)}, bf16[8,1,32,1024]{3,2,1,0:T(8,128)(2,1)S(1)}, bf16[8,1,32,1024]{3,2,1,0:T(8,128)(2,1)}, bf16[8,1,32,1024]{3,2,1,0:T(8,128)(2,1)S(1)}, bf16[8,1,32,1024]{3,2,1,0:T(8,128)(2,1)}) fusion(bf16[8,1536,1152]{2,1,0:T(8,128)(2,1)} %get-tuple-element.262, s32[256]{0:T(256)S(1)} %copy-done.92, ...), kind=kCustom, calls=%fused_computation.211 | custom fusion | flops 5000000000 | bytes 31327232 | tf_op jit(solution)/shard_map/expert/pallas_call | solution.py:722
  361.1 11.4 %expert.12 = (bf16[8,1536,1152]{2,1,0:T(8,128)(2,1)}, bf16[8,1,32,1024]{3,2,1,0:T(8,128)(2,1)S(1)}, bf16[8,1,32,1024]{3,2,1,0:T(8,128)(2,1)}, bf16[8,1,32,1024]{3,2,1,0:T(8,128)(2,1)S(1)}, bf16[8,1,32,1024]{3,2,1,0:T(8,128)(2,1)}) fusion(bf16[8,1536,1152]{2,1,0:T(8,128)(2,1)} %get-tuple-element.282, s32[256]{0:T(256)S(1)} %copy-done.92, ...), kind=kCustom, calls=%fused_computation.210 | custom fusion | flops 5000000000 | bytes 31327232 | tf_op jit(solution)/shard_map/expert/pallas_call | solution.py:722
  372.7 15.5 %expert.11 = (bf16[8,1536,1152]{2,1,0:T(8,128)(2,1)}, bf16[8,1,32,1024]{3,2,1,0:T(8,128)(2,1)S(1)}, bf16[8,1,32,1024]{3,2,1,0:T(8,128)(2,1)}, bf16[8,1,32,1024]{3,2,1,0:T(8,128)(2,1)S(1)}, bf16[8,1,32,1024]{3,2,1,0:T(8,128)(2,1)}) fusion(bf16[8,1536,1152]{2,1,0:T(8,128)(2,1)} %get-tuple-element.252, s32[256]{0:T(256)S(1)} %copy-done.92, ...), kind=kCustom, calls=%fused_computation.209 | custom fusion | flops 5000000000 | bytes 31327232 | tf_op jit(solution)/shard_map/expert/pallas_call | solution.py:722
  388.3 12.9 %expert.10 = (bf16[8,1536,1152]{2,1,0:T(8,128)(2,1)}, bf16[8,1,32,1024]{3,2,1,0:T(8,128)(2,1)}, bf16[8,1,32,1024]{3,2,1,0:T(8,128)(2,1)}, bf16[8,1,32,1024]{3,2,1,0:T(8,128)(2,1)S(1)}, bf16[8,1,32,1024]{3,2,1,0:T(8,128)(2,1)}) fusion(bf16[8,1536,1152]{2,1,0:T(8,128)(2,1)} %get-tuple-element.312, s32[256]{0:T(256)S(1)} %copy-done.92, ...), kind=kCustom, calls=%fused_computation.208 | custom fusion | flops 5000000000 | bytes 31327232 | tf_op jit(solution)/shard_map/expert/pallas_call | solution.py:722
  401.3 15.8 %expert.9 = (bf16[8,1536,1152]{2,1,0:T(8,128)(2,1)}, bf16[8,1,32,1024]{3,2,1,0:T(8,128)(2,1)}, bf16[8,1,32,1024]{3,2,1,0:T(8,128)(2,1)}, bf16[8,1,32,1024]{3,2,1,0:T(8,128)(2,1)}, bf16[8,1,32,1024]{3,2,1,0:T(8,128)(2,1)}) fusion(bf16[8,1536,1152]{2,1,0:T(8,128)(2,1)} %get-tuple-element.302, s32[256]{0:T(256)S(1)} %copy-done.92, ...), kind=kCustom, calls=%fused_computation.207 | custom fusion | flops 5000000000 | bytes 31327232 | tf_op jit(solution)/shard_map/expert/pallas_call | solution.py:722
  417.2 18.4 %combine.3 = bf16[8,208,1152]{2,1,0:T(8,128)(2,1)} custom-call(s32[256]{0:T(256)} %concatenate.181.info, bf16[8,1536,1152]{2,1,0:T(8,128)(2,1)} %get-tuple-element.292.y_hbm, bf16[2,8,208,128]{3,2,1,0:T(8,128)(2,1)} %pad_convert_fusion.mask), custom_call_target="tpu_custom_call" | custom-call | flops 5000000000 | bytes 25000000 | tf_op jit(solution)/shard_map/combine/pallas_call | solution.py:759
  435.6 17.8 %combine.2.comb_own = f32[8,208,1152]{2,1,0:T(8,128)} custom-call(s32[256]{0:T(256)} %concatenate.181.info, bf16[8,1536,1152]{2,1,0:T(8,128)(2,1)} %get-tuple-element.292.y_hbm, bf16[2,8,208,128]{3,2,1,0:T(8,128)(2,1)} %pad_convert_fusion.mask), custom_call_target="tpu_custom_call" | custom-call | flops 5000000000 | bytes 25000000 | tf_op jit(solution)/shard_map/combine/pallas_call | solution.py:759
  461.4 7.2 collective-permute-done.138
  470.7 9.1 %collective-permute-done.134 = bf16[8,1,32,1024]{3,2,1,0:T(8,128)(2,1)S(1)} collective-permute-done((bf16[8,1,32,1024]{3,2,1,0:T(8,128)(2,1)}, bf16[8,1,32,1024]{3,2,1,0:T(8,128)(2,1)S(1)}, u32[]{:S(2)}, u32[]{:S(2)}) %collective-permute-start.134) | collective-permute-done | bytes 524320 | tf_op jit(solution)/shard_map/ppermute | solution.py:526
  481.9 9.1 %collective-permute-done.130 = bf16[8,1,32,1024]{3,2,1,0:T(8,128)(2,1)S(1)} collective-permute-done((bf16[8,1,32,1024]{3,2,1,0:T(8,128)(2,1)}, bf16[8,1,32,1024]{3,2,1,0:T(8,128)(2,1)S(1)}, u32[]{:S(2)}, u32[]{:S(2)}) %collective-permute-start.130) | collective-permute-done | bytes 524320 | tf_op jit(solution)/shard_map/ppermute | solution.py:526
  493.1 9.1 %collective-permute-done.126 = bf16[8,1,32,1024]{3,2,1,0:T(8,128)(2,1)S(1)} collective-permute-done((bf16[8,1,32,1024]{3,2,1,0:T(8,128)(2,1)S(1)}, bf16[8,1,32,1024]{3,2,1,0:T(8,128)(2,1)S(1)}, u32[]{:S(2)}, u32[]{:S(2)}) %collective-permute-start.126) | collective-permute-done | bytes 524320 | tf_op jit(solution)/shard_map/ppermute | solution.py:526
  504.3 9.1 %collective-permute-done.122 = bf16[8,1,32,1024]{3,2,1,0:T(8,128)(2,1)S(1)} collective-permute-done((bf16[8,1,32,1024]{3,2,1,0:T(8,128)(2,1)S(1)}, bf16[8,1,32,1024]{3,2,1,0:T(8,128)(2,1)S(1)}, u32[]{:S(2)}, u32[]{:S(2)}) %collective-permute-start.122) | collective-permute-done | bytes 524320 | tf_op jit(solution)/shard_map/ppermute | solution.py:526
  513.7 10.8 %collective-permute-done.118 = bf16[8,1,32,1024]{3,2,1,0:T(8,128)(2,1)S(1)} collective-permute-done((bf16[8,1,32,1024]{3,2,1,0:T(8,128)(2,1)S(1)}, bf16[8,1,32,1024]{3,2,1,0:T(8,128)(2,1)S(1)}, u32[]{:S(2)}, u32[]{:S(2)}) %collective-permute-start.118) | collective-permute-done | bytes 524320 | tf_op jit(solution)/shard_map/ppermute | solution.py:526
  524.9 10.8 %collective-permute-done.114 = bf16[8,1,32,1024]{3,2,1,0:T(8,128)(2,1)S(1)} collective-permute-done((bf16[8,1,32,1024]{3,2,1,0:T(8,128)(2,1)S(1)}, bf16[8,1,32,1024]{3,2,1,0:T(8,128)(2,1)S(1)}, u32[]{:S(2)}, u32[]{:S(2)}) %collective-permute-start.114) | collective-permute-done | bytes 524320 | tf_op jit(solution)/shard_map/ppermute | solution.py:526
  535.8 5.6 collective-permute-done.79
  541.8 5.2 collective-permute-done.107
  547.4 5.2 collective-permute-done.103
  553.0 5.2 collective-permute-done.99
  558.6 4.2 collective-permute-done.95
  569.1 20.1 %collective-permute-start.80 = (bf16[2,1,32,1024]{3,2,1,0:T(8,128)(2,1)S(1)}, bf16[2,1,32,1024]{3,2,1,0:T(8,128)(2,1)S(1)}, u32[]{:S(2)}, u32[]{:S(2)}) collective-permute-start(bf16[2,1,32,1024]{3,2,1,0:T(8,128)(2,1)S(1)} %get-tuple-element.218), channel_id=1, source_target_pairs={{0,8},{2,10},{4,12},{6,14},{8,0},{10,2},{12,4},{14,6},{16,24},{18,... | collective-permute-start | bytes 393224 | tf_op jit(solution)/shard_map/ppermute | solution.py:526
  631.9 3.5 collective-permute-done.113
  638.5 4.7 collective-permute-done.85
  644.2 6.6 collective-permute-done.89
  650.8 5.8 collective-permute-done.93
  656.7 5.3 collective-permute-done.97
  662.0 5.1 collective-permute-done.101
  667.2 3.0 collective-permute-start.129
  673.4 42.2 %backward.1 = (bf16[8,197,512]{2,1,0:T(8,128)(2,1)}, bf16[8,197,512]{2,1,0:T(8,128)(2,1)}, bf16[16,32,1152]{2,1,0:T(8,128)(2,1)}, bf16[16,32,1152]{2,1,0:T(8,128)(2,1)}) custom-call(s32[256]{0:T(256)} %concatenate.181.info, bf16[2,8,197,512]{3,2,1,0:T(8,128)(2,1)} %copy.75.tok, bf16[2,8,197,512]{3,2,1,0:T(8,128)(2,1)} %copy.76.gy.gy_ref, ...), custom_call_target="tpu_custom_call" | custom-call | flops 24999999488 | bytes 30000000 | tf_op jit(solution)/shard_map/backward/pallas_call | solution.py:787
  723.4 3.3 collective-permute-done.133
  729.6 13.8 %collective-permute-done.74 = bf16[8,32,1152]{2,1,0:T(8,128)(2,1)S(1)} collective-permute-done((bf16[8,32,1152]{2,1,0:T(8,128)(2,1)S(1)}, bf16[8,32,1152]{2,1,0:T(8,128)(2,1)S(1)}, u32[]{:S(2)}, u32[]{:S(2)}) %collective-permute-start.74) | collective-permute-done | bytes 589856 | tf_op jit(solution)/shard_map/ppermute | solution.py:526
  744.6 7.6 collective-permute-done.75
  752.3 10.6 %collective-permute-start.76 = (bf16[2,32,1152]{2,1,0:T(8,128)(2,1)S(1)}, bf16[2,32,1152]{2,1,0:T(8,128)(2,1)S(1)}, u32[]{:S(2)}, u32[]{:S(2)}) collective-permute-start(bf16[2,32,1152]{2,1,0:T(8,128)(2,1)S(1)} %get-tuple-element.186), channel_id=1, source_target_pairs={{0,8},{2,10},{4,12},{6,14},{8,0},{10,2},{12,4},{14,6},{16,24},{18,... | collective-permute-start | bytes 442376 | tf_op jit(solution)/shard_map/ppermute | solution.py:526
  763.2 3.2 collective-permute-done.76
  767.3 5.0 copy.84
  772.3 7.8 reshape.222
  780.1 5.0 copy.80
  785.2 7.7 reshape.221
  (608 shorter events, 229.8 us)
Async XLA Ops:
  4.7 87.6 %collective-permute-start = (bf16[1,32,1152]{2,1,0:T(8,128)(2,1)S(1)}, bf16[1,32,1152]{2,1,0:T(8,128)(2,1)}, u32[]{:S(2)}, u32[]{:S(2)}) collective-permute-start(bf16[1,32,1152]{2,1,0:T(8,128)(2,1)S(1)} %bitcast.115), channel_id=1, source_target_pairs={{0,16},{2,18},{4,20},{6,22},{8,24},{10,26},{12,28},{14,30},{16,0},... | collective-permute-start | bytes 221192 | tf_op jit(solution)/shard_map/ppermute | solution.py:520
  10.6 51.6 %collective-permute-start.62 = (bf16[1,1,32,1024]{3,2,1,0:T(8,128)(2,1)S(1)}, bf16[1,1,32,1024]{3,2,1,0:T(8,128)(2,1)}, u32[]{:S(2)}, u32[]{:S(2)}) collective-permute-start(bf16[1,1,32,1024]{3,2,1,0:T(8,128)(2,1)S(1)} %get-tuple-element.227), channel_id=1, source_target_pairs={{0,16},{2,18},{4,20},{6,22},{8,24},{10,26},{12,28},{14,30},{16,0},... | collective-permute-start | bytes 196616 | tf_op jit(solution)/shard_map/ppermute | solution.py:520
  10.6 50.6 %collective-permute-start.46 = (bf16[1,1,32,1024]{3,2,1,0:T(8,128)(2,1)S(1)}, bf16[1,1,32,1024]{3,2,1,0:T(8,128)(2,1)}, u32[]{:S(2)}, u32[]{:S(2)}) collective-permute-start(bf16[1,1,32,1024]{3,2,1,0:T(8,128)(2,1)S(1)} %get-tuple-element.228), channel_id=1, source_target_pairs={{0,16},{2,18},{4,20},{6,22},{8,24},{10,26},{12,28},{14,30},{16,0},... | collective-permute-start | bytes 196616 | tf_op jit(solution)/shard_map/ppermute | solution.py:520
  13.5 43.8 %collective-permute-start.38 = (bf16[1,1,32,1024]{3,2,1,0:T(8,128)(2,1)}, bf16[1,1,32,1024]{3,2,1,0:T(8,128)(2,1)}, u32[]{:S(2)}, u32[]{:S(2)}) collective-permute-start(bf16[1,1,32,1024]{3,2,1,0:T(8,128)(2,1)} %get-tuple-element.229), channel_id=1, source_target_pairs={{0,16},{2,18},{4,20},{6,22},{8,24},{10,26},{12,28},{14,30},{16,0},... | collective-permute-start | bytes 196616 | tf_op jit(solution)/shard_map/ppermute | solution.py:520
  57.3 38.8 %collective-permute-start.66 = (bf16[1,1,32,1024]{3,2,1,0:T(8,128)(2,1)S(1)}, bf16[1,1,32,1024]{3,2,1,0:T(8,128)(2,1)S(1)}, u32[]{:S(2)}, u32[]{:S(2)}) collective-permute-start(bf16[1,1,32,1024]{3,2,1,0:T(8,128)(2,1)S(1)} %copy-done.8), channel_id=1, source_target_pairs={{0,16},{2,18},{4,20},{6,22},{8,24},{10,26},{12,28},{14,30},{16,0},... | collective-permute-start | bytes 196616 | tf_op jit(solution)/shard_map/ppermute | solution.py:520
  57.4 38.0 %collective-permute-start.58 = (bf16[1,1,32,1024]{3,2,1,0:T(8,128)(2,1)S(1)}, bf16[1,1,32,1024]{3,2,1,0:T(8,128)(2,1)S(1)}, u32[]{:S(2)}, u32[]{:S(2)}) collective-permute-start(bf16[1,1,32,1024]{3,2,1,0:T(8,128)(2,1)S(1)} %copy-done.9), channel_id=1, source_target_pairs={{0,16},{2,18},{4,20},{6,22},{8,24},{10,26},{12,28},{14,30},{16,0},... | collective-permute-start | bytes 196616 | tf_op jit(solution)/shard_map/ppermute | solution.py:520
  61.2 31.0 %collective-permute-start.50 = (bf16[1,1,32,1024]{3,2,1,0:T(8,128)(2,1)S(1)}, bf16[1,1,32,1024]{3,2,1,0:T(8,128)(2,1)S(1)}, u32[]{:S(2)}, u32[]{:S(2)}) collective-permute-start(bf16[1,1,32,1024]{3,2,1,0:T(8,128)(2,1)S(1)} %copy-done.12), channel_id=1, source_target_pairs={{0,16},{2,18},{4,20},{6,22},{8,24},{10,26},{12,28},{14,30},{16,0},... | collective-permute-start | bytes 196616 | tf_op jit(solution)/shard_map/ppermute | solution.py:520
  89.5 46.0 %collective-permute-start.63 = (bf16[2,1,32,1024]{3,2,1,0:T(8,128)(2,1)S(1)}, bf16[2,1,32,1024]{3,2,1,0:T(8,128)(2,1)S(1)}, u32[]{:S(2)}, u32[]{:S(2)}) collective-permute-start(bf16[2,1,32,1024]{3,2,1,0:T(8,128)(2,1)S(1)} %pad_maximum_fusion.51), channel_id=1, source_target_pairs={{0,8},{2,10},{4,12},{6,14},{8,0},{10,2},{12,4},{14,6},{16,24},{18,... | collective-permute-start | bytes 393224 | tf_op jit(solution)/shard_map/ppermute | solution.py:520
  92.2 40.6 %collective-permute-start.47 = (bf16[2,1,32,1024]{3,2,1,0:T(8,128)(2,1)S(1)}, bf16[2,1,32,1024]{3,2,1,0:T(8,128)(2,1)S(1)}, u32[]{:S(2)}, u32[]{:S(2)}) collective-permute-start(bf16[2,1,32,1024]{3,2,1,0:T(8,128)(2,1)S(1)} %pad_maximum_fusion.47), channel_id=1, source_target_pairs={{0,8},{2,10},{4,12},{6,14},{8,0},{10,2},{12,4},{14,6},{16,24},{18,... | collective-permute-start | bytes 393224 | tf_op jit(solution)/shard_map/ppermute | solution.py:520
  92.3 18.8 %collective-permute-start.7 = (bf16[2,1,32,1024]{3,2,1,0:T(8,128)(2,1)S(1)}, bf16[2,1,32,1024]{3,2,1,0:T(8,128)(2,1)S(1)}, u32[]{:S(2)}, u32[]{:S(2)}) collective-permute-start(bf16[2,1,32,1024]{3,2,1,0:T(8,128)(2,1)S(1)} %pad_maximum_fusion.37), channel_id=1, source_target_pairs={{0,8},{2,10},{4,12},{6,14},{8,0},{10,2},{12,4},{14,6},{16,24},{18,... | collective-permute-start | bytes 393224 | tf_op jit(solution)/shard_map/ppermute | solution.py:520
  109.2 22.4 %collective-permute-start.39 = (bf16[2,1,32,1024]{3,2,1,0:T(8,128)(2,1)S(1)}, bf16[2,1,32,1024]{3,2,1,0:T(8,128)(2,1)S(1)}, u32[]{:S(2)}, u32[]{:S(2)}) collective-permute-start(bf16[2,1,32,1024]{3,2,1,0:T(8,128)(2,1)S(1)} %pad_maximum_fusion.45), channel_id=1, source_target_pairs={{0,8},{2,10},{4,12},{6,14},{8,0},{10,2},{12,4},{14,6},{16,24},{18,... | collective-permute-start | bytes 393224 | tf_op jit(solution)/shard_map/ppermute | solution.py:520
  128.9 27.7 %collective-permute-start.67 = (bf16[2,1,32,1024]{3,2,1,0:T(8,128)(2,1)S(1)}, bf16[2,1,32,1024]{3,2,1,0:T(8,128)(2,1)S(1)}, u32[]{:S(2)}, u32[]{:S(2)}) collective-permute-start(bf16[2,1,32,1024]{3,2,1,0:T(8,128)(2,1)S(1)} %pad_maximum_fusion.52), channel_id=1, source_target_pairs={{0,8},{2,10},{4,12},{6,14},{8,0},{10,2},{12,4},{14,6},{16,24},{18,... | collective-permute-start | bytes 393224 | tf_op jit(solution)/shard_map/ppermute | solution.py:520
  130.6 27.3 %collective-permute-start.4 = (bf16[16,32,1152]{2,1,0:T(8,128)(2,1)S(1)}, bf16[16,32,1152]{2,1,0:T(8,128)(2,1)S(1)}, u32[]{:S(2)}, u32[]{:S(2)}) collective-permute-start(bf16[16,32,1152]{2,1,0:T(8,128)(2,1)S(1)} %constant_dynamic-update-slice_fusion.refs_0_), channel_id=1, source_target_pairs={{0,1},{1,0},{2,3},{3,2},{4,5},{5,4},{6,7},{7,6},{8,9},{9,8},{10,11... | collective-permute-start | bytes 3538952 | tf_op jit(solution)/shard_map/ppermute | solution.py:593
  131.6 50.6 %collective-permute-start.59 = (bf16[2,1,32,1024]{3,2,1,0:T(8,128)(2,1)}, bf16[2,1,32,1024]{3,2,1,0:T(8,128)(2,1)S(1)}, u32[]{:S(2)}, u32[]{:S(2)}) collective-permute-start(bf16[2,1,32,1024]{3,2,1,0:T(8,128)(2,1)} %pad_maximum_fusion.50), channel_id=1, source_target_pairs={{0,8},{2,10},{4,12},{6,14},{8,0},{10,2},{12,4},{14,6},{16,24},{18,... | collective-permute-start | bytes 393224 | tf_op jit(solution)/shard_map/ppermute | solution.py:520
  153.0 29.4 %collective-permute-start.64 = (bf16[4,1,32,1024]{3,2,1,0:T(8,128)(2,1)S(1)}, bf16[4,1,32,1024]{3,2,1,0:T(8,128)(2,1)S(1)}, u32[]{:S(2)}, u32[]{:S(2)}) collective-permute-start(bf16[4,1,32,1024]{3,2,1,0:T(8,128)(2,1)S(1)} %pad_maximum_fusion.34), channel_id=1, source_target_pairs={{0,4},{2,6},{4,0},{6,2},{8,12},{10,14},{12,8},{14,10},{16,20},{18,... | collective-permute-start | bytes 786440 | tf_op jit(solution)/shard_map/ppermute | solution.py:520
  155.2 27.3 %collective-permute-start.48 = (bf16[4,1,32,1024]{3,2,1,0:T(8,128)(2,1)S(1)}, bf16[4,1,32,1024]{3,2,1,0:T(8,128)(2,1)S(1)}, u32[]{:S(2)}, u32[]{:S(2)}) collective-permute-start(bf16[4,1,32,1024]{3,2,1,0:T(8,128)(2,1)S(1)} %pad_maximum_fusion.30), channel_id=1, source_target_pairs={{0,4},{2,6},{4,0},{6,2},{8,12},{10,14},{12,8},{14,10},{16,20},{18,... | collective-permute-start | bytes 786440 | tf_op jit(solution)/shard_map/ppermute | solution.py:520
  156.5 28.0 %collective-permute-start.8 = (bf16[4,1,32,1024]{3,2,1,0:T(8,128)(2,1)}, bf16[4,1,32,1024]{3,2,1,0:T(8,128)(2,1)S(1)}, u32[]{:S(2)}, u32[]{:S(2)}) collective-permute-start(bf16[4,1,32,1024]{3,2,1,0:T(8,128)(2,1)} %pad_maximum_fusion.20), channel_id=1, source_target_pairs={{0,4},{2,6},{4,0},{6,2},{8,12},{10,14},{12,8},{14,10},{16,20},{18,... | collective-permute-start | bytes 786440 | tf_op jit(solution)/shard_map/ppermute | solution.py:520
  159.0 25.8 %collective-permute-start.56 = (bf16[4,1,32,1024]{3,2,1,0:T(8,128)(2,1)}, bf16[4,1,32,1024]{3,2,1,0:T(8,128)(2,1)S(1)}, u32[]{:S(2)}, u32[]{:S(2)}) collective-permute-start(bf16[4,1,32,1024]{3,2,1,0:T(8,128)(2,1)} %pad_maximum_fusion.32), channel_id=1, source_target_pairs={{0,4},{2,6},{4,0},{6,2},{8,12},{10,14},{12,8},{14,10},{16,20},{18,... | collective-permute-start | bytes 786440 | tf_op jit(solution)/shard_map/ppermute | solution.py:520
  182.2 91.7 %collective-permute-start.5 = (bf16[8,208,640]{2,1,0:T(8,128)(2,1)}, bf16[8,208,640]{2,1,0:T(8,128)(2,1)}, u32[]{:S(2)}, u32[]{:S(2)}) collective-permute-start(bf16[8,208,640]{2,1,0:T(8,128)(2,1)} %get-tuple-element.59.own), channel_id=1, source_target_pairs={{0,1},{1,0},{2,3},{3,2},{4,5},{5,4},{6,7},{7,6},{8,9},{9,8},{10,11... | collective-permute-start | bytes 6389768 | tf_op jit(solution)/shard_map/ppermute | solution.py:593
  208.0 20.8 %collective-permute-start.12 = (bf16[4,1,32,1024]{3,2,1,0:T(8,128)(2,1)S(1)}, bf16[4,1,32,1024]{3,2,1,0:T(8,128)(2,1)S(1)}, u32[]{:S(2)}, u32[]{:S(2)}) collective-permute-start(bf16[4,1,32,1024]{3,2,1,0:T(8,128)(2,1)S(1)} %copy-done.87), channel_id=1, source_target_pairs={{0,2},{2,0},{4,6},{6,4},{8,10},{10,8},{12,14},{14,12},{16,18},{18,... | collective-permute-start | bytes 786440 | tf_op jit(solution)/shard_map/ppermute | solution.py:520
  212.0 27.1 %collective-permute-start.53 = (bf16[8,1,32,1024]{3,2,1,0:T(8,128)(2,1)S(1)}, bf16[8,1,32,1024]{3,2,1,0:T(8,128)(2,1)S(1)}, u32[]{:S(2)}, u32[]{:S(2)}) collective-permute-start(bf16[8,1,32,1024]{3,2,1,0:T(8,128)(2,1)S(1)} %pad_maximum_fusion.14), channel_id=1, source_target_pairs={{0,4},{2,6},{4,0},{6,2},{8,12},{10,14},{12,8},{14,10},{16,20},{18,... | collective-permute-start | bytes 1572872 | tf_op jit(solution)/shard_map/ppermute | solution.py:520
  217.7 23.0 %collective-permute-start.45 = (bf16[8,1,32,1024]{3,2,1,0:T(8,128)(2,1)S(1)}, bf16[8,1,32,1024]{3,2,1,0:T(8,128)(2,1)S(1)}, u32[]{:S(2)}, u32[]{:S(2)}) collective-permute-start(bf16[8,1,32,1024]{3,2,1,0:T(8,128)(2,1)S(1)} %pad_maximum_fusion.12), channel_id=1, source_target_pairs={{0,4},{2,6},{4,0},{6,2},{8,12},{10,14},{12,8},{14,10},{16,20},{18,... | collective-permute-start | bytes 1572872 | tf_op jit(solution)/shard_map/ppermute | solution.py:520
  238.6 22.1 %collective-permute-start.29 = (bf16[8,1,32,1024]{3,2,1,0:T(8,128)(2,1)S(1)}, bf16[8,1,32,1024]{3,2,1,0:T(8,128)(2,1)}, u32[]{:S(2)}, u32[]{:S(2)}) collective-permute-start(bf16[8,1,32,1024]{3,2,1,0:T(8,128)(2,1)S(1)} %pad_maximum_fusion.8), channel_id=1, source_target_pairs={{0,4},{2,6},{4,0},{6,2},{8,12},{10,14},{12,8},{14,10},{16,20},{18,... | collective-permute-start | bytes 1572872 | tf_op jit(solution)/shard_map/ppermute | solution.py:520
  239.1 32.8 %collective-permute-start.13 = (bf16[8,1,32,1024]{3,2,1,0:T(8,128)(2,1)S(1)}, bf16[8,1,32,1024]{3,2,1,0:T(8,128)(2,1)}, u32[]{:S(2)}, u32[]{:S(2)}) collective-permute-start(bf16[8,1,32,1024]{3,2,1,0:T(8,128)(2,1)S(1)} %pad_maximum_fusion.4), channel_id=1, source_target_pairs={{0,4},{2,6},{4,0},{6,2},{8,12},{10,14},{12,8},{14,10},{16,20},{18,... | collective-permute-start | bytes 1572872 | tf_op jit(solution)/shard_map/ppermute | solution.py:520
  240.6 31.3 %collective-permute-start.9 = (bf16[8,1,32,1024]{3,2,1,0:T(8,128)(2,1)S(1)}, bf16[8,1,32,1024]{3,2,1,0:T(8,128)(2,1)}, u32[]{:S(2)}, u32[]{:S(2)}) collective-permute-start(bf16[8,1,32,1024]{3,2,1,0:T(8,128)(2,1)S(1)} %pad_maximum_fusion.3), channel_id=1, source_target_pairs={{0,2},{2,0},{4,6},{6,4},{8,10},{10,8},{12,14},{14,12},{16,18},{18,... | collective-permute-start | bytes 1572872 | tf_op jit(solution)/shard_map/ppermute | solution.py:520
  249.4 65.9 %collective-permute-start.21 = (bf16[8,1,32,1024]{3,2,1,0:T(8,128)(2,1)}, bf16[8,1,32,1024]{3,2,1,0:T(8,128)(2,1)}, u32[]{:S(2)}, u32[]{:S(2)}) collective-permute-start(bf16[8,1,32,1024]{3,2,1,0:T(8,128)(2,1)} %pad_maximum_fusion.6), channel_id=1, source_target_pairs={{0,4},{2,6},{4,0},{6,2},{8,12},{10,14},{12,8},{14,10},{16,20},{18,... | collective-permute-start | bytes 1572872 | tf_op jit(solution)/shard_map/ppermute | solution.py:520
  260.7 54.7 %collective-permute-start.41 = (bf16[8,1,32,1024]{3,2,1,0:T(8,128)(2,1)}, bf16[8,1,32,1024]{3,2,1,0:T(8,128)(2,1)S(1)}, u32[]{:S(2)}, u32[]{:S(2)}) collective-permute-start(bf16[8,1,32,1024]{3,2,1,0:T(8,128)(2,1)} %pad_maximum_fusion.11), channel_id=1, source_target_pairs={{0,2},{2,0},{4,6},{6,4},{8,10},{10,8},{12,14},{14,12},{16,18},{18,... | collective-permute-start | bytes 1572872 | tf_op jit(solution)/shard_map/ppermute | solution.py:520
  271.9 45.4 %collective-permute-start.33 = (bf16[8,1,32,1024]{3,2,1,0:T(8,128)(2,1)}, bf16[8,1,32,1024]{3,2,1,0:T(8,128)(2,1)S(1)}, u32[]{:S(2)}, u32[]{:S(2)}) collective-permute-start(bf16[8,1,32,1024]{3,2,1,0:T(8,128)(2,1)} %pad_maximum_fusion.9), channel_id=1, source_target_pairs={{0,2},{2,0},{4,6},{6,4},{8,10},{10,8},{12,14},{14,12},{16,18},{18,... | collective-permute-start | bytes 1572872 | tf_op jit(solution)/shard_map/ppermute | solution.py:520
  271.9 45.5 %collective-permute-start.25 = (bf16[8,1,32,1024]{3,2,1,0:T(8,128)(2,1)}, bf16[8,1,32,1024]{3,2,1,0:T(8,128)(2,1)}, u32[]{:S(2)}, u32[]{:S(2)}) collective-permute-start(bf16[8,1,32,1024]{3,2,1,0:T(8,128)(2,1)} %pad_maximum_fusion.7), channel_id=1, source_target_pairs={{0,2},{2,0},{4,6},{6,4},{8,10},{10,8},{12,14},{14,12},{16,18},{18,... | collective-permute-start | bytes 1572872 | tf_op jit(solution)/shard_map/ppermute | solution.py:520
  274.0 45.5 %collective-permute-start.17 = (bf16[8,1,32,1024]{3,2,1,0:T(8,128)(2,1)}, bf16[8,1,32,1024]{3,2,1,0:T(8,128)(2,1)}, u32[]{:S(2)}, u32[]{:S(2)}) collective-permute-start(bf16[8,1,32,1024]{3,2,1,0:T(8,128)(2,1)} %pad_maximum_fusion.5), channel_id=1, source_target_pairs={{0,2},{2,0},{4,6},{6,4},{8,10},{10,8},{12,14},{14,12},{16,18},{18,... | collective-permute-start | bytes 1572872 | tf_op jit(solution)/shard_map/ppermute | solution.py:520
  315.3 86.0 %collective-permute-start.69 = (bf16[8,1,32,1024]{3,2,1,0:T(8,128)(2,1)}, bf16[8,1,32,1024]{3,2,1,0:T(8,128)(2,1)}, u32[]{:S(2)}, u32[]{:S(2)}) collective-permute-start(bf16[8,1,32,1024]{3,2,1,0:T(8,128)(2,1)} %pad_maximum_fusion.18), channel_id=1, source_target_pairs={{0,4},{2,6},{4,0},{6,2},{8,12},{10,14},{12,8},{14,10},{16,20},{18,... | collective-permute-start | bytes 1572872 | tf_op jit(solution)/shard_map/ppermute | solution.py:520
  315.4 72.8 %collective-permute-start.61 = (bf16[8,1,32,1024]{3,2,1,0:T(8,128)(2,1)}, bf16[8,1,32,1024]{3,2,1,0:T(8,128)(2,1)}, u32[]{:S(2)}, u32[]{:S(2)}) collective-permute-start(bf16[8,1,32,1024]{3,2,1,0:T(8,128)(2,1)} %pad_maximum_fusion.16), channel_id=1, source_target_pairs={{0,4},{2,6},{4,0},{6,2},{8,12},{10,14},{12,8},{14,10},{16,20},{18,... | collective-permute-start | bytes 1572872 | tf_op jit(solution)/shard_map/ppermute | solution.py:520
  317.4 83.9 %collective-permute-start.65 = (bf16[8,1,32,1024]{3,2,1,0:T(8,128)(2,1)}, bf16[8,1,32,1024]{3,2,1,0:T(8,128)(2,1)}, u32[]{:S(2)}, u32[]{:S(2)}) collective-permute-start(bf16[8,1,32,1024]{3,2,1,0:T(8,128)(2,1)} %pad_maximum_fusion.17), channel_id=1, source_target_pairs={{0,2},{2,0},{4,6},{6,4},{8,10},{10,8},{12,14},{14,12},{16,18},{18,... | collective-permute-start | bytes 1572872 | tf_op jit(solution)/shard_map/ppermute | solution.py:520
  317.4 55.1 %collective-permute-start.49 = (bf16[8,1,32,1024]{3,2,1,0:T(8,128)(2,1)}, bf16[8,1,32,1024]{3,2,1,0:T(8,128)(2,1)}, u32[]{:S(2)}, u32[]{:S(2)}) collective-permute-start(bf16[8,1,32,1024]{3,2,1,0:T(8,128)(2,1)} %pad_maximum_fusion.13), channel_id=1, source_target_pairs={{0,2},{2,0},{4,6},{6,4},{8,10},{10,8},{12,14},{14,12},{16,18},{18,... | collective-permute-start | bytes 1572872 | tf_op jit(solution)/shard_map/ppermute | solution.py:520
  319.4 68.9 %collective-permute-start.57 = (bf16[8,1,32,1024]{3,2,1,0:T(8,128)(2,1)}, bf16[8,1,32,1024]{3,2,1,0:T(8,128)(2,1)}, u32[]{:S(2)}, u32[]{:S(2)}) collective-permute-start(bf16[8,1,32,1024]{3,2,1,0:T(8,128)(2,1)} %pad_maximum_fusion.15), channel_id=1, source_target_pairs={{0,2},{2,0},{4,6},{6,4},{8,10},{10,8},{12,14},{14,12},{16,18},{18,... | collective-permute-start | bytes 1572872 | tf_op jit(solution)/shard_map/ppermute | solution.py:520
  372.6 81.0 %collective-permute-start.78 = (bf16[8,1,32,1024]{3,2,1,0:T(8,128)(2,1)}, bf16[8,1,32,1024]{3,2,1,0:T(8,128)(2,1)}, u32[]{:S(2)}, u32[]{:S(2)}) collective-permute-start(bf16[8,1,32,1024]{3,2,1,0:T(8,128)(2,1)} %get-tuple-element.78), channel_id=1, source_target_pairs={{0,2},{2,0},{4,6},{6,4},{8,10},{10,8},{12,14},{14,12},{16,18},{18,... | collective-permute-start | bytes 1572872 | tf_op jit(solution)/shard_map/ppermute | solution.py:526
  388.2 68.5 %collective-permute-start.110 = (bf16[8,1,32,1024]{3,2,1,0:T(8,128)(2,1)}, bf16[8,1,32,1024]{3,2,1,0:T(8,128)(2,1)}, u32[]{:S(2)}, u32[]{:S(2)}) collective-permute-start(bf16[8,1,32,1024]{3,2,1,0:T(8,128)(2,1)} %get-tuple-element.94), channel_id=1, source_target_pairs={{0,4},{2,6},{4,0},{6,2},{8,12},{10,14},{12,8},{14,10},{16,20},{18,... | collective-permute-start | bytes 1572872 | tf_op jit(solution)/shard_map/ppermute | solution.py:526
  417.1 43.0 %collective-permute-start.106 = (bf16[8,1,32,1024]{3,2,1,0:T(8,128)(2,1)}, bf16[8,1,32,1024]{3,2,1,0:T(8,128)(2,1)}, u32[]{:S(2)}, u32[]{:S(2)}) collective-permute-start(bf16[8,1,32,1024]{3,2,1,0:T(8,128)(2,1)} %get-tuple-element.295), channel_id=1, source_target_pairs={{0,2},{2,0},{4,6},{6,4},{8,10},{10,8},{12,14},{14,12},{16,18},{18,... | collective-permute-start | bytes 1572872 | tf_op jit(solution)/shard_map/ppermute | solution.py:526
  453.6 26.2 %collective-permute-start.134 = (bf16[8,1,32,1024]{3,2,1,0:T(8,128)(2,1)}, bf16[8,1,32,1024]{3,2,1,0:T(8,128)(2,1)S(1)}, u32[]{:S(2)}, u32[]{:S(2)}) collective-permute-start(bf16[8,1,32,1024]{3,2,1,0:T(8,128)(2,1)} %get-tuple-element.309), channel_id=1, source_target_pairs={{0,4},{2,6},{4,0},{6,2},{8,12},{10,14},{12,8},{14,10},{16,20},{18,... | collective-permute-start | bytes 1572872 | tf_op jit(solution)/shard_map/ppermute | solution.py:526
  456.8 23.1 %collective-permute-start.98 = (bf16[8,1,32,1024]{3,2,1,0:T(8,128)(2,1)}, bf16[8,1,32,1024]{3,2,1,0:T(8,128)(2,1)S(1)}, u32[]{:S(2)}, u32[]{:S(2)}) collective-permute-start(bf16[8,1,32,1024]{3,2,1,0:T(8,128)(2,1)} %get-tuple-element.315), channel_id=1, source_target_pairs={{0,2},{2,0},{4,6},{6,4},{8,10},{10,8},{12,14},{14,12},{16,18},{18,... | collective-permute-start | bytes 1572872 | tf_op jit(solution)/shard_map/ppermute | solution.py:526
  460.1 30.9 %collective-permute-start.130 = (bf16[8,1,32,1024]{3,2,1,0:T(8,128)(2,1)}, bf16[8,1,32,1024]{3,2,1,0:T(8,128)(2,1)S(1)}, u32[]{:S(2)}, u32[]{:S(2)}) collective-permute-start(bf16[8,1,32,1024]{3,2,1,0:T(8,128)(2,1)} %get-tuple-element.319), channel_id=1, source_target_pairs={{0,4},{2,6},{4,0},{6,2},{8,12},{10,14},{12,8},{14,10},{16,20},{18,... | collective-permute-start | bytes 1572872 | tf_op jit(solution)/shard_map/ppermute | solution.py:526
  468.6 22.5 %collective-permute-start.94 = (bf16[8,1,32,1024]{3,2,1,0:T(8,128)(2,1)S(1)}, bf16[8,1,32,1024]{3,2,1,0:T(8,128)(2,1)S(1)}, u32[]{:S(2)}, u32[]{:S(2)}) collective-permute-start(bf16[8,1,32,1024]{3,2,1,0:T(8,128)(2,1)S(1)} %copy-done.82), channel_id=1, source_target_pairs={{0,2},{2,0},{4,6},{6,4},{8,10},{10,8},{12,14},{14,12},{16,18},{18,... | collective-permute-start | bytes 1572872 | tf_op jit(solution)/shard_map/ppermute | solution.py:526
  468.7 33.6 %collective-permute-start.126 = (bf16[8,1,32,1024]{3,2,1,0:T(8,128)(2,1)S(1)}, bf16[8,1,32,1024]{3,2,1,0:T(8,128)(2,1)S(1)}, u32[]{:S(2)}, u32[]{:S(2)}) collective-permute-start(bf16[8,1,32,1024]{3,2,1,0:T(8,128)(2,1)S(1)} %copy-done.80), channel_id=1, source_target_pairs={{0,4},{2,6},{4,0},{6,2},{8,12},{10,14},{12,8},{14,10},{16,20},{18,... | collective-permute-start | bytes 1572872 | tf_op jit(solution)/shard_map/ppermute | solution.py:526
  479.8 22.5 %collective-permute-start.90 = (bf16[8,1,32,1024]{3,2,1,0:T(8,128)(2,1)S(1)}, bf16[8,1,32,1024]{3,2,1,0:T(8,128)(2,1)S(1)}, u32[]{:S(2)}, u32[]{:S(2)}) collective-permute-start(bf16[8,1,32,1024]{3,2,1,0:T(8,128)(2,1)S(1)} %copy-done.78), channel_id=1, source_target_pairs={{0,2},{2,0},{4,6},{6,4},{8,10},{10,8},{12,14},{14,12},{16,18},{18,... | collective-permute-start | bytes 1572872 | tf_op jit(solution)/shard_map/ppermute | solution.py:526
  479.9 33.6 %collective-permute-start.122 = (bf16[8,1,32,1024]{3,2,1,0:T(8,128)(2,1)S(1)}, bf16[8,1,32,1024]{3,2,1,0:T(8,128)(2,1)S(1)}, u32[]{:S(2)}, u32[]{:S(2)}) collective-permute-start(bf16[8,1,32,1024]{3,2,1,0:T(8,128)(2,1)S(1)} %copy-done.77), channel_id=1, source_target_pairs={{0,4},{2,6},{4,0},{6,2},{8,12},{10,14},{12,8},{14,10},{16,20},{18,... | collective-permute-start | bytes 1572872 | tf_op jit(solution)/shard_map/ppermute | solution.py:526
  491.0 22.5 %collective-permute-start.86 = (bf16[8,1,32,1024]{3,2,1,0:T(8,128)(2,1)S(1)}, bf16[8,1,32,1024]{3,2,1,0:T(8,128)(2,1)S(1)}, u32[]{:S(2)}, u32[]{:S(2)}) collective-permute-start(bf16[8,1,32,1024]{3,2,1,0:T(8,128)(2,1)S(1)} %copy-done.76), channel_id=1, source_target_pairs={{0,2},{2,0},{4,6},{6,4},{8,10},{10,8},{12,14},{14,12},{16,18},{18,... | collective-permute-start | bytes 1572872 | tf_op jit(solution)/shard_map/ppermute | solution.py:526
  491.1 33.4 %collective-permute-start.118 = (bf16[8,1,32,1024]{3,2,1,0:T(8,128)(2,1)S(1)}, bf16[8,1,32,1024]{3,2,1,0:T(8,128)(2,1)S(1)}, u32[]{:S(2)}, u32[]{:S(2)}) collective-permute-start(bf16[8,1,32,1024]{3,2,1,0:T(8,128)(2,1)S(1)} %copy-done.75), channel_id=1, source_target_pairs={{0,4},{2,6},{4,0},{6,2},{8,12},{10,14},{12,8},{14,10},{16,20},{18,... | collective-permute-start | bytes 1572872 | tf_op jit(solution)/shard_map/ppermute | solution.py:526
  502.3 22.3 %collective-permute-start.82 = (bf16[8,1,32,1024]{3,2,1,0:T(8,128)(2,1)S(1)}, bf16[8,1,32,1024]{3,2,1,0:T(8,128)(2,1)S(1)}, u32[]{:S(2)}, u32[]{:S(2)}) collective-permute-start(bf16[8,1,32,1024]{3,2,1,0:T(8,128)(2,1)S(1)} %copy-done.74), channel_id=1, source_target_pairs={{0,2},{2,0},{4,6},{6,4},{8,10},{10,8},{12,14},{14,12},{16,18},{18,... | collective-permute-start | bytes 1572872 | tf_op jit(solution)/shard_map/ppermute | solution.py:526
  502.3 33.4 %collective-permute-start.114 = (bf16[8,1,32,1024]{3,2,1,0:T(8,128)(2,1)S(1)}, bf16[8,1,32,1024]{3,2,1,0:T(8,128)(2,1)S(1)}, u32[]{:S(2)}, u32[]{:S(2)}) collective-permute-start(bf16[8,1,32,1024]{3,2,1,0:T(8,128)(2,1)S(1)} %copy-done.73), channel_id=1, source_target_pairs={{0,4},{2,6},{4,0},{6,2},{8,12},{10,14},{12,8},{14,10},{16,20},{18,... | collective-permute-start | bytes 1572872 | tf_op jit(solution)/shard_map/ppermute | solution.py:526
  513.5 156.9 %collective-permute-start.70 = (bf16[8,208,1152]{2,1,0:T(8,128)(2,1)S(1)}, bf16[8,208,1152]{2,1,0:T(8,128)(2,1)S(1)}, u32[]{:S(2)}, u32[]{:S(2)}) collective-permute-start(bf16[8,208,1152]{2,1,0:T(8,128)(2,1)S(1)} %copy-done.2), channel_id=1, source_target_pairs={{0,1},{1,0},{2,3},{3,2},{4,5},{5,4},{6,7},{7,6},{8,9},{9,8},{10,11... | collective-permute-start | bytes 11501576 | tf_op jit(solution)/shard_map/ppermute | solution.py:593
  513.6 27.8 %collective-permute-start.79 = (bf16[4,1,32,1024]{3,2,1,0:T(8,128)(2,1)S(1)}, bf16[4,1,32,1024]{3,2,1,0:T(8,128)(2,1)S(1)}, u32[]{:S(2)}, u32[]{:S(2)}) collective-permute-start(bf16[4,1,32,1024]{3,2,1,0:T(8,128)(2,1)S(1)} %get-tuple-element.184), channel_id=1, source_target_pairs={{0,4},{2,6},{4,0},{6,2},{8,12},{10,14},{12,8},{14,10},{16,20},{18,... | collective-permute-start | bytes 786440 | tf_op jit(solution)/shard_map/ppermute | solution.py:526
  524.5 22.4 %collective-permute-start.107 = (bf16[4,1,32,1024]{3,2,1,0:T(8,128)(2,1)S(1)}, bf16[4,1,32,1024]{3,2,1,0:T(8,128)(2,1)S(1)}, u32[]{:S(2)}, u32[]{:S(2)}) collective-permute-start(bf16[4,1,32,1024]{3,2,1,0:T(8,128)(2,1)S(1)} %get-tuple-element.170), channel_id=1, source_target_pairs={{0,4},{2,6},{4,0},{6,2},{8,12},{10,14},{12,8},{14,10},{16,20},{18,... | collective-permute-start | bytes 786440 | tf_op jit(solution)/shard_map/ppermute | solution.py:526
  563.1 26.2 %collective-permute-start.119 = (bf16[4,1,32,1024]{3,2,1,0:T(8,128)(2,1)S(1)}, bf16[4,1,32,1024]{3,2,1,0:T(8,128)(2,1)S(1)}, u32[]{:S(2)}, u32[]{:S(2)}) collective-permute-start(bf16[4,1,32,1024]{3,2,1,0:T(8,128)(2,1)S(1)} %get-tuple-element.164), channel_id=1, source_target_pairs={{0,2},{2,0},{4,6},{6,4},{8,10},{10,8},{12,14},{14,12},{16,18},{18,... | collective-permute-start | bytes 786440 | tf_op jit(solution)/shard_map/ppermute | solution.py:526
  565.6 24.1 %collective-permute-start.83 = (bf16[4,1,32,1024]{3,2,1,0:T(8,128)(2,1)S(1)}, bf16[4,1,32,1024]{3,2,1,0:T(8,128)(2,1)S(1)}, u32[]{:S(2)}, u32[]{:S(2)}) collective-permute-start(bf16[4,1,32,1024]{3,2,1,0:T(8,128)(2,1)S(1)} %get-tuple-element.182), channel_id=1, source_target_pairs={{0,4},{2,6},{4,0},{6,2},{8,12},{10,14},{12,8},{14,10},{16,20},{18,... | collective-permute-start | bytes 786440 | tf_op jit(solution)/shard_map/ppermute | solution.py:526
  565.9 26.2 %collective-permute-start.115 = (bf16[4,1,32,1024]{3,2,1,0:T(8,128)(2,1)S(1)}, bf16[4,1,32,1024]{3,2,1,0:T(8,128)(2,1)S(1)}, u32[]{:S(2)}, u32[]{:S(2)}) collective-permute-start(bf16[4,1,32,1024]{3,2,1,0:T(8,128)(2,1)S(1)} %get-tuple-element.166), channel_id=1, source_target_pairs={{0,2},{2,0},{4,6},{6,4},{8,10},{10,8},{12,14},{14,12},{16,18},{18,... | collective-permute-start | bytes 786440 | tf_op jit(solution)/shard_map/ppermute | solution.py:526
  569.1 24.5 %collective-permute-start.80 = (bf16[2,1,32,1024]{3,2,1,0:T(8,128)(2,1)S(1)}, bf16[2,1,32,1024]{3,2,1,0:T(8,128)(2,1)S(1)}, u32[]{:S(2)}, u32[]{:S(2)}) collective-permute-start(bf16[2,1,32,1024]{3,2,1,0:T(8,128)(2,1)S(1)} %get-tuple-element.218), channel_id=1, source_target_pairs={{0,8},{2,10},{4,12},{6,14},{8,0},{10,2},{12,4},{14,6},{16,24},{18,... | collective-permute-start | bytes 393224 | tf_op jit(solution)/shard_map/ppermute | solution.py:526
  628.9 41.3 %collective-permute-start.109 = (bf16[1,1,32,1024]{3,2,1,0:T(8,128)(2,1)S(1)}, bf16[1,1,32,1024]{3,2,1,0:T(8,128)(2,1)S(1)}, u32[]{:S(2)}, u32[]{:S(2)}) collective-permute-start(bf16[1,1,32,1024]{3,2,1,0:T(8,128)(2,1)S(1)} %slice_add_fusion.86), channel_id=1, source_target_pairs={{0,16},{2,18},{4,20},{6,22},{8,24},{10,26},{12,28},{14,30},{16,0},... | collective-permute-start | bytes 196616 | tf_op jit(solution)/shard_map/ppermute | solution.py:526
  630.3 97.5 %collective-permute-start.141 = (bf16[1,1,32,1024]{3,2,1,0:T(8,128)(2,1)S(1)}, bf16[1,1,32,1024]{3,2,1,0:T(8,128)(2,1)S(1)}, u32[]{:S(2)}, u32[]{:S(2)}) collective-permute-start(bf16[1,1,32,1024]{3,2,1,0:T(8,128)(2,1)S(1)} %slice_add_fusion.70), channel_id=1, source_target_pairs={{0,16},{2,18},{4,20},{6,22},{8,24},{10,26},{12,28},{14,30},{16,0},... | collective-permute-start | bytes 196616 | tf_op jit(solution)/shard_map/ppermute | solution.py:526
  635.4 31.8 %collective-permute-start.105 = (bf16[1,1,32,1024]{3,2,1,0:T(8,128)(2,1)S(1)}, bf16[1,1,32,1024]{3,2,1,0:T(8,128)(2,1)S(1)}, u32[]{:S(2)}, u32[]{:S(2)}) collective-permute-start(bf16[1,1,32,1024]{3,2,1,0:T(8,128)(2,1)S(1)} %slice_add_fusion.88), channel_id=1, source_target_pairs={{0,16},{2,18},{4,20},{6,22},{8,24},{10,26},{12,28},{14,30},{16,0},... | collective-permute-start | bytes 196616 | tf_op jit(solution)/shard_map/ppermute | solution.py:526
  667.2 59.5 %collective-permute-start.137 = (bf16[1,1,32,1024]{3,2,1,0:T(8,128)(2,1)S(1)}, bf16[1,1,32,1024]{3,2,1,0:T(8,128)(2,1)S(1)}, u32[]{:S(2)}, u32[]{:S(2)}) collective-permute-start(bf16[1,1,32,1024]{3,2,1,0:T(8,128)(2,1)S(1)} %slice_add_fusion.72), channel_id=1, source_target_pairs={{0,16},{2,18},{4,20},{6,22},{8,24},{10,26},{12,28},{14,30},{16,0},... | collective-permute-start | bytes 196616 | tf_op jit(solution)/shard_map/ppermute | solution.py:526
  667.2 54.0 %collective-permute-start.129 = (bf16[1,1,32,1024]{3,2,1,0:T(8,128)(2,1)S(1)}, bf16[1,1,32,1024]{3,2,1,0:T(8,128)(2,1)S(1)}, u32[]{:S(2)}, u32[]{:S(2)}) collective-permute-start(bf16[1,1,32,1024]{3,2,1,0:T(8,128)(2,1)S(1)} %slice_add_fusion.76), channel_id=1, source_target_pairs={{0,16},{2,18},{4,20},{6,22},{8,24},{10,26},{12,28},{14,30},{16,0},... | collective-permute-start | bytes 196616 | tf_op jit(solution)/shard_map/ppermute | solution.py:526
  670.2 45.4 %collective-permute-start.121 = (bf16[1,1,32,1024]{3,2,1,0:T(8,128)(2,1)S(1)}, bf16[1,1,32,1024]{3,2,1,0:T(8,128)(2,1)S(1)}, u32[]{:S(2)}, u32[]{:S(2)}) collective-permute-start(bf16[1,1,32,1024]{3,2,1,0:T(8,128)(2,1)S(1)} %slice_add_fusion.80), channel_id=1, source_target_pairs={{0,16},{2,18},{4,20},{6,22},{8,24},{10,26},{12,28},{14,30},{16,0},... | collective-permute-start | bytes 196616 | tf_op jit(solution)/shard_map/ppermute | solution.py:526
  670.4 45.2 %collective-permute-start.117 = (bf16[1,1,32,1024]{3,2,1,0:T(8,128)(2,1)S(1)}, bf16[1,1,32,1024]{3,2,1,0:T(8,128)(2,1)S(1)}, u32[]{:S(2)}, u32[]{:S(2)}) collective-permute-start(bf16[1,1,32,1024]{3,2,1,0:T(8,128)(2,1)S(1)} %slice_add_fusion.82), channel_id=1, source_target_pairs={{0,16},{2,18},{4,20},{6,22},{8,24},{10,26},{12,28},{14,30},{16,0},... | collective-permute-start | bytes 196616 | tf_op jit(solution)/shard_map/ppermute | solution.py:526
  766.4 26.5 %collective-permute-start.77 = (bf16[1,32,1152]{2,1,0:T(8,128)(2,1)S(1)}, bf16[1,32,1152]{2,1,0:T(8,128)(2,1)}, u32[]{:S(2)}, u32[]{:S(2)}) collective-permute-start(bf16[1,32,1152]{2,1,0:T(8,128)(2,1)S(1)} %slice_add_fusion.68), channel_id=1, source_target_pairs={{0,16},{2,18},{4,20},{6,22},{8,24},{10,26},{12,28},{14,30},{16,0},... | collective-permute-start | bytes 221192 | tf_op jit(solution)/shard_map/ppermute | solution.py:526
  (177 other events, 4475.4 us)

commit v2 on v1

v2 whole, which is shorter than its diff:
```python
import functools

import jax
import jax.numpy as jnp
from jax import lax
from jax.experimental import pallas as pl
from jax.experimental.pallas import tpu as pltpu
from jax.sharding import PartitionSpec as P

F32 = jnp.float32
BF16 = jnp.bfloat16
HD = 64
SEQ = 197
ROWS = 208
SLOTS = 1280
SPAN = 1536
SCALE = 100
FEW = 16
MOST = 640
TILE = 256
TILES = 40
EXPERTS = 8
LANES = 128
CALLS = ((0, 4), (4, 2), (6, 2))
GROUPS = ((0,), (1, 2))
FAR = (0, 8, 4, 12)
VMEM = 58 * 1024 * 1024

LIVE, START, TOTAL, TABLE = 8, 32, 160, 256
OWNER, PART, FIRST, RING = 256, 296, 336, 344
AROUND = (0, 4, 8, 12, 14, 10, 6, 2)
FIRST_FAR, THEN_FAR = (4, 3, -3), (2, -2, 1, -1, 0)


def nt(a, b):
    return lax.dot_general(a, b, (((1,), (1,)), ((), ())), preferred_element_type=F32)


def tn(a, b):
    return lax.dot_general(a, b, (((0,), (0,)), ((), ())), preferred_element_type=F32)


def mm(a, b):
    return jnp.dot(a, b, preferred_element_type=F32)


def iota(shape, dim):
    return lax.broadcasted_iota(jnp.int32, shape, dim)


def layer_stats(values):
    centre = values - jnp.mean(values, -1, keepdims=True)
    factor = lax.rsqrt(jnp.mean(centre * centre, -1, keepdims=True) + 1e-06)
    return centre * factor, factor


def norm_back(grad, normed, factor):
    return factor * (
        grad - jnp.mean(grad, -1, keepdims=True) - normed * jnp.mean(grad * normed, -1, keepdims=True)
    )


def gelu_both(u):
    t = 1.0 / (1.0 + (0.3275911 * 0.7071067811865476) * jnp.abs(u))
    bell = jnp.exp(u * (u * -0.5))
    poly = t * (
        0.127414796 + t * (-0.142248368 + t * (0.7107068705 + t * (-0.7265760135 + t * 0.5307027145)))
    )
    tail = poly * bell
    phi = jnp.where(u >= 0.0, 1.0 - tail, tail)
    return u * phi, phi + u * bell * 0.3989422804014327


def split_low(values):
    high = values.astype(BF16).astype(F32)
    return high, values - high


def load_weights(info, parts, weights, sems, rel, rows):
    c, me = info[0], info[1]
    copies = []
    for side, part in enumerate(parts):
        t = c ^ side
        for k, r in enumerate(rel):
            where = pl.multiple_of((me ^ r) * rows, 16)
            copies.append(
                pltpu.make_async_copy(part.at[k], weights.at[t, pl.ds(where, rows), :], sems.at[side, k])
            )
    for copy in copies:
        copy.start()
    for copy in copies:
        copy.wait()


def head_mask(which):
    lane = iota((ROWS, LANES), 1)
    return (lane < HD) if which == 0 else (lane >= HD)


def forward_kernel(rel, rows, info, tok, mask, *refs):
    i = pl.program_id(0)
    w_parts, refs = refs[:-10], refs[-10:]
    src, mid, proj, att, lse, gates, weights, gains, xs, sems = refs
    shares, _, cols = weights.shape
    local = (cols - LANES) // 4
    aux_at = 4 * local

    @pl.when(i == 0)
    def _():
        load_weights(info, w_parts, weights, sems, rel, rows)
        gains[...] = weights[0, :, aux_at:].astype(F32).T[0:16, :]

    @pl.when(info[LIVE + i] == 1)
    def _():
        xs[192:ROWS, :] = jnp.zeros((ROWS - 192, 512), F32)
        xs[0:SEQ, :] = tok[0, 0].astype(F32)
        x = xs[...]
        normed, _ = layer_stats(x)
        act = (normed * gains[8:9, :]).astype(BF16)
        for t in range(shares):
            proj[0, :, t * 3 * local : (t + 1) * 3 * local] = mm(act, weights[t, :, 0 : 3 * local]).astype(BF16)
        key_ok = iota((ROWS, ROWS), 1) < SEQ
        lane = iota((ROWS, LANES), 1)
        saved = jnp.zeros((ROWS, LANES), F32)
        for t in range(shares):
            for p in range(local // LANES):
                at = t * 3 * local + p * LANES
                q = proj[0, :, at : at + LANES]
                k = proj[0, :, at + local : at + local + LANES]
                v = proj[0, :, at + 2 * local : at + 2 * local + LANES]
                halves = []
                for h in range(2):
                    qm = jnp.where(head_mask(h), q.astype(F32), 0.0).astype(BF16)
                    s = jnp.where(key_ok, nt(qm, k) * (HD**-0.5), -1e30)
                    top = jnp.max(s, -1, keepdims=True)
                    e = jnp.exp(s - top)
                    total = jnp.sum(e, -1, keepdims=True)
                    probs = (e * (1.0 / total)).astype(BF16)
                    halves.append(mm(probs, v))
                    saved = jnp.where(lane == (t * local + p * LANES) // HD + h, top + jnp.log(total), saved)
                att[0, :, t * local + p * LANES : t * local + (p + 1) * LANES] = jnp.where(
                    lane < HD, halves[0], halves[1]
                ).astype(BF16)
        lse[0] = saved
        branch = nt(att[0, :, 0:local], weights[0, :, 3 * local : aux_at])
        for t in range(1, shares):
            branch = branch + nt(att[0, :, t * local : (t + 1) * local], weights[t, :, 3 * local : aux_at])
        middle = x + branch
        mid[0] = middle
        normed2, _ = layer_stats(middle)
        act2 = (normed2 * gains[9:10, :]).astype(BF16)
        src[0, :, 0:512] = act2
        chosen = mask[0, 0].astype(F32)
        logits = jnp.where(chosen > 0.0, mm(act2, weights[0, :, aux_at:]), -1e30)
        top = jnp.max(logits, -1, keepdims=True)
        e = jnp.exp(logits - top) * chosen
        gate = e / jnp.maximum(jnp.sum(e, -1, keepdims=True), 0.5)
        gates[0] = gate
        high, low = split_low(gate)
        src[0, :, 512:640] = (high + pltpu.roll(low, 8, 1)).astype(BF16)


def blocks_of(info, i, e):
    begin, end = info[START + i * 8 + e], info[START + i * 8 + 8 + e]
    first = begin // FEW
    return first, jnp.where(end > begin, (end + FEW - 1) // FEW - first, 0)


def places(info, i, mask):
    chosen = mask[0, 0]
    lower = (iota((ROWS, ROWS), 0) > iota((ROWS, ROWS), 1)).astype(F32).astype(BF16)
    lane = iota((1, LANES), 1)
    shift = jnp.zeros((1, LANES), F32)
    base = 0
    for e in range(EXPERTS):
        _, count = blocks_of(info, i, e)
        shift = jnp.where(lane == e, (base * FEW + info[START + i * 8 + e] % FEW).astype(F32), shift)
        base = base + count
    return jnp.where(chosen.astype(F32) > 0.0, mm(lower, chosen) + shift, -1.0)


def dispatch_kernel(with_act, count, info, *refs):
    i = pl.program_id(0)
    if with_act:
        own, oth, mask, x_hbm, xbuf, tbuf, pbuf, res, sems = refs
    else:
        gy, mask, x_hbm, xbuf, tbuf, pbuf, res, sems = refs
    cols = res.shape[1]

    @pl.when(i == 0)
    def _():
        tbuf[...] = jnp.zeros(tbuf.shape, BF16)
        pbuf[...] = jnp.full(pbuf.shape, -1.0, F32)

    @pl.when(info[LIVE + i] == 1)
    def _():
        if with_act:

            @pl.when(i < count)
            def _():
                tbuf[0:ROWS, :] = own[0]

            @pl.when(i >= count)
            def _():
                tbuf[0:ROWS, :] = oth[0]
        else:
            tbuf[0:SEQ, :] = gy[0, 0]
        pbuf[0:ROWS, :] = places(info, i, mask)
        place = pbuf[...].T[0:EXPERTS, :]
        high = jnp.max(place, 0, keepdims=True)
        low = jnp.min(jnp.where(place < 0.0, 4096.0, place), 0, keepdims=True)
        row = iota((MOST, TILE), 0).astype(F32)
        pick = jnp.where((row == high) | (row == low), 1.0, 0.0).astype(BF16)
        res[...] = mm(pick, tbuf[...]).astype(BF16)
        base = 0
        for e in range(EXPERTS):
            first, blocks = blocks_of(info, i, e)
            off = info[START + i * 8 + e] % FEW

            @pl.when(blocks > 0)
            def _():
                to = pl.ds(pl.multiple_of(first * FEW, FEW), FEW)
                new = res[pl.ds(pl.multiple_of(base * FEW, FEW), FEW), :].astype(F32)
                old = xbuf[e, to, :].astype(F32)
                xbuf[e, to, :] = jnp.where(iota((FEW, cols), 0) < off, old, new).astype(BF16)

            def move(k, carry):
                to = pl.ds(pl.multiple_of((first + k) * FEW, FEW), FEW)
                xbuf[e, to, :] = res[pl.ds(pl.multiple_of((base + k) * FEW, FEW), FEW), :]
                return carry

            lax.fori_loop(1, blocks, move, 0)
            base = base + blocks

    @pl.when(i == 15)
    def _():
        for e in range(EXPERTS):
            end = pl.multiple_of((info[TOTAL + e] + FEW - 1) // FEW * FEW, FEW)
            xbuf[e, pl.ds(end, TILE), :] = jnp.zeros((TILE, cols), BF16)
        for start in (True, False):
            for e in range(EXPERTS):
                for k in range(SLOTS // TILE):

                    @pl.when(k * TILE < jnp.maximum(info[TOTAL + e], 1))
                    def _():
                        rows = pl.ds(k * TILE, TILE)
                        copy = pltpu.make_async_copy(xbuf.at[e, rows, :], x_hbm.at[e, rows, :], sems.at[e, k])
                        if start:
                            copy.start()
                        else:
                            copy.wait()


def expert_kernel(number, plan, fast, rows, n_pieces, info, xa, xg, *refs):
    pieces, refs = refs[:n_pieces], refs[n_pieces:]
    w_in, w_out, acc_in, acc_out, sems = refs[-5:]
    y, grads = refs[0], refs[1:-5]
    i = pl.program_id(0)
    n = info[FIRST + number + 1] - info[FIRST + number]
    at = info[FIRST + number] + jnp.minimum(i, n - 1)
    expert = info[OWNER + at]
    slot = expert % 2

    def owned_by(far, flip):
        return pl.multiple_of((info[RING + far % 8] ^ flip) * rows, 16)

    def copies(ex, to, start):
        for side, (entries, buf) in enumerate(zip(plan, (w_in, w_out))):
            for k, (owner, sources) in enumerate(entries):
                where = owned_by(*owner) if isinstance(owner, tuple) else owner * rows
                for ref, b, low, high in sources:
                    copy = pltpu.make_async_copy(
                        pieces[ref].at[b, ex - low], buf.at[to, pl.ds(where, rows), :], sems.at[to, side, k]
                    )

                    @pl.when((ex >= low) & (ex < high))
                    def _():
                        if start:
                            copy.start()
                        else:
                            copy.wait()

    @pl.when(i == 0)
    def _():
        copies(expert, slot, True)

    @pl.when((info[PART + at] == 0) & (i < n))
    def _():
        copies(expert, slot, False)

        @pl.when(expert + 1 < sum(CALLS[number]))
        def _():
            copies(expert + 1, 1 - slot, True)

    @pl.when(i < n)
    def _():
        rows_x = xa[0, :, 0:512]
        g = xg[0].astype(F32)
        lane = iota((TILE, LANES), 1)
        mine = (lane == expert) | (lane == expert + 8)
        gate = jnp.sum(jnp.where(mine, xa[0, :, 512:640].astype(F32), 0.0), -1, keepdims=True)
        inner = mm(rows_x, w_in[slot])
        act, slope = gelu_both(inner)
        hid = act.astype(BF16)
        out = nt(hid, w_out[slot])
        deo = (gate * g).astype(BF16)
        dinner = (mm(deo, w_out[slot]) * slope).astype(BF16)
        dgate = jnp.sum(g * out, -1, keepdims=True)
        high, low = split_low(dgate)
        y[0, :, 0:512] = (gate * out).astype(BF16)
        y[0, :, 512:1024] = nt(dinner, w_in[slot]).astype(BF16)
        y[0, :, 1024:1152] = jnp.where(lane == expert, high, jnp.where(lane == expert + 8, low, 0.0)).astype(BF16)

        @pl.when(info[PART + at] == 0)
        def _():
            acc_in[...] = tn(rows_x, dinner)
            acc_out[...] = tn(deo, hid)

        @pl.when(info[PART + at] > 0)
        def _():
            acc_in[...] += tn(rows_x, dinner)
            acc_out[...] += tn(deo, hid)

    @pl.when((i == n - 1) | ((i < n) & (info[PART + at + 1] == 0)))
    def _():
        if fast:
            sent, turned = grads[:8], grads[8:]
            for k, far in enumerate(FIRST_FAR + THEN_FAR):
                here, there = pl.ds(owned_by(far, 0), rows), pl.ds(owned_by(far, 1), rows)
                sent[k][0, 0] = acc_in[here, :].astype(BF16)
                sent[k][1, 0] = acc_out[here, :].astype(BF16)
                sent[k][2, 0] = acc_out[there, :].astype(BF16)
                to, place = (0, k) if k < len(FIRST_FAR) else (1, k - len(FIRST_FAR))
                turned[to][place, 0] = acc_in[there, :].astype(BF16)
        else:
            grads[0][0] = acc_in[...].astype(BF16)
            grads[1][0] = acc_out[...].astype(BF16)


def at_call(expert):
    return [(k, expert - first) for k, (first, count) in enumerate(CALLS) if first <= expert < first + count][0]


def add_kernel(step, counts, *refs):
    e = pl.program_id(0)
    calls, total = len(counts), sum(counts)
    ways = 1 if step in (0, 3) else 2
    half = total // 2

    def pick(parts):
        value = parts[0][...].astype(F32)
        for k in range(1, calls):
            value = jnp.where(e < sum(counts[:k]), value, parts[k][...].astype(F32))
        return value

    sums = []
    for _ in range(ways):
        q, x, refs = pick(refs[:calls]), pick(refs[calls : 2 * calls]), refs[2 * calls :]
        sums.append((q[0:1] + x, q[1:3]))
    if step == 0:
        for out, here in zip(refs, (e < half, e >= half)):

            @pl.when(here)
            def _():
                out[0:1] = sums[0][0].astype(BF16)
                out[1:3] = sums[0][1].astype(BF16)
    elif step == 3:
        up, down, first, second, third = refs
        first[...] = (sums[0][0] + up[0:1].astype(F32) + down[0:1].astype(F32))[0]
        rest = sums[0][1] + up[1:3].astype(F32) + down[1:3].astype(F32)
        second[...] = rest[0]
        third[...] = rest[1].astype(BF16)
    else:
        for k in range(2):
            arrived, out = refs[k][...].astype(F32), refs[2 + k]
            if step == 1:
                arrived = jnp.where((e < half) if k == 0 else (e >= half), arrived, 0.0)
            out[0:1] = (sums[k][0] + arrived[0:1]).astype(BF16)
            out[1:3] = (sums[k][1] + arrived[1:3]).astype(BF16)


def combine_kernel(base, info, *refs):
    y_parts, (mask, out, ybuf, sems) = refs[:-4], refs[-4:]
    i = pl.program_id(0)
    slot = i % 2

    def fetch(j, buf, start):
        @pl.when(info[LIVE + base + j] == 1)
        def _():
            at = 0
            for e in range(EXPERTS):
                first, blocks = blocks_of(info, base + j, e)

                def move(k, carry, e=e, first=first, at=at):
                    copy = pltpu.make_async_copy(
                        y_parts[at_call(e)[0]].at[at_call(e)[1], pl.ds(pl.multiple_of((first + k) * FEW, FEW), FEW), :],
                        ybuf.at[buf, pl.ds(pl.multiple_of((at + k) * FEW, FEW), FEW), :],
                        sems.at[buf],
                    )
                    if start:
                        copy.start()
                    else:
                        copy.wait()
                    return carry

                lax.fori_loop(0, blocks, move, 0)
                at = at + blocks

    @pl.when(i == 0)
    def _():
        ybuf[...] = jnp.zeros(ybuf.shape, BF16)
        fetch(i, slot, True)

    @pl.when(i + 1 < pl.num_programs(0))
    def _():
        fetch(i + 1, 1 - slot, True)

    fetch(i, slot, False)

    @pl.when(info[LIVE + base + i] == 1)
    def _():
        place = places(info, base + i, mask)
        high = jnp.max(place, -1, keepdims=True)
        low = jnp.min(jnp.where(place < 0.0, 4096.0, place), -1, keepdims=True)
        lane = iota((ROWS, MOST), 1).astype(F32)
        pick = jnp.where((lane == high) | (lane == low), 1.0, 0.0).astype(BF16)
        if out.dtype == F32:
            out[0] = mm(pick, ybuf[slot])
        else:
            out[0, :, 0:1024] = mm(pick, ybuf[slot, :, 0:1024]).astype(BF16)
            aux = mm(pick, ybuf[slot, :, 1024:1152])
            both = jnp.where(iota((ROWS, LANES), 1) < 8, aux + pltpu.roll(aux, LANES - 8, 1), 0.0)
            high, low = split_low(both)
            out[0, :, 1024:1152] = (high + pltpu.roll(low, 8, 1)).astype(BF16)


def assemble_kernel(shares, info, *refs):
    parts, (out, scratch) = refs[:-2], refs[-2:]
    c = info[0]
    for micro in range(2):

        @pl.when(pl.program_id(0) == micro)
        def _():
            for side in range(shares):
                some = [(a, j) for a in parts[3 * side : 3 * side + 3] for j in range(a.shape[0])]
                here = some[: len(some) // 2] if micro == 0 else some[len(some) // 2 :]
                for slot, (part, j) in enumerate(here):
                    for k in range(4):
                        values = part[j, 0:SEQ, k * LANES : (k + 1) * LANES].astype(F32)
                        scratch[k, pl.ds(shares * slot + (c ^ side), SEQ, stride=8), :] = values

    for k in range(4):
        out[0, :, :, k * LANES : (k + 1) * LANES] = scratch[k].reshape(SEQ, 8, LANES).astype(BF16)


def backward_kernel(
    base,
    rel,
    order,
    rows,
    info,
    tok,
    gy_ref,
    comb_own,
    comb_oth,
    mid,
    proj,
    att,
    lse,
    gates,
    *refs,
):
    i = pl.program_id(0)
    c, me = info[0], info[1]
    scratch, refs = refs[-11:], refs[:-11]
    weights, gains, twice, xs, gs, dproj, acc_qkv, acc_out, acc_router, acc_gain, sems = scratch
    shares, _, cols = weights.shape
    w_parts, refs = refs[:shares], refs[shares:]
    block_out, grad_tok = refs[:2]
    grads = refs[2:]
    local = (cols - LANES) // 4
    aux_at = 4 * local

    @pl.when(i == 0)
    def _():
        load_weights(info, w_parts, weights, sems, rel, rows)
        aux = weights[0, :, aux_at:].astype(F32)
        gains[...] = aux.T[0:16, :]
        lane = iota((512, LANES), 1)
        router = jnp.where(lane < 8, aux, 0.0)
        twice[...] = (router + pltpu.roll(router, 8, 1)).astype(BF16)
        acc_qkv[...] = jnp.zeros(acc_qkv.shape, F32)
        acc_out[...] = jnp.zeros(acc_out.shape, F32)
        acc_router[...] = jnp.zeros(acc_router.shape, F32)
        acc_gain[...] = jnp.zeros(acc_gain.shape, F32)

    @pl.when(info[LIVE + base + i] == 0)
    def _():
        block_out[...] = jnp.zeros(block_out.shape, BF16)
        grad_tok[...] = jnp.zeros(grad_tok.shape, BF16)

    @pl.when(info[LIVE + base + i] == 1)
    def _():
        xs[192:ROWS, :] = jnp.zeros((ROWS - 192, 512), F32)
        xs[0:SEQ, :] = tok[0, 0].astype(F32)
        gs[192:ROWS, :] = jnp.zeros((ROWS - 192, 512), F32)
        gs[0:SEQ, :] = gy_ref[0, 0].astype(F32)
        gy = gs[...]
        lane = iota((ROWS, LANES), 1)
        middle = mid[0]
        mixed = comb_own[0, :, 0:512] + comb_oth[0, :, 0:512].astype(F32)
        block_out[0] = (middle + mixed).astype(BF16)
        normed2, factor2 = layer_stats(middle)
        act2 = (normed2 * gains[9:10, :]).astype(BF16)
        gate = gates[0]
        aux = comb_own[0, :, 1024:1152] + comb_oth[0, :, 1024:1152].astype(F32)
        dgate = jnp.where(lane < 8, aux + pltpu.roll(aux, LANES - 8, 1), 0.0)
        dlogits = gate * (dgate - jnp.sum(gate * dgate, -1, keepdims=True))
        high, low = split_low(dlogits)
        packed = (high + pltpu.roll(low, 8, 1)).astype(BF16)
        acc_router[...] += tn(act2, packed)
        dact2 = (
            comb_own[0, :, 512:1024] + comb_oth[0, :, 512:1024].astype(F32) + nt(packed, twice[...])
        )
        acc_gain[9:10, :] += jnp.sum(dact2 * normed2, 0, keepdims=True)
        dmiddle = gy + norm_back(dact2 * gains[9:10, :], normed2, factor2)
        gs[...] = dmiddle
        dbranch = dmiddle.astype(BF16)
        x = xs[...]
        normed1, factor1 = layer_stats(x)
        act1 = (normed1 * gains[8:9, :]).astype(BF16)
        key_ok = iota((ROWS, ROWS), 1) < SEQ
        for t in range(shares):
            acc_out[t] += tn(dbranch, att[0, :, t * local : (t + 1) * local])
            datt_t = mm(dbranch, weights[t, :, 3 * local : aux_at]).astype(BF16)
            for p in range(local // LANES):
                at = t * 3 * local + p * LANES
                q = proj[0, :, at : at + LANES]
                k = proj[0, :, at + local : at + local + LANES]
                v = proj[0, :, at + 2 * local : at + 2 * local + LANES]
                datt = datt_t[:, p * LANES : (p + 1) * LANES]
                parts = []
                for h in range(2):
                    qm = jnp.where(head_mask(h), q.astype(F32), 0.0).astype(BF16)
                    dm = jnp.where(head_mask(h), datt.astype(F32), 0.0).astype(BF16)
                    head = (t * local + p * LANES) // HD + h
                    s = nt(qm, k) * (HD**-0.5) - lse[0, :, head : head + 1]
                    probs = jnp.where(key_ok, jnp.exp(jnp.where(key_ok, s, 0.0)), 0.0)
                    dprobs = nt(dm, v)
                    ds = (probs * (dprobs - jnp.sum(dprobs * probs, -1, keepdims=True))).astype(BF16)
                    parts.append((mm(ds, k), tn(ds, q), tn(probs.astype(BF16), datt)))
                for j in range(3):
                    both = jnp.where(lane < HD, parts[0][j], parts[1][j])
                    if j < 2:
                        both = both * (HD**-0.5)
                    dproj[:, at + j * local : at + j * local + LANES] = both.astype(BF16)
        dact1 = jnp.zeros((ROWS, 512), F32)
        for t in range(shares):
            dp = dproj[:, t * 3 * local : (t + 1) * 3 * local]
            acc_qkv[t] += tn(act1, dp)
            dact1 = dact1 + nt(dp, weights[t, :, 0 : 3 * local])
        acc_gain[8:9, :] += jnp.sum(dact1 * normed1, 0, keepdims=True)
        total = gs[...] + norm_back(dact1 * gains[8:9, :], normed1, factor1)
        grad_tok[0] = total.astype(BF16)

    @pl.when(i == pl.num_programs(0) - 1)
    def _():
        lane = iota((512, LANES), 1)
        router = acc_router[...]
        aux = jnp.where(lane < 8, router + pltpu.roll(router, LANES - 8, 1), acc_gain[...].T)
        acc_router[...] = aux
        for k, r in enumerate(order):
            where = pl.ds(pl.multiple_of((me ^ r) * rows, 16), rows)
            for side, out in enumerate(grads):
                out[k, :, 0 : 3 * local] = acc_qkv[c ^ side, where, :].astype(BF16)
                out[k, :, 3 * local : aux_at] = acc_out[c ^ side, where, :].astype(BF16)
                out[k, :, aux_at:] = acc_router[where, :].astype(BF16)


def swap(n, bit):
    return [(i, i ^ bit) for i in range(n)]


def hop(a, n, bits):
    return lax.ppermute(a, "dp", swap(n, bits))


def plus(*parts):
    return sum(a.astype(F32) for a in parts).astype(BF16)


def order(token, *lists):
    out = list(lax.optimization_barrier((token, *[a for arrays in lists for a in arrays])))
    got, out = [out[0]], out[1:]
    for arrays in lists:
        got.append(out[: len(arrays)])
        out = out[len(arrays) :]
    return got


def in_turn(kernel, operands):
    def run(info, earlier, *refs):
        ran, refs = refs[operands], refs[:operands] + refs[operands + 1 :]

        @pl.when(pl.program_id(0) == 0)
        def _():
            ran[...] = jnp.zeros(ran.shape, F32)

        kernel(info, *refs)

    return run


def cost(microseconds):
    return pl.CostEstimate(flops=int(microseconds * SCALE), bytes_accessed=1000, transcendentals=0)


def call(kernel, grid, token, args, in_specs, out_specs, out_shape, scratch, name, microseconds):
    token, info = token
    got = pl.pallas_call(
        in_turn(kernel, len(args)),
        grid_spec=pltpu.PrefetchScalarGridSpec(
            num_scalar_prefetch=1,
            grid=grid,
            in_specs=[any_spec()] + in_specs,
            out_specs=[pl.BlockSpec((8, LANES), lambda i, s: (0, 0))] + out_specs,
            scratch_shapes=scratch,
        ),
        out_shape=[shape((8, LANES), F32)] + out_shape,
        compiler_params=params(),
        cost_estimate=cost(microseconds),
        name=name,
    )(info, token, *args)
    return (got[0], info), got[1:]


def ring(a, n, way):
    pairs = []
    for at, here in enumerate(AROUND):
        there = AROUND[(at + way) % len(AROUND)]
        pairs += [(here, there), (here ^ 1, there ^ 1)]
    return lax.ppermute(a, "dp", pairs)


def shifted(r):
    return tuple(z ^ r for z in FAR)


def gather_line(shard, n, others):
    near = shard[None]
    near = jnp.concatenate([near, hop(near, n, 8)], 0)
    near = jnp.concatenate([near, hop(near, n, 4)], 0)
    return order(near, others)


def gather_square(near, n, others):
    by_x, by_y = hop(near, n, 1), hop(near, n, 2)
    by_x, (by_y, *others) = order(by_x, [by_y, *others])
    whole = jnp.concatenate([near, by_x, by_y, hop(by_y[:2], n, 1), hop(by_x[2:], n, 2)], 0)
    return whole, others, by_x


def scatter_far(far, n):
    half = plus(far[:2], hop(far[2:], n, 4))
    return (half[0].astype(F32) + hop(half[1:], n, 8)[0].astype(F32))


def scatter_small(whole, n):
    here, by_x, by_y, both = whole[0:4], whole[4:8], whole[8:12], whole[12:16]
    by_y = jnp.concatenate([plus(by_y[:2], hop(both[:2], n, 1)), by_y[2:]], 0)
    by_x = jnp.concatenate([by_x[:2], plus(by_x[2:], hop(both[2:], n, 2))], 0)
    return scatter_far(plus(here, hop(by_x, n, 1), hop(by_y, n, 2)), n)


def any_spec():
    return pl.BlockSpec(memory_space=pl.ANY)


def params():
    return pltpu.CompilerParams(vmem_limit_bytes=VMEM)


def shape(s, d):
    return jax.ShapeDtypeStruct(s, d)


def body(
    n,
    shares,
    tokens,
    held,
    routes,
    ln1_gain,
    qkv_weight,
    out_weight,
    ln2_gain,
    router_weight,
    expert_in,
    expert_out,
    grad_out,
):
    rows = qkv_weight.shape[1]
    width = expert_in.shape[2]
    local = qkv_weight.shape[2]
    pack = 4 * local + LANES
    mine_count = 16 // shares
    per_micro = 8 // shares
    fast = n == 16 and rows % 16 == 0
    c = lax.axis_index("tensor")
    me = lax.axis_index("dp")
    if fast:
        block = rows
        rel = FAR + shifted(1) + shifted(2) + shifted(3)
        orders = (FAR, shifted(1), shifted(2), shifted(3))
    else:
        block = 512
        rel = (0,)
        orders = ((0,),)
    blocks = len(rel)
    spot = me if fast else jnp.zeros((), jnp.int32)

    live = jnp.arange(8, dtype=jnp.int32)[None, :] < held
    lane = jnp.arange(LANES, dtype=jnp.int32)
    picked = (routes[..., 0:1] == lane) | (routes[..., 1:2] == lane)
    picked = (picked & live[:, :, None, None]).astype(BF16)
    mask = jnp.pad(picked, ((0, 0), (0, 0), (0, ROWS - SEQ), (0, 0)))
    counts = jnp.sum(
        (routes[..., None] == jnp.arange(EXPERTS, dtype=jnp.int32)).astype(jnp.int32), (2, 3)
    ) * live.astype(jnp.int32)[:, :, None]

    def own_first(a):
        a = a.reshape((2, per_micro, shares) + a.shape[2:])
        out = []
        for r in range(shares):
            part = a[:, :, 0]
            for t in range(1, shares):
                part = jnp.where(c ^ r == t, a[:, :, t], part)
            out.append(part.reshape((mine_count,) + a.shape[3:]))
        return jnp.concatenate(out, 0)

    counts = own_first(counts)
    live_list = own_first(live.astype(jnp.int32))
    ends = jnp.sum(
        jnp.where(jnp.arange(16)[:, None, None] >= jnp.arange(16)[None, :, None], counts[None], 0), 1
    )
    tiles = jnp.maximum((ends[15] + TILE - 1) // TILE, 1)
    numbers = jnp.arange(EXPERTS)
    tile_ends = jnp.sum(jnp.where(numbers[:, None] >= numbers[None, :], tiles[None, :], 0), 1)
    listed = jnp.arange(TILES)
    passed = (listed[:, None] >= tile_ends[None, :]).astype(jnp.int32)
    owner = jnp.minimum(jnp.sum(passed, 1), EXPERTS - 1)
    part = listed - jnp.sum(passed * tiles[None, :], 1)
    places = jnp.array(AROUND, jnp.int32)
    at = jnp.sum(jnp.where(places == (spot & 14), numbers, 0))
    around = jnp.sum(jnp.where((at + numbers)[:, None] % 8 == numbers[None, :], places[None, :], 0), 1) | (spot & 1)
    call_ends = [tile_ends[first + count - 1] for first, count in CALLS]
    call_starts = jnp.stack([jnp.zeros((), jnp.int32), *call_ends])
    info = jnp.concatenate(
        [
            jnp.stack([c, spot]).astype(jnp.int32),
            jnp.zeros((LIVE - 2,), jnp.int32),
            live_list,
            jnp.zeros((START - LIVE - 16,), jnp.int32),
            (ends - counts).reshape(-1),
            ends[15],
            jnp.zeros((TABLE - TOTAL - EXPERTS,), jnp.int32),
            owner,
            part,
            call_starts,
            jnp.zeros((RING - FIRST - 1 - len(CALLS),), jnp.int32),
            around,
        ]
    ).astype(jnp.int32)

    aux = jnp.concatenate(
        [router_weight, ln1_gain[:, None], ln2_gain[:, None], jnp.zeros((rows, LANES - 10), BF16)], 1
    )
    small = jnp.concatenate([qkv_weight[0], qkv_weight[1], qkv_weight[2], out_weight.T, aux], 1)
    if fast:
        line, (mask, info) = gather_line(small, n, [mask, info])
        w_own, (tokens, grad_out), by_x = gather_square(line, n, [tokens, grad_out])
    else:
        w_own = lax.all_gather(small, "dp", axis=0, tiled=True)[None]

    def across(a, r):
        return lax.ppermute(a, "tensor", swap(shares, r))

    shard = jnp.stack([expert_in, jnp.swapaxes(expert_out, 1, 2)])
    half = EXPERTS // 2

    def next_ring(two):
        return [ring(two[0], n, 1), ring(two[1], n, -1)]

    def over_x(blocks, axis=0):
        return hop(jnp.concatenate([b[:1] for b in blocks], axis), n, 1)

    if not fast:
        gathered = lax.all_gather(shard, "dp", axis=2, tiled=True)
        plan = [[(0, [(0, side, 0, EXPERTS)])] for side in range(2)]
    else:
        x0 = [hop(shard[1:], n, 1), hop(shard[:1], n, 1)]
        shard, x0, _ = order(shard, x0, [by_x])
        one = next_ring([jnp.concatenate([shard, x0[0]], 0)] * 2)
        plan = [[], []]
        for side in range(2):
            plan[side].append(((0, 0), [(0, side, 0, EXPERTS)]))
            plan[side].append(((0, 1), [(2 - side, 0, 0, EXPERTS)]))
            for k in range(1, 4):
                for b, far in enumerate((-k, k)):
                    plan[side].append(((far, 0), [(2 * k + 1 + b, side, 0, EXPERTS)]))
                    other = (2 * k + 1 + b, 2, 0, EXPERTS) if side == 1 else (10 + k, b, 0, EXPERTS)
                    plan[side].append(((far, 1), [other]))
            plan[side].append(((4, 0), [(9, side, 0, half), (10, side, half, EXPERTS)]))
            others = [(9, 2, 0, half), (10, 2, half, EXPERTS)] if side == 1 else [(14, 0, 0, EXPERTS)]
            plan[side].append(((4, 1), others))

    w_parts = [w_own] + [across(w_own, r) for r in range(1, shares)]

    def image(i, s):
        j = i % mine_count
        return (j // per_micro, shares * (j % per_micro) + (s[0] ^ (i // mine_count)), 0, 0)

    tok_spec = pl.BlockSpec((1, 1, SEQ, 512), image)
    mask_spec = pl.BlockSpec((1, 1, ROWS, LANES), image)

    def row_spec(cols):
        return pl.BlockSpec((1, ROWS, cols), lambda i, s: (i, 0, 0))

    def dispatch(token, with_act, cols, specs, args):
        return call(
            functools.partial(dispatch_kernel, with_act, mine_count),
            (16,),
            token,
            args + [mask],
            specs + [mask_spec],
            [any_spec()],
            [shape((EXPERTS, SLOTS, cols), BF16)],
            [
                pltpu.VMEM((EXPERTS, SPAN, cols), BF16),
                pltpu.VMEM((TILE, cols), BF16),
                pltpu.VMEM((TILE, LANES), F32),
                pltpu.VMEM((MOST, cols), BF16),
                pltpu.SemaphoreType.DMA((EXPERTS, SLOTS // TILE)),
            ],
            "dispatch",
            20,
        )

    token = (mask[0, 0, :8, :].astype(F32), info)
    if fast:
        first, one = order(token[0], one)
        token = (first, info)
        two = next_ring(one)
        x1 = over_x(one)
    token, (src, mid, proj, att, lse, gates) = call(
        functools.partial(forward_kernel, rel, block),
        (mine_count,),
        token,
        [tokens, mask, *w_parts],
        [tok_spec, mask_spec] + [any_spec()] * shares,
        [row_spec(640), row_spec(512), row_spec(1536), row_spec(512), row_spec(LANES), row_spec(LANES)],
        [
            shape((mine_count, ROWS, 640), BF16),
            shape((mine_count, ROWS, 512), F32),
            shape((mine_count, ROWS, 1536), BF16),
            shape((mine_count, ROWS, 512), BF16),
            shape((mine_count, ROWS, LANES), F32),
            shape((mine_count, ROWS, LANES), F32),
        ],
        [
            pltpu.VMEM((shares, 512, pack), BF16),
            pltpu.VMEM((16, 512), F32),
            pltpu.VMEM((ROWS, 512), F32),
            pltpu.SemaphoreType.DMA((shares, blocks)),
        ],
        "forward",
        23,
    )

    if fast:
        first, (src, mid, proj, att, lse, gates), two, (x1,) = order(
            token[0], [src, mid, proj, att, lse, gates], two, [x1]
        )
        token = (first, info)
        three = next_ring(two)
        x2 = over_x(two)
    src_oth = [across(src, r) for r in range(1, shares)]
    src_oth = src_oth[0] if shares == 2 else jnp.concatenate(src_oth, 0)
    token, (rows_a,) = dispatch(
        token,
        True,
        640,
        [
            pl.BlockSpec((1, ROWS, 640), lambda i, s: (jnp.minimum(i, mine_count - 1), 0, 0)),
            pl.BlockSpec((1, ROWS, 640), lambda i, s: (jnp.maximum(i - mine_count, 0), 0, 0)),
        ],
        [src, src_oth],
    )
    if fast:
        first, (rows_a,), three, (x2,) = order(token[0], [rows_a], three, [x2])
        token = (first, info)
        four = [ring(three[0][:, :half], n, 1), ring(three[1][:, half:], n, -1)]
        x3 = over_x(three)
    token, (rows_g,) = dispatch(token, False, 512, [tok_spec], [grad_out])

    def run_experts(token, number, pieces):
        opening, count = CALLS[number]

        def tile_at(i, s):
            at = jnp.minimum(s[FIRST + number] + i, s[FIRST + number + 1] - 1)
            return s[OWNER + at], s[PART + at]

        def out_at(i, s):
            e, t = tile_at(i, s)
            return e - opening, t, 0

        if fast:
            grad_specs = [pl.BlockSpec((3, 1, block, width), lambda i, s: (0, out_at(i, s)[0], 0, 0))] * 8
            grad_shapes = [shape((3, count, block, width), BF16)] * 8
            for far in (FIRST_FAR, THEN_FAR):
                grad_specs.append(
                    pl.BlockSpec((len(far), 1, block, width), lambda i, s: (0, out_at(i, s)[0], 0, 0))
                )
                grad_shapes.append(shape((len(far), count, block, width), BF16))
        else:
            grad_specs = [pl.BlockSpec((1, block, width), lambda i, s: (out_at(i, s)[0], 0, 0))] * 2
            grad_shapes = [shape((count, block, width), BF16)] * 2
        return call(
            functools.partial(expert_kernel, number, plan, fast, block, len(pieces)),
            (count * SLOTS // TILE,),
            token,
            [rows_a, rows_g, *pieces],
            [
                pl.BlockSpec((1, TILE, 640), lambda i, s: (*tile_at(i, s), 0)),
                pl.BlockSpec((1, TILE, 512), lambda i, s: (*tile_at(i, s), 0)),
            ]
            + [any_spec()] * len(pieces),
            [pl.BlockSpec((1, TILE, 1152), out_at)] + grad_specs,
            [shape((count, SPAN, 1152), BF16)] + grad_shapes,
            [
                pltpu.VMEM((2, 512, width), BF16),
                pltpu.VMEM((2, 512, width), BF16),
                pltpu.VMEM((512, width), F32),
                pltpu.VMEM((512, width), F32),
                pltpu.SemaphoreType.DMA((2, 2, blocks)),
            ],
            "expert",
            10 * count,
        )

    def combine(token, base, dtype):
        return call(
            functools.partial(combine_kernel, base),
            (mine_count,),
            token,
            [*y_parts, mask],
            [any_spec()] * len(y_parts) + [pl.BlockSpec((1, 1, ROWS, LANES), lambda i, s: image(i + base, s))],
            [row_spec(1152)],
            [shape((mine_count, ROWS, 1152), dtype)],
            [pltpu.VMEM((2, MOST, 1152), BF16), pltpu.SemaphoreType.DMA((2,))],
            "combine",
            14,
        )

    def turn(k, side):
        return hop(got[k][9 + side], n, 1)

    def ring_sums(group, step, ks, *arrived):
        counts = [CALLS[c][1] for c in GROUPS[group]]
        total = sum(counts)
        half = total // 2
        args, specs = [], []

        def add_spec(size, place, begin, count):
            specs.append(
                pl.BlockSpec((size, 1, block, width), lambda e: (place, jnp.clip(e - begin, 0, count - 1), 0, 0))
            )

        for k in ks:
            side, place = (0, k) if k < len(FIRST_FAR) else (1, k - len(FIRST_FAR))
            for c, begin in zip(GROUPS[group], (0, counts[0])):
                args.append(got[c][1 + k])
                add_spec(3, 0, begin, CALLS[c][1])
            for c, begin in zip(GROUPS[group], (0, counts[0])):
                args.append(turns[c][side])
                add_spec(1, place, begin, CALLS[c][1])
        for k, a in enumerate(arrived):
            args.append(a)
            add_spec(3, 0, k * half if step == 1 else 0, half if step == 1 else total)
        if step == 3:
            out_specs = [pl.BlockSpec((1, block, width), lambda e: (e, 0, 0))] * 3
            out_shape = [shape((total, block, width), t) for t in (F32, F32, BF16)]
        else:
            size = half if step == 0 else total
            out_specs = [
                pl.BlockSpec(
                    (3, 1, block, width), lambda e, b=(k * half if step == 0 else 0): (0, jnp.clip(e - b, 0, size - 1), 0, 0)
                )
                for k in range(2)
            ]
            out_shape = [shape((3, size, block, width), BF16)] * 2
        return pl.pallas_call(
            functools.partial(add_kernel, step, counts),
            grid=(total,),
            in_specs=specs,
            out_specs=out_specs,
            out_shape=out_shape,
            compiler_params=params(),
            cost_estimate=cost(3),
            name="add",
        )(*args)

    def round_on(group, step, ks, arrived=()):
        up, down = ring_sums(group, step, ks, *arrived)
        return [ring(up, n, 1), ring(down, n, -1)]

    def finish(group, arrived):
        first, second, third = ring_sums(group, 3, (7,), *arrived)
        return first, second + hop(third, n, 1).astype(F32)

    got, turns, rounds = [], [], []
    if fast:
        first, (rows_g,), four = order(token[0], [rows_g], four)
        token = (first, info)
        x4 = over_x(four, 1)
        pieces = (shard, *x0, *one, *two, *three, *four, x1, x2, x3, x4)
        token, some = run_experts(token, 0, pieces)
        first, some = order(token[0], some)
        got.append(some)
        turns = [[turn(0, 0)]]
        token, some = run_experts((first, info), 1, pieces)
        first, some, turns[0], got[0] = order(token[0], some, turns[0], got[0])
        got.append(some)
        rounds.append(round_on(0, 0, (0,)))
        turns[0].append(turn(0, 1))
        turns.append([turn(1, 0)])
        token, some = run_experts((first, info), 2, pieces)
        first, some, rounds[0], turns[0], turns[1], got[1] = order(
            token[0], some, rounds[0], turns[0], turns[1], got[1]
        )
        got.append(some)
        rounds[0] = round_on(0, 1, (1, 2), rounds[0])
        turns[1].append(turn(1, 1))
        turns.append([turn(2, 0)])
        token = (first, info)
    else:
        for number in range(len(CALLS)):
            token, some = run_experts(token, number, (gathered,))
            got.append(some)
    y_parts = [some[0] for some in got]

    comb_oth = []
    for r in range(1, shares):
        token, (sent,) = combine(token, mine_count * r, BF16)
        if fast:
            first, (sent,), rounds[0] = order(token[0], [sent], rounds[0])
            token = (first, info)
            rounds[0] = round_on(0, 2, (3, 4), rounds[0])
        comb_oth.append(across(sent, r))
    comb_oth = comb_oth[0] if shares == 2 else sum(a.astype(F32) for a in comb_oth).astype(BF16)
    token, (comb_own,) = combine(token, 0, F32)
    if fast:
        first, (comb_own, comb_oth), rounds[0], turns[1], turns[2], got[2] = order(
            token[0], [comb_own, comb_oth], rounds[0], turns[1], turns[2], got[2]
        )
        token = (first, info)
        turns[2].append(turn(2, 1))
        rounds[0] = round_on(0, 2, (5, 6), rounds[0])
        rounds.append(round_on(1, 0, (0,)))

    small_spec = pl.BlockSpec((blocks, block, pack), lambda i, s: (0, 0, 0))
    tok_out = pl.BlockSpec((1, ROWS, 512), lambda i, s: (i, 0, 0))
    def backward(token, base, count):

        def later(spec):
            return pl.BlockSpec(spec.block_shape, lambda i, s: spec.index_map(i + base, s))

        return call(
            functools.partial(backward_kernel, base, rel, rel, block),
            (count,),
            token,
            [tokens, grad_out, comb_own, comb_oth, mid, proj, att, lse, gates, *w_parts],
            [
                later(spec)
                for spec in (
                    tok_spec,
                    tok_spec,
                    row_spec(1152),
                    row_spec(1152),
                    row_spec(512),
                    row_spec(1536),
                    row_spec(512),
                    row_spec(LANES),
                    row_spec(LANES),
                )
            ]
            + [any_spec()] * shares,
            [tok_out, tok_out] + [small_spec] * shares,
            [shape((count, ROWS, 512), BF16)] * 2 + [shape((blocks, block, pack), BF16)] * shares,
            [
                pltpu.VMEM((shares, 512, pack), BF16),
                pltpu.VMEM((16, 512), F32),
                pltpu.VMEM((512, LANES), BF16),
                pltpu.VMEM((ROWS, 512), F32),
                pltpu.VMEM((ROWS, 512), F32),
                pltpu.VMEM((ROWS, 1536), BF16),
                pltpu.VMEM((shares, 512, 3 * local), F32),
                pltpu.VMEM((shares, 512, local), F32),
                pltpu.VMEM((512, LANES), F32),
                pltpu.VMEM((LANES, 512), F32),
                pltpu.SemaphoreType.DMA((shares, blocks)),
            ],
            "backward",
            22,
        )

    parts = []
    some = mine_count // 2
    token, part = backward(token, 0, some)
    if fast:
        first, part, rounds[0], rounds[1], turns[2] = order(token[0], part, rounds[0], rounds[1], turns[2])
        token = (first, info)
        rounds[1] = round_on(1, 1, (1, 2), rounds[1])
        total = [finish(0, rounds[0])]
    parts.append(part)
    token, part = backward(token, some, some // 2)
    if fast:
        first, part, rounds[1] = order(token[0], part, rounds[1])
        token = (first, info)
        rounds[1] = round_on(1, 2, (3, 4), rounds[1])
    parts.append(part)
    token, part = backward(token, some + some // 2, some // 2)
    if fast:
        first, part, rounds[1] = order(token[0], part, rounds[1])
    parts.append(part)
    grads = [[part[2 + r] for part in parts] for r in range(shares)]
    both = sum(a.astype(F32) for a in grads[0])
    for r in range(1, shares):
        both = both + across(plus(*grads[r]), r).astype(F32)
    both = both.astype(BF16)
    if fast:
        mine = scatter_small(both, n)
    else:
        mine = lax.psum_scatter(both[0], "dp", scatter_dimension=0, tiled=True).astype(F32)

    if fast:
        rounds[1] = round_on(1, 2, (5, 6), rounds[1])
        total.append(finish(1, rounds[1]))
        sums_in, sums_out = [[t[side] for t in total] for side in range(2)]
    else:
        sums_in, sums_out = [
            [lax.psum_scatter(g[side], "dp", scatter_dimension=1, tiled=True).astype(F32) for g in got]
            for side in (1, 2)
        ]

    def whole(which):
        pieces = []
        for r in range(shares):
            pieces += [across(part[which], r) if r else part[which] for part in parts]
        out = pl.pallas_call(
            functools.partial(assemble_kernel, shares),
            grid_spec=pltpu.PrefetchScalarGridSpec(
                num_scalar_prefetch=1,
                grid=(2,),
                in_specs=[pl.BlockSpec(a.shape, lambda i, s: (0, 0, 0)) for a in pieces],
                out_specs=pl.BlockSpec((1, SEQ, 8, 512), lambda i, s: (i, 0, 0, 0)),
                scratch_shapes=[pltpu.VMEM((4, SEQ * 8, LANES), F32)],
            ),
            out_shape=shape((2, SEQ, 8, 512), BF16),
            compiler_params=params(),
            cost_estimate=cost(6),
            name="assemble",
        )(info, *pieces)
        return jnp.swapaxes(out, 1, 2)

    return (
        whole(0),
        whole(1),
        mine[:, 4 * local + 8],
        jnp.stack([mine[:, j * local : (j + 1) * local] for j in range(3)]),
        mine[:, 3 * local : 4 * local].T,
        mine[:, 4 * local + 9],
        mine[:, 4 * local : 4 * local + 8],
        jnp.concatenate(sums_in, 0),
        jnp.swapaxes(jnp.concatenate(sums_out, 0), 1, 2),
    )


def solution(mesh):
    placed = (
        P(None, "dp", None, None),
        P(None, "dp"),
        P(None, "dp", None, None),
        P("dp"),
        P(None, "dp", "tensor"),
        P("tensor", "dp"),
        P("dp"),
        P("dp", None),
        P(None, "dp", "tensor"),
        P(None, "tensor", "dp"),
        P(None, "dp", None, None),
    )
    return jax.shard_map(
        functools.partial(body, mesh.shape["dp"], mesh.shape["tensor"]),
        mesh=mesh,
        in_specs=placed,
        out_specs=(
            P(None, "dp", None, None),
            P(None, "dp", None, None),
            P("dp"),
            P(None, "dp", "tensor"),
            P("tensor", "dp"),
            P("dp"),
            P("dp", None),
            P(None, "dp", "tensor"),
            P(None, "tensor", "dp"),
        ),
        check_vma=False,
    )
```

time: 810 us -> 541 us (0.67)
  waiting for transfers between devices: 299 us -> 100 us
  Pallas kernels: 142 us -> 266 us
  other arithmetic: 139 us -> 21.9 us
  starting transfers between devices: 158 us -> 108 us
  local copies, waits for them, and re-layouts: 54.7 us -> 32.8 us
    ppermute x136 -> x50, waiting for transfers between devices: 299 us -> 99.9 us  [the longest x24 54.3 us: ring(): return lax.ppermute(a, 'dp', pairs)]
    pallas_call x6 -> x23, Pallas kernels: 142 us -> 266 us  [the longest x11 212 us: call(): pl.pallas_call(in_turn(kernel, len(args)), grid_spec=pltpu.PrefetchScalar...]
    pallas_call x7 -> x0, other arithmetic: 93.1 us -> none  [body(): pl.pallas_call(functools.partial(expert_kernel, at, rel_a, rel_b, scat_a,...]
    ppermute x136 -> x50, starting transfers between devices: 158 us -> 107 us  [the longest x24 67.4 us: ring(): return lax.ppermute(a, 'dp', pairs)]
    concatenate x55 -> x9, other arithmetic: 31.9 us -> 5.4 us  [the longest x4 2.36 us: over_x(): return hop(jnp.concatenate([b[:1] for b in blocks], axis), n, 1)]
    reshape x2 -> x0, local copies, waits for them, and re-layouts: 15.5 us -> none  [whole(): return jnp.concatenate(out, 2).reshape(2, 8, SEQ, 512)]
    unnamed x207 -> x125, local copies, waits for them, and re-layouts: 16.3 us -> 11.8 us
  transfers between devices with their start and end apart: 142 -> 60, of which waited for: 70 -> 20; matrix products, arithmetic and copies ran while one was open for 23% -> 6% of each run, Pallas kernels for 18% -> 40%
where the time goes in v2:
time: 541 us; the launch traced here: 532 us
  Pallas kernels  266 us (49%)
  starting transfers between devices  108 us (20%)
  waiting for transfers between devices  100 us (18%)
  local copies, waits for them, and re-layouts  32.8 us (6%)
  other arithmetic  21.9 us (4%)
    pallas_call x11, Pallas kernels, call(): pl.pallas_call(in_turn(kernel, len(args)), grid_spec=pltpu.PrefetchScalar...  212 us
    ppermute x24, starting transfers between devices, ring(): return lax.ppermute(a, 'dp', pairs)  67.4 us
    ppermute x24, waiting for transfers between devices, ring(): return lax.ppermute(a, 'dp', pairs)  54.3 us
    ppermute x26, waiting for transfers between devices, hop(): return lax.ppermute(a, 'dp', swap(n, bits))  45.7 us
    pallas_call x10, Pallas kernels, ring_sums(): pl.pallas_call(functools.partial(add_kernel, step, counts), grid=(total,)...  42.5 us
    ppermute x26, starting transfers between devices, hop(): return lax.ppermute(a, 'dp', swap(n, bits))  39.7 us
    pallas_call x2, Pallas kernels, whole(): pl.pallas_call(functools.partial(assemble_kernel, shares), grid_spec=pltp...  12.2 us
    unnamed x125, local copies, waits for them, and re-layouts  11.8 us
  transfers between devices with their start and end apart: 60, of which 20 were waited for; matrix products, arithmetic and copies ran while one was open for 6% of the time, Pallas kernels for 40%

profile of v2, /device:TPU:0, one launch (start us, length us, event | category | flops | bytes accessed | tf_op | source)
XLA Modules:
  0.0 532.0 jit_solution(2598848376674237264)
XLA Ops:
  4.6 4.1 collective-permute-start
  19.2 1.6 collective-permute-start.1
  21.7 2.6 concatenate.50.info
  24.5 1.6 collective-permute-start.5
  28.8 3.5 collective-permute-done.5
  32.2 7.6 %collective-permute-done.4 = bf16[4,32,1152]{2,1,0:T(8,128)(2,1)S(1)} collective-permute-done((bf16[4,32,1152]{2,1,0:T(8,128)(2,1)S(1)}, bf16[4,32,1152]{2,1,0:T(8,128)(2,1)S(1)}, u32[]{:S(2)}, u32[]{:S(2)}) %collective-permute-start.4) | collective-permute-done | bytes 294944 | tf_op jit(solution)/shard_map/ppermute | solution.py:585
  40.8 1.6 collective-permute-start.7
  43.6 1.6 collective-permute-start.9
  46.7 29.7 %collective-permute-done.7.refs_6_ = bf16[3,8,32,1024]{3,2,1,0:T(8,128)(2,1)S(1)} collective-permute-done((bf16[3,8,32,1024]{3,2,1,0:T(8,128)(2,1)S(1)}, bf16[3,8,32,1024]{3,2,1,0:T(8,128)(2,1)S(1)}, u32[]{:S(2)}, u32[]{:S(2)}) %collective-permute-start.7) | collective-permute-done | bytes 1572896 | tf_op jit(solution)/shard_map/ppermute | solution.py:642
  76.4 3.4 collective-permute-done.6.refs_5_
  79.8 2.0 collective-permute-start.12
  87.1 2.9 copy.58.refs_0_
  91.1 20.5 %forward.1 = (f32[8,128]{1,0:T(8,128)}, bf16[8,208,640]{2,1,0:T(8,128)(2,1)}, f32[8,208,512]{2,1,0:T(8,128)}, bf16[8,208,1536]{2,1,0:T(8,128)(2,1)}, bf16[8,208,...) custom-call(s32[352]{0:T(512)} %concatenate.50.info, f32[8,128]{1,0:T(8,128)} %bitcast_convert_fusion.earlier, ...), custom_call_target="tpu_custom_call" | custom-call | flops 2300 | bytes 1000 | tf_op jit(solution)/shard_map/forward/pallas_call | solution.py:620
  111.7 2.4 collective-permute-done.11.refs_7_
  114.1 2.0 collective-permute-start.16
  120.9 19.6 %dispatch.2 = (f32[8,128]{1,0:T(8,128)}, bf16[8,1280,640]{2,1,0:T(8,128)(2,1)}) custom-call(s32[352]{0:T(512)} %concatenate.50.info, f32[8,128]{1,0:T(8,128)} %get-tuple-element.241.earlier, bf16[8,208,640]{2,1,0:T(8,128)(2,1)} %get-tuple-element.242.refs_0_, bf16[8,208,640]{2,1,0:T(8,128)(2,1)} %collective-permute-done.14.refs_1_, ...), custom_call_target="tpu_custom_call" | custom-call | flops 2000 | bytes 1000 | tf_op jit(solution)/shard_map/dispatch/pallas_call | solution.py:620
  140.5 4.1 collective-permute-done.17.refs_14_
  144.6 6.5 %collective-permute-done.15.refs_9_ = bf16[3,8,32,1024]{3,2,1,0:T(8,128)(2,1)S(1)} collective-permute-done((bf16[3,8,32,1024]{3,2,1,0:T(8,128)(2,1)}, bf16[3,8,32,1024]{3,2,1,0:T(8,128)(2,1)S(1)}, u32[]{:S(2)}, u32[]{:S(2)}) %collective-permute-start.15) | collective-permute-done | bytes 1572896 | tf_op jit(solution)/shard_map/ppermute | solution.py:642
  156.0 2.4 collective-permute-start.20
  158.4 2.9 copy.59.refs_0_.refs_1_
  161.3 17.6 %dispatch.3 = (f32[8,128]{1,0:T(8,128)}, bf16[8,1280,512]{2,1,0:T(8,128)(2,1)}) custom-call(s32[352]{0:T(512)} %concatenate.50.info, f32[8,128]{1,0:T(8,128)} %get-tuple-element.247.earlier, bf16[2,8,197,512]{3,2,1,0:T(8,128)(2,1)} %copy.59.refs_0_.refs_1_, bf16[2,8,208,128]{3,2,1,0:T(8,128)(2,1)} %copy-done.2), custom_call_target="tpu_custom_call" | custom-call | flops 2000 | bytes 1000 | tf_op jit(solution)/shard_map/dispatch/pallas_call | solution.py:620
  180.7 11.4 %collective-permute-done.21.refs_16_ = bf16[1,8,32,1024]{3,2,1,0:T(8,128)(2,1)S(1)} collective-permute-done((bf16[1,8,32,1024]{3,2,1,0:T(8,128)(2,1)S(1)}, bf16[1,8,32,1024]{3,2,1,0:T(8,128)(2,1)S(1)}, u32[]{:S(2)}, u32[]{:S(2)}) %collective-permute-start.21) | collective-permute-done | bytes 524320 | tf_op jit(solution)/shard_map/ppermute | solution.py:585
  193.0 37.4 %expert.3 = (f32[8,128]{1,0:T(8,128)}, bf16[4,1536,1152]{2,1,0:T(8,128)(2,1)}, bf16[3,4,32,1024]{3,2,1,0:T(8,128)(2,1)}, bf16[3,4,32,1024]{3,2,1,0:T(8,128)(2,1)...) custom-call(s32[352]{0:T(512)} %concatenate.50.info, ...), custom_call_target="tpu_custom_call" | custom-call | flops 4000 | bytes 1000 | tf_op jit(solution)/shard_map/expert/pallas_call | solution.py:620
  230.5 25.3 %expert.4 = (f32[8,128]{1,0:T(8,128)}, bf16[2,1536,1152]{2,1,0:T(8,128)(2,1)}, bf16[3,2,32,1024]{3,2,1,0:T(8,128)(2,1)}, bf16[3,2,32,1024]{3,2,1,0:T(8,128)(2,1)...) custom-call(s32[352]{0:T(512)} %concatenate.50.info, ...), custom_call_target="tpu_custom_call" | custom-call | flops 2000 | bytes 1000 | tf_op jit(solution)/shard_map/expert/pallas_call | solution.py:620
  255.8 2.0 collective-permute-start.26
  257.8 3.4 add.125
  261.3 24.3 %collective-permute-start.23 = (bf16[3,2,32,1024]{3,2,1,0:T(8,128)(2,1)}, bf16[3,2,32,1024]{3,2,1,0:T(8,128)(2,1)S(1)}, u32[]{:S(2)}, u32[]{:S(2)}) collective-permute-start(bf16[3,2,32,1024]{3,2,1,0:T(8,128)(2,1)} %get-tuple-element.300), channel_id=1, source_target_pairs={{0,8},{2,10},{8,16},{10,18},{16,24},{18,26},{24,28},{26,30},{28,20... | collective-permute-start | bytes 1179656 | tf_op jit(solution)/shard_map/ppermute | solution.py:642
  285.7 17.5 %expert.5 = (f32[8,128]{1,0:T(8,128)}, bf16[2,1536,1152]{2,1,0:T(8,128)(2,1)}, bf16[3,2,32,1024]{3,2,1,0:T(8,128)(2,1)}, bf16[3,2,32,1024]{3,2,1,0:T(8,128)(2,1)...) custom-call(s32[352]{0:T(512)} %concatenate.50.info, ...), custom_call_target="tpu_custom_call" | custom-call | flops 2000 | bytes 1000 | tf_op jit(solution)/shard_map/expert/pallas_call | solution.py:620
  304.1 4.2 add.126
  308.3 14.4 %collective-permute-start.27 = (bf16[3,4,32,1024]{3,2,1,0:T(8,128)(2,1)}, bf16[3,4,32,1024]{3,2,1,0:T(8,128)(2,1)S(1)}, u32[]{:S(2)}, u32[]{:S(2)}) collective-permute-start(bf16[3,4,32,1024]{3,2,1,0:T(8,128)(2,1)} %get-tuple-element.325), channel_id=1, source_target_pairs={{0,8},{2,10},{8,16},{10,18},{16,24},{18,26},{24,28},{26,30},{28,20... | collective-permute-start | bytes 2359304 | tf_op jit(solution)/shard_map/ppermute | solution.py:642
  322.7 12.1 %combine.2 = (f32[8,128]{1,0:T(8,128)}, bf16[8,208,1152]{2,1,0:T(8,128)(2,1)}) custom-call(s32[352]{0:T(512)} %concatenate.50.info, f32[8,128]{1,0:T(8,128)} %get-tuple-element.314.earlier, bf16[4,1536,1152]{2,1,0:T(8,128)(2,1)} %get-tuple-element.315.refs_0_, bf16[2,1536,1152]{2,1,0:T(8,128)(2,1)} %get-tuple-element.316.refs_1_, ...), custom_call_target="tpu_custom_call" | custom-call | flops 1400 | bytes 1000 | tf_op jit(solution)/shard_map/combine/pallas_call | solution.py:620
  334.8 2.6 collective-permute-done.27.refs_4_
  337.5 2.1 collective-permute-done.28.refs_5_
  340.5 4.2 add.127
  346.7 1.7 collective-permute-start.32
  348.8 12.5 %combine.3 = (f32[8,128]{1,0:T(8,128)}, f32[8,208,1152]{2,1,0:T(8,128)}) custom-call(s32[352]{0:T(512)} %concatenate.50.info, f32[8,128]{1,0:T(8,128)} %get-tuple-element.327.earlier, bf16[4,1536,1152]{2,1,0:T(8,128)(2,1)} %get-tuple-element.315.refs_0_, bf16[2,1536,1152]{2,1,0:T(8,128)(2,1)} %get-tuple-element.316.refs_1_, ...), custom_call_target="tpu_custom_call" | custom-call | flops 1400 | bytes 1000 | tf_op jit(solution)/shard_map/combine/pallas_call | solution.py:620
  361.3 9.9 %collective-permute-done.33.refs_3_.refs_7_ = bf16[3,2,32,1024]{3,2,1,0:T(8,128)(2,1)S(1)} collective-permute-done((bf16[3,2,32,1024]{3,2,1,0:T(8,128)(2,1)S(1)}, bf16[3,2,32,1024]{3,2,1,0:T(8,128)(2,1)S(1)}, u32[]{:S(2)}, u32[]{:S(2)}) %collective-permute-start.33) | collective-permute-done | bytes 393248 | tf_op jit(solution)/shard_map/ppermute | solution.py:585
  372.1 5.1 add.128
  377.3 2.9 collective-permute-start.34
  381.1 3.7 add.129
  384.8 1.7 collective-permute-start.36
  387.0 23.7 %backward.3 = (f32[8,128]{1,0:T(8,128)}, bf16[4,208,512]{2,1,0:T(8,128)(2,1)}, bf16[4,208,512]{2,1,0:T(8,128)(2,1)}, bf16[16,32,1152]{2,1,0:T(8,128)(2,1)}, bf16[16,32,1152]{2,1,0:T(8,128)(2,1)}) custom-call(s32[352]{0:T(512)} %concatenate.50.info, f32[8,128]{1,0:T(8,128)} %get-tuple-element.350.earlier, bf16[2,8,197,512]{3,2,1,0:T(8,128)(2,1)} %copy.58.refs_0_, ...), custom_call_target="tpu_custom_call" | custom-call | flops 2200 | bytes 1000 | tf_op jit(solution)/shard_map/backward/pallas_call | solution.py:620
  411.6 4.8 add.130
  416.5 2.0 collective-permute-start.40
  418.5 18.1 %backward.4 = (f32[8,128]{1,0:T(8,128)}, bf16[2,208,512]{2,1,0:T(8,128)(2,1)}, bf16[2,208,512]{2,1,0:T(8,128)(2,1)}, bf16[16,32,1152]{2,1,0:T(8,128)(2,1)}, bf16[16,32,1152]{2,1,0:T(8,128)(2,1)}) custom-call(s32[352]{0:T(512)} %concatenate.50.info, f32[8,128]{1,0:T(8,128)} %get-tuple-element.377.earlier, bf16[2,8,197,512]{3,2,1,0:T(8,128)(2,1)} %copy.58.refs_0_, ...), custom_call_target="tpu_custom_call" | custom-call | flops 2200 | bytes 1000 | tf_op jit(solution)/shard_map/backward/pallas_call | solution.py:620
  437.7 4.6 add.131
  443.8 4.3 collective-permute-start.42
  448.1 7.5 %backward.5 = (f32[8,128]{1,0:T(8,128)}, bf16[2,208,512]{2,1,0:T(8,128)(2,1)}, bf16[2,208,512]{2,1,0:T(8,128)(2,1)}, bf16[16,32,1152]{2,1,0:T(8,128)(2,1)}, bf16[16,32,1152]{2,1,0:T(8,128)(2,1)}) custom-call(s32[352]{0:T(512)} %concatenate.50.info, f32[8,128]{1,0:T(8,128)} %get-tuple-element.393.earlier, bf16[2,8,197,512]{3,2,1,0:T(8,128)(2,1)} %copy.58.refs_0_, ...), custom_call_target="tpu_custom_call" | custom-call | flops 2200 | bytes 1000 | tf_op jit(solution)/shard_map/backward/pallas_call | solution.py:620
  455.7 6.6 %collective-permute-done.41.refs_8_ = bf16[3,4,32,1024]{3,2,1,0:T(8,128)(2,1)S(1)} collective-permute-done((bf16[3,4,32,1024]{3,2,1,0:T(8,128)(2,1)}, bf16[3,4,32,1024]{3,2,1,0:T(8,128)(2,1)S(1)}, u32[]{:S(2)}, u32[]{:S(2)}) %collective-permute-start.41) | collective-permute-done | bytes 786464 | tf_op jit(solution)/shard_map/ppermute | solution.py:642
  463.4 2.7 add_convert_fusion.1
  466.2 4.0 add.132
  470.1 4.4 collective-permute-start.58
  475.8 3.6 collective-permute-start.50
  479.4 4.6 add.133
  484.7 4.5 collective-permute-start.56
  492.2 1.6 collective-permute-start.51
  494.8 6.1 %assemble.2 = bf16[2,197,8,512]{3,2,1,0:T(8,128)(2,1)} custom-call(s32[352]{0:T(512)} %concatenate.50.info, bf16[4,208,512]{2,1,0:T(8,128)(2,1)} %get-tuple-element.376.refs_0_, bf16[2,208,512]{2,1,0:T(8,128)(2,1)} %get-tuple-element.392.refs_1_, bf16[2,208,512]{2,1,0:T(8,128)(2,1)} %get-tuple-element.408.refs_2_, ...), custom_call_target="tpu_custom_call" | custom-call | flops 600 | bytes 1000 | tf_op jit(solution)/shard_map/assemble/pallas_call | solution.py:1160
  501.7 6.1 %assemble.3 = bf16[2,197,8,512]{3,2,1,0:T(8,128)(2,1)} custom-call(s32[352]{0:T(512)} %concatenate.50.info, bf16[4,208,512]{2,1,0:T(8,128)(2,1)} %get-tuple-element.409.refs_0_, bf16[2,208,512]{2,1,0:T(8,128)(2,1)} %get-tuple-element.410.refs_1_, bf16[2,208,512]{2,1,0:T(8,128)(2,1)} %get-tuple-element.411.refs_2_, ...), custom_call_target="tpu_custom_call" | custom-call | flops 600 | bytes 1000 | tf_op jit(solution)/shard_map/assemble/pallas_call | solution.py:1160
  509.6 4.0 add.134
  515.0 2.2 pad_maximum_fusion.4
  519.7 2.1 collective-permute-done.59
  521.9 1.7 collective-permute-done.54
  523.6 2.0 collective-permute-start.55
  526.6 2.3 collective-permute-done.55
  (286 shorter events, 67.7 us)
Async XLA Ops:
  3.7 24.0 %copy-start.42 = (bf16[8,32,1024]{2,1,0:T(8,128)(2,1)S(1)}, bf16[8,32,1024]{2,1,0:T(8,128)(2,1)}, u32[]{:S(2)}) copy-start(bf16[8,32,1024]{2,1,0:T(8,128)(2,1)} %param.20) | copy-start | bytes 1572868
  4.6 14.6 %collective-permute-start = (bf16[1,32,1152]{2,1,0:T(8,128)(2,1)S(1)}, bf16[1,32,1152]{2,1,0:T(8,128)(2,1)S(1)}, u32[]{:S(2)}, u32[]{:S(2)}) collective-permute-start(bf16[1,32,1152]{2,1,0:T(8,128)(2,1)S(1)} %bitcast.51), channel_id=1, source_target_pairs={{0,16},{2,18},{4,20},{6,22},{8,24},{10,26},{12,28},{14,30},{16,0},... | collective-permute-start | bytes 221192 | tf_op jit(solution)/shard_map/ppermute | solution.py:585
  8.6 31.2 %collective-permute-start.3 = (bf16[1,8,32,1024]{3,2,1,0:T(8,128)(2,1)}, bf16[1,8,32,1024]{3,2,1,0:T(8,128)(2,1)S(1)}, u32[]{:S(2)}, u32[]{:S(2)}) collective-permute-start(bf16[1,8,32,1024]{3,2,1,0:T(8,128)(2,1)} %bitcast.54), channel_id=1, source_target_pairs={{0,2},{2,0},{4,6},{6,4},{8,10},{10,8},{12,14},{14,12},{16,18},{18,... | collective-permute-start | bytes 1572872 | tf_op jit(solution)/shard_map/ppermute | solution.py:585
  10.1 29.7 %collective-permute-start.2 = (bf16[1,8,32,1024]{3,2,1,0:T(8,128)(2,1)}, bf16[1,8,32,1024]{3,2,1,0:T(8,128)(2,1)S(1)}, u32[]{:S(2)}, u32[]{:S(2)}) collective-permute-start(bf16[1,8,32,1024]{3,2,1,0:T(8,128)(2,1)} %bitcast.56), channel_id=1, source_target_pairs={{0,2},{2,0},{4,6},{6,4},{8,10},{10,8},{12,14},{14,12},{16,18},{18,... | collective-permute-start | bytes 1572872 | tf_op jit(solution)/shard_map/ppermute | solution.py:585
  19.2 5.3 %collective-permute-start.1 = (bf16[2,32,1152]{2,1,0:T(8,128)(2,1)S(1)}, bf16[2,32,1152]{2,1,0:T(8,128)(2,1)S(1)}, u32[]{:S(2)}, u32[]{:S(2)}) collective-permute-start(bf16[2,32,1152]{2,1,0:T(8,128)(2,1)S(1)} %pad_maximum_fusion.9), channel_id=1, source_target_pairs={{0,8},{2,10},{4,12},{6,14},{8,0},{10,2},{12,4},{14,6},{16,24},{18,... | collective-permute-start | bytes 442376 | tf_op jit(solution)/shard_map/ppermute | solution.py:585
  24.5 7.7 %collective-permute-start.5 = (bf16[4,32,1152]{2,1,0:T(8,128)(2,1)S(1)}, bf16[4,32,1152]{2,1,0:T(8,128)(2,1)S(1)}, u32[]{:S(2)}, u32[]{:S(2)}) collective-permute-start(bf16[4,32,1152]{2,1,0:T(8,128)(2,1)S(1)} %pad_maximum_fusion.6), channel_id=1, source_target_pairs={{0,4},{2,6},{4,0},{6,2},{8,12},{10,14},{12,8},{14,10},{16,20},{18,... | collective-permute-start | bytes 884744 | tf_op jit(solution)/shard_map/ppermute | solution.py:585
  26.1 13.7 %collective-permute-start.4 = (bf16[4,32,1152]{2,1,0:T(8,128)(2,1)S(1)}, bf16[4,32,1152]{2,1,0:T(8,128)(2,1)S(1)}, u32[]{:S(2)}, u32[]{:S(2)}) collective-permute-start(bf16[4,32,1152]{2,1,0:T(8,128)(2,1)S(1)} %pad_maximum_fusion.6), channel_id=1, source_target_pairs={{0,2},{2,0},{4,6},{6,4},{8,10},{10,8},{12,14},{14,12},{16,18},{18,... | collective-permute-start | bytes 884744 | tf_op jit(solution)/shard_map/ppermute | solution.py:585
  40.8 35.6 %collective-permute-start.7 = (bf16[3,8,32,1024]{3,2,1,0:T(8,128)(2,1)S(1)}, bf16[3,8,32,1024]{3,2,1,0:T(8,128)(2,1)S(1)}, u32[]{:S(2)}, u32[]{:S(2)}) collective-permute-start(bf16[3,8,32,1024]{3,2,1,0:T(8,128)(2,1)S(1)} %constant_dynamic-update-slice_fusion), channel_id=1, source_target_pairs={{0,4},{2,6},{8,0},{10,2},{16,8},{18,10},{24,16},{26,18},{28,24},{3... | collective-permute-start | bytes 4718600 | tf_op jit(solution)/shard_map/ppermute | solution.py:642
  42.4 37.4 %collective-permute-start.6 = (bf16[3,8,32,1024]{3,2,1,0:T(8,128)(2,1)S(1)}, bf16[3,8,32,1024]{3,2,1,0:T(8,128)(2,1)}, u32[]{:S(2)}, u32[]{:S(2)}) collective-permute-start(bf16[3,8,32,1024]{3,2,1,0:T(8,128)(2,1)S(1)} %constant_dynamic-update-slice_fusion), channel_id=1, source_target_pairs={{0,8},{2,10},{8,16},{10,18},{16,24},{18,26},{24,28},{26,30},{28,20... | collective-permute-start | bytes 4718600 | tf_op jit(solution)/shard_map/ppermute | solution.py:642
  43.6 39.3 %collective-permute-start.9 = (bf16[2,32,1152]{2,1,0:T(8,128)(2,1)S(1)}, bf16[2,32,1152]{2,1,0:T(8,128)(2,1)S(1)}, u32[]{:S(2)}, u32[]{:S(2)}) collective-permute-start(bf16[2,32,1152]{2,1,0:T(8,128)(2,1)S(1)} %slice.161), channel_id=1, source_target_pairs={{0,4},{2,6},{4,0},{6,2},{8,12},{10,14},{12,8},{14,10},{16,20},{18,... | collective-permute-start | bytes 442376 | tf_op jit(solution)/shard_map/ppermute | solution.py:585
  45.2 36.7 %collective-permute-start.8 = (bf16[2,32,1152]{2,1,0:T(8,128)(2,1)S(1)}, bf16[2,32,1152]{2,1,0:T(8,128)(2,1)S(1)}, u32[]{:S(2)}, u32[]{:S(2)}) collective-permute-start(bf16[2,32,1152]{2,1,0:T(8,128)(2,1)S(1)} %slice.160), channel_id=1, source_target_pairs={{0,2},{2,0},{4,6},{6,4},{8,10},{10,8},{12,14},{14,12},{16,18},{18,... | collective-permute-start | bytes 442376 | tf_op jit(solution)/shard_map/ppermute | solution.py:585
  79.8 34.2 %collective-permute-start.11 = (bf16[3,8,32,1024]{3,2,1,0:T(8,128)(2,1)}, bf16[3,8,32,1024]{3,2,1,0:T(8,128)(2,1)}, u32[]{:S(2)}, u32[]{:S(2)}) collective-permute-start(bf16[3,8,32,1024]{3,2,1,0:T(8,128)(2,1)} %collective-permute-done.6.refs_5_), channel_id=1, source_target_pairs={{0,8},{2,10},{8,16},{10,18},{16,24},{18,26},{24,28},{26,30},{28,20... | collective-permute-start | bytes 4718600 | tf_op jit(solution)/shard_map/ppermute | solution.py:642
  79.8 34.2 %collective-permute-start.12 = (bf16[3,8,32,1024]{3,2,1,0:T(8,128)(2,1)S(1)}, bf16[3,8,32,1024]{3,2,1,0:T(8,128)(2,1)}, u32[]{:S(2)}, u32[]{:S(2)}) collective-permute-start(bf16[3,8,32,1024]{3,2,1,0:T(8,128)(2,1)S(1)} %collective-permute-done.7.refs_6_), channel_id=1, source_target_pairs={{0,4},{2,6},{8,0},{10,2},{16,8},{18,10},{24,16},{26,18},{28,24},{3... | collective-permute-start | bytes 4718600 | tf_op jit(solution)/shard_map/ppermute | solution.py:642
  82.9 7.1 %collective-permute-start.10 = (bf16[16,32,1152]{2,1,0:T(8,128)(2,1)S(1)}, bf16[16,32,1152]{2,1,0:T(8,128)(2,1)S(1)}, u32[]{:S(2)}, u32[]{:S(2)}) collective-permute-start(bf16[16,32,1152]{2,1,0:T(8,128)(2,1)S(1)} %constant_dynamic-update-slice_fusion.2.refs_2_.refs_9_), channel_id=1, source_target_pairs={{0,1},{1,0},{2,3},{3,2},{4,5},{5,4},{6,7},{7,6},{8,9},{9,8},{10,11... | collective-permute-start | bytes 3538952 | tf_op jit(solution)/shard_map/ppermute | solution.py:786
  85.6 26.0 %collective-permute-start.13 = (bf16[2,8,32,1024]{3,2,1,0:T(8,128)(2,1)}, bf16[2,8,32,1024]{3,2,1,0:T(8,128)(2,1)S(1)}, u32[]{:S(2)}, u32[]{:S(2)}) collective-permute-start(bf16[2,8,32,1024]{3,2,1,0:T(8,128)(2,1)} %pad_maximum_fusion.1), channel_id=1, source_target_pairs={{0,2},{2,0},{4,6},{6,4},{8,10},{10,8},{12,14},{14,12},{16,18},{18,... | collective-permute-start | bytes 3145736 | tf_op jit(solution)/shard_map/ppermute | solution.py:585
  114.0 6.8 %collective-permute-start.14 = (bf16[8,208,640]{2,1,0:T(8,128)(2,1)}, bf16[8,208,640]{2,1,0:T(8,128)(2,1)}, u32[]{:S(2)}, u32[]{:S(2)}) collective-permute-start(bf16[8,208,640]{2,1,0:T(8,128)(2,1)} %get-tuple-element.242.refs_0_), channel_id=1, source_target_pairs={{0,1},{1,0},{2,3},{3,2},{4,5},{5,4},{6,7},{7,6},{8,9},{9,8},{10,11... | collective-permute-start | bytes 6389768 | tf_op jit(solution)/shard_map/ppermute | solution.py:786
  114.0 37.0 %collective-permute-start.15 = (bf16[3,8,32,1024]{3,2,1,0:T(8,128)(2,1)}, bf16[3,8,32,1024]{3,2,1,0:T(8,128)(2,1)S(1)}, u32[]{:S(2)}, u32[]{:S(2)}) collective-permute-start(bf16[3,8,32,1024]{3,2,1,0:T(8,128)(2,1)} %collective-permute-done.11.refs_7_), channel_id=1, source_target_pairs={{0,8},{2,10},{8,16},{10,18},{16,24},{18,26},{24,28},{26,30},{28,20... | collective-permute-start | bytes 4718600 | tf_op jit(solution)/shard_map/ppermute | solution.py:642
  114.1 37.0 %collective-permute-start.16 = (bf16[3,8,32,1024]{3,2,1,0:T(8,128)(2,1)}, bf16[3,8,32,1024]{3,2,1,0:T(8,128)(2,1)S(1)}, u32[]{:S(2)}, u32[]{:S(2)}) collective-permute-start(bf16[3,8,32,1024]{3,2,1,0:T(8,128)(2,1)} %collective-permute-done.12.refs_8_), channel_id=1, source_target_pairs={{0,4},{2,6},{8,0},{10,2},{16,8},{18,10},{24,16},{26,18},{28,24},{3... | collective-permute-start | bytes 4718600 | tf_op jit(solution)/shard_map/ppermute | solution.py:642
  119.4 25.2 %collective-permute-start.17 = (bf16[2,8,32,1024]{3,2,1,0:T(8,128)(2,1)}, bf16[2,8,32,1024]{3,2,1,0:T(8,128)(2,1)S(1)}, u32[]{:S(2)}, u32[]{:S(2)}) collective-permute-start(bf16[2,8,32,1024]{3,2,1,0:T(8,128)(2,1)} %pad_maximum_fusion.2), channel_id=1, source_target_pairs={{0,2},{2,0},{4,6},{6,4},{8,10},{10,8},{12,14},{14,12},{16,18},{18,... | collective-permute-start | bytes 3145736 | tf_op jit(solution)/shard_map/ppermute | solution.py:585
  153.3 25.7 %collective-permute-start.19 = (bf16[3,4,32,1024]{3,2,1,0:T(8,128)(2,1)}, bf16[3,4,32,1024]{3,2,1,0:T(8,128)(2,1)S(1)}, u32[]{:S(2)}, u32[]{:S(2)}) collective-permute-start(bf16[3,4,32,1024]{3,2,1,0:T(8,128)(2,1)} %slice.167), channel_id=1, source_target_pairs={{0,4},{2,6},{8,0},{10,2},{16,8},{18,10},{24,16},{26,18},{28,24},{3... | collective-permute-start | bytes 2359304 | tf_op jit(solution)/shard_map/ppermute | solution.py:642
  154.8 24.2 %collective-permute-start.18 = (bf16[3,4,32,1024]{3,2,1,0:T(8,128)(2,1)}, bf16[3,4,32,1024]{3,2,1,0:T(8,128)(2,1)S(1)}, u32[]{:S(2)}, u32[]{:S(2)}) collective-permute-start(bf16[3,4,32,1024]{3,2,1,0:T(8,128)(2,1)} %slice.166), channel_id=1, source_target_pairs={{0,8},{2,10},{8,16},{10,18},{16,24},{18,26},{24,28},{26,30},{28,20... | collective-permute-start | bytes 2359304 | tf_op jit(solution)/shard_map/ppermute | solution.py:642
  156.0 24.7 %collective-permute-start.20 = (bf16[2,8,32,1024]{3,2,1,0:T(8,128)(2,1)S(1)}, bf16[2,8,32,1024]{3,2,1,0:T(8,128)(2,1)S(1)}, u32[]{:S(2)}, u32[]{:S(2)}) collective-permute-start(bf16[2,8,32,1024]{3,2,1,0:T(8,128)(2,1)S(1)} %pad_maximum_fusion.3), channel_id=1, source_target_pairs={{0,2},{2,0},{4,6},{6,4},{8,10},{10,8},{12,14},{14,12},{16,18},{18,... | collective-permute-start | bytes 3145736 | tf_op jit(solution)/shard_map/ppermute | solution.py:585
  179.1 13.0 %collective-permute-start.21 = (bf16[1,8,32,1024]{3,2,1,0:T(8,128)(2,1)S(1)}, bf16[1,8,32,1024]{3,2,1,0:T(8,128)(2,1)S(1)}, u32[]{:S(2)}, u32[]{:S(2)}) collective-permute-start(bf16[1,8,32,1024]{3,2,1,0:T(8,128)(2,1)S(1)} %pad_maximum_fusion.5), channel_id=1, source_target_pairs={{0,2},{2,0},{4,6},{6,4},{8,10},{10,8},{12,14},{14,12},{16,18},{18,... | collective-permute-start | bytes 1572872 | tf_op jit(solution)/shard_map/ppermute | solution.py:585
  230.4 25.4 %collective-permute-start.22 = (bf16[3,4,32,1024]{3,2,1,0:T(8,128)(2,1)}, bf16[3,4,32,1024]{3,2,1,0:T(8,128)(2,1)S(1)}, u32[]{:S(2)}, u32[]{:S(2)}) collective-permute-start(bf16[3,4,32,1024]{3,2,1,0:T(8,128)(2,1)} %get-tuple-element.274), channel_id=1, source_target_pairs={{0,2},{2,0},{4,6},{6,4},{8,10},{10,8},{12,14},{14,12},{16,18},{18,... | collective-permute-start | bytes 2359304 | tf_op jit(solution)/shard_map/ppermute | solution.py:585
  230.4 25.3 %copy-start.57 = (bf16[5,4,32,1024]{3,2,1,0:T(8,128)(2,1)S(1)}, bf16[5,4,32,1024]{3,2,1,0:T(8,128)(2,1)}, u32[]{:S(2)}) copy-start(bf16[5,4,32,1024]{3,2,1,0:T(8,128)(2,1)} %get-tuple-element.302) | copy-start | bytes 3932164
  255.8 47.5 %collective-permute-start.25 = (bf16[5,4,32,1024]{3,2,1,0:T(8,128)(2,1)S(1)}, bf16[5,4,32,1024]{3,2,1,0:T(8,128)(2,1)S(1)}, u32[]{:S(2)}, u32[]{:S(2)}) collective-permute-start(bf16[5,4,32,1024]{3,2,1,0:T(8,128)(2,1)S(1)} %copy-done.57), channel_id=1, source_target_pairs={{0,2},{2,0},{4,6},{6,4},{8,10},{10,8},{12,14},{14,12},{16,18},{18,... | collective-permute-start | bytes 3932168 | tf_op jit(solution)/shard_map/ppermute | solution.py:585
  255.8 47.3 %collective-permute-start.26 = (bf16[3,2,32,1024]{3,2,1,0:T(8,128)(2,1)}, bf16[3,2,32,1024]{3,2,1,0:T(8,128)(2,1)S(1)}, u32[]{:S(2)}, u32[]{:S(2)}) collective-permute-start(bf16[3,2,32,1024]{3,2,1,0:T(8,128)(2,1)} %get-tuple-element.303), channel_id=1, source_target_pairs={{0,2},{2,0},{4,6},{6,4},{8,10},{10,8},{12,14},{14,12},{16,18},{18,... | collective-permute-start | bytes 1179656 | tf_op jit(solution)/shard_map/ppermute | solution.py:585
  261.3 41.9 %collective-permute-start.23 = (bf16[3,2,32,1024]{3,2,1,0:T(8,128)(2,1)}, bf16[3,2,32,1024]{3,2,1,0:T(8,128)(2,1)S(1)}, u32[]{:S(2)}, u32[]{:S(2)}) collective-permute-start(bf16[3,2,32,1024]{3,2,1,0:T(8,128)(2,1)} %get-tuple-element.300), channel_id=1, source_target_pairs={{0,8},{2,10},{8,16},{10,18},{16,24},{18,26},{24,28},{26,30},{28,20... | collective-permute-start | bytes 1179656 | tf_op jit(solution)/shard_map/ppermute | solution.py:642
  285.5 17.7 %collective-permute-start.24 = (bf16[3,2,32,1024]{3,2,1,0:T(8,128)(2,1)}, bf16[3,2,32,1024]{3,2,1,0:T(8,128)(2,1)S(1)}, u32[]{:S(2)}, u32[]{:S(2)}) collective-permute-start(bf16[3,2,32,1024]{3,2,1,0:T(8,128)(2,1)} %get-tuple-element.301), channel_id=1, source_target_pairs={{0,4},{2,6},{8,0},{10,2},{16,8},{18,10},{24,16},{26,18},{28,24},{3... | collective-permute-start | bytes 1179656 | tf_op jit(solution)/shard_map/ppermute | solution.py:642
  308.3 29.2 %collective-permute-start.27 = (bf16[3,4,32,1024]{3,2,1,0:T(8,128)(2,1)}, bf16[3,4,32,1024]{3,2,1,0:T(8,128)(2,1)S(1)}, u32[]{:S(2)}, u32[]{:S(2)}) collective-permute-start(bf16[3,4,32,1024]{3,2,1,0:T(8,128)(2,1)} %get-tuple-element.325), channel_id=1, source_target_pairs={{0,8},{2,10},{8,16},{10,18},{16,24},{18,26},{24,28},{26,30},{28,20... | collective-permute-start | bytes 2359304 | tf_op jit(solution)/shard_map/ppermute | solution.py:642
  322.7 16.9 %collective-permute-start.28 = (bf16[3,4,32,1024]{3,2,1,0:T(8,128)(2,1)}, bf16[3,4,32,1024]{3,2,1,0:T(8,128)(2,1)S(1)}, u32[]{:S(2)}, u32[]{:S(2)}) collective-permute-start(bf16[3,4,32,1024]{3,2,1,0:T(8,128)(2,1)} %get-tuple-element.326), channel_id=1, source_target_pairs={{0,4},{2,6},{8,0},{10,2},{16,8},{18,10},{24,16},{26,18},{28,24},{3... | collective-permute-start | bytes 2359304 | tf_op jit(solution)/shard_map/ppermute | solution.py:642
  339.6 31.6 %collective-permute-start.29 = (bf16[8,208,1152]{2,1,0:T(8,128)(2,1)}, bf16[8,208,1152]{2,1,0:T(8,128)(2,1)S(1)}, u32[]{:S(2)}, u32[]{:S(2)}) collective-permute-start(bf16[8,208,1152]{2,1,0:T(8,128)(2,1)} %get-tuple-element.330), channel_id=1, source_target_pairs={{0,1},{1,0},{2,3},{3,2},{4,5},{5,4},{6,7},{7,6},{8,9},{9,8},{10,11... | collective-permute-start | bytes 11501576 | tf_op jit(solution)/shard_map/ppermute | solution.py:786
  344.7 26.5 %collective-permute-start.30 = (bf16[3,4,32,1024]{3,2,1,0:T(8,128)(2,1)}, bf16[3,4,32,1024]{3,2,1,0:T(8,128)(2,1)S(1)}, u32[]{:S(2)}, u32[]{:S(2)}) collective-permute-start(bf16[3,4,32,1024]{3,2,1,0:T(8,128)(2,1)} %get-tuple-element.336), channel_id=1, source_target_pairs={{0,8},{2,10},{8,16},{10,18},{16,24},{18,26},{24,28},{26,30},{28,20... | collective-permute-start | bytes 2359304 | tf_op jit(solution)/shard_map/ppermute | solution.py:642
  345.2 26.0 %collective-permute-start.31 = (bf16[3,4,32,1024]{3,2,1,0:T(8,128)(2,1)}, bf16[3,4,32,1024]{3,2,1,0:T(8,128)(2,1)}, u32[]{:S(2)}, u32[]{:S(2)}) collective-permute-start(bf16[3,4,32,1024]{3,2,1,0:T(8,128)(2,1)} %get-tuple-element.337), channel_id=1, source_target_pairs={{0,4},{2,6},{8,0},{10,2},{16,8},{18,10},{24,16},{26,18},{28,24},{3... | collective-permute-start | bytes 2359304 | tf_op jit(solution)/shard_map/ppermute | solution.py:642
  346.7 24.4 %collective-permute-start.32 = (bf16[5,2,32,1024]{3,2,1,0:T(8,128)(2,1)}, bf16[5,2,32,1024]{3,2,1,0:T(8,128)(2,1)S(1)}, u32[]{:S(2)}, u32[]{:S(2)}) collective-permute-start(bf16[5,2,32,1024]{3,2,1,0:T(8,128)(2,1)} %get-tuple-element.339), channel_id=1, source_target_pairs={{0,2},{2,0},{4,6},{6,4},{8,10},{10,8},{12,14},{14,12},{16,18},{18,... | collective-permute-start | bytes 1966088 | tf_op jit(solution)/shard_map/ppermute | solution.py:585
  348.4 22.8 %collective-permute-start.33 = (bf16[3,2,32,1024]{3,2,1,0:T(8,128)(2,1)S(1)}, bf16[3,2,32,1024]{3,2,1,0:T(8,128)(2,1)S(1)}, u32[]{:S(2)}, u32[]{:S(2)}) collective-permute-start(bf16[3,2,32,1024]{3,2,1,0:T(8,128)(2,1)S(1)} %copy-done.58), channel_id=1, source_target_pairs={{0,2},{2,0},{4,6},{6,4},{8,10},{10,8},{12,14},{14,12},{16,18},{18,... | collective-permute-start | bytes 1179656 | tf_op jit(solution)/shard_map/ppermute | solution.py:585
  377.3 33.5 %collective-permute-start.34 = (bf16[3,4,32,1024]{3,2,1,0:T(8,128)(2,1)}, bf16[3,4,32,1024]{3,2,1,0:T(8,128)(2,1)S(1)}, u32[]{:S(2)}, u32[]{:S(2)}) collective-permute-start(bf16[3,4,32,1024]{3,2,1,0:T(8,128)(2,1)} %get-tuple-element.367), channel_id=1, source_target_pairs={{0,8},{2,10},{8,16},{10,18},{16,24},{18,26},{24,28},{26,30},{28,20... | collective-permute-start | bytes 2359304 | tf_op jit(solution)/shard_map/ppermute | solution.py:642
  380.2 30.5 %collective-permute-start.35 = (bf16[3,4,32,1024]{3,2,1,0:T(8,128)(2,1)}, bf16[3,4,32,1024]{3,2,1,0:T(8,128)(2,1)S(1)}, u32[]{:S(2)}, u32[]{:S(2)}) collective-permute-start(bf16[3,4,32,1024]{3,2,1,0:T(8,128)(2,1)} %get-tuple-element.368), channel_id=1, source_target_pairs={{0,4},{2,6},{8,0},{10,2},{16,8},{18,10},{24,16},{26,18},{28,24},{3... | collective-permute-start | bytes 2359304 | tf_op jit(solution)/shard_map/ppermute | solution.py:642
  380.2 30.5 %collective-permute-start.38 = (bf16[5,2,32,1024]{3,2,1,0:T(8,128)(2,1)}, bf16[5,2,32,1024]{3,2,1,0:T(8,128)(2,1)S(1)}, u32[]{:S(2)}, u32[]{:S(2)}) collective-permute-start(bf16[5,2,32,1024]{3,2,1,0:T(8,128)(2,1)} %get-tuple-element.375), channel_id=1, source_target_pairs={{0,2},{2,0},{4,6},{6,4},{8,10},{10,8},{12,14},{14,12},{16,18},{18,... | collective-permute-start | bytes 1966088 | tf_op jit(solution)/shard_map/ppermute | solution.py:585
  384.8 25.9 %collective-permute-start.36 = (bf16[3,2,32,1024]{3,2,1,0:T(8,128)(2,1)}, bf16[3,2,32,1024]{3,2,1,0:T(8,128)(2,1)S(1)}, u32[]{:S(2)}, u32[]{:S(2)}) collective-permute-start(bf16[3,2,32,1024]{3,2,1,0:T(8,128)(2,1)} %get-tuple-element.373), channel_id=1, source_target_pairs={{0,8},{2,10},{8,16},{10,18},{16,24},{18,26},{24,28},{26,30},{28,20... | collective-permute-start | bytes 1179656 | tf_op jit(solution)/shard_map/ppermute | solution.py:642
  386.5 24.2 %collective-permute-start.37 = (bf16[3,2,32,1024]{3,2,1,0:T(8,128)(2,1)}, bf16[3,2,32,1024]{3,2,1,0:T(8,128)(2,1)S(1)}, u32[]{:S(2)}, u32[]{:S(2)}) collective-permute-start(bf16[3,2,32,1024]{3,2,1,0:T(8,128)(2,1)} %get-tuple-element.374), channel_id=1, source_target_pairs={{0,4},{2,6},{8,0},{10,2},{16,8},{18,10},{24,16},{26,18},{28,24},{3... | collective-permute-start | bytes 1179656 | tf_op jit(solution)/shard_map/ppermute | solution.py:642
  416.4 20.1 %collective-permute-start.39 = (bf16[3,4,32,1024]{3,2,1,0:T(8,128)(2,1)}, bf16[3,4,32,1024]{3,2,1,0:T(8,128)(2,1)S(1)}, u32[]{:S(2)}, u32[]{:S(2)}) collective-permute-start(bf16[3,4,32,1024]{3,2,1,0:T(8,128)(2,1)} %get-tuple-element.390), channel_id=1, source_target_pairs={{0,8},{2,10},{8,16},{10,18},{16,24},{18,26},{24,28},{26,30},{28,20... | collective-permute-start | bytes 2359304 | tf_op jit(solution)/shard_map/ppermute | solution.py:642
  416.5 20.1 %collective-permute-start.40 = (bf16[3,4,32,1024]{3,2,1,0:T(8,128)(2,1)}, bf16[3,4,32,1024]{3,2,1,0:T(8,128)(2,1)S(1)}, u32[]{:S(2)}, u32[]{:S(2)}) collective-permute-start(bf16[3,4,32,1024]{3,2,1,0:T(8,128)(2,1)} %get-tuple-element.391), channel_id=1, source_target_pairs={{0,4},{2,6},{8,0},{10,2},{16,8},{18,10},{24,16},{26,18},{28,24},{3... | collective-permute-start | bytes 2359304 | tf_op jit(solution)/shard_map/ppermute | solution.py:642
  442.3 20.0 %collective-permute-start.41 = (bf16[3,4,32,1024]{3,2,1,0:T(8,128)(2,1)}, bf16[3,4,32,1024]{3,2,1,0:T(8,128)(2,1)S(1)}, u32[]{:S(2)}, u32[]{:S(2)}) collective-permute-start(bf16[3,4,32,1024]{3,2,1,0:T(8,128)(2,1)} %get-tuple-element.406), channel_id=1, source_target_pairs={{0,8},{2,10},{8,16},{10,18},{16,24},{18,26},{24,28},{26,30},{28,20... | collective-permute-start | bytes 2359304 | tf_op jit(solution)/shard_map/ppermute | solution.py:642
  443.8 19.7 %copy-start.25 = (bf16[16,32,1152]{2,1,0:T(8,128)(2,1)S(1)}, bf16[16,32,1152]{2,1,0:T(8,128)(2,1)}, u32[]{:S(2)}) copy-start(bf16[16,32,1152]{2,1,0:T(8,128)(2,1)} %get-tuple-element.415) | copy-start | bytes 3538948
  443.8 19.7 %copy-start.27 = (bf16[16,32,1152]{2,1,0:T(8,128)(2,1)S(1)}, bf16[16,32,1152]{2,1,0:T(8,128)(2,1)}, u32[]{:S(2)}) copy-start(bf16[16,32,1152]{2,1,0:T(8,128)(2,1)} %get-tuple-element.416) | copy-start | bytes 3538948
  443.8 18.5 %collective-permute-start.42 = (bf16[3,4,32,1024]{3,2,1,0:T(8,128)(2,1)}, bf16[3,4,32,1024]{3,2,1,0:T(8,128)(2,1)S(1)}, u32[]{:S(2)}, u32[]{:S(2)}) collective-permute-start(bf16[3,4,32,1024]{3,2,1,0:T(8,128)(2,1)} %get-tuple-element.407), channel_id=1, source_target_pairs={{0,4},{2,6},{8,0},{10,2},{16,8},{18,10},{24,16},{26,18},{28,24},{3... | collective-permute-start | bytes 2359304 | tf_op jit(solution)/shard_map/ppermute | solution.py:642
  466.2 8.9 %collective-permute-start.49 = (bf16[16,32,1152]{2,1,0:T(8,128)(2,1)}, bf16[16,32,1152]{2,1,0:T(8,128)(2,1)S(1)}, u32[]{:S(2)}, u32[]{:S(2)}) collective-permute-start(bf16[16,32,1152]{2,1,0:T(8,128)(2,1)} %add_convert_fusion.1), channel_id=1, source_target_pairs={{0,1},{1,0},{2,3},{3,2},{4,5},{5,4},{6,7},{7,6},{8,9},{9,8},{10,11... | collective-permute-start | bytes 3538952 | tf_op jit(solution)/shard_map/ppermute | solution.py:786
  470.1 13.9 %collective-permute-start.58 = (bf16[4,32,1024]{2,1,0:T(8,128)(2,1)}, bf16[4,32,1024]{2,1,0:T(8,128)(2,1)S(1)}, u32[]{:S(2)}, u32[]{:S(2)}) collective-permute-start(bf16[4,32,1024]{2,1,0:T(8,128)(2,1)} %get-tuple-element.434), channel_id=1, source_target_pairs={{0,2},{2,0},{4,6},{6,4},{8,10},{10,8},{12,14},{14,12},{16,18},{18,... | collective-permute-start | bytes 786440 | tf_op jit(solution)/shard_map/ppermute | solution.py:585
  474.5 15.1 %collective-permute-start.43 = (bf16[4,208,512]{2,1,0:T(8,128)(2,1)}, bf16[4,208,512]{2,1,0:T(8,128)(2,1)}, u32[]{:S(2)}, u32[]{:S(2)}) collective-permute-start(bf16[4,208,512]{2,1,0:T(8,128)(2,1)} %get-tuple-element.376.refs_0_), channel_id=1, source_target_pairs={{0,1},{1,0},{2,3},{3,2},{4,5},{5,4},{6,7},{7,6},{8,9},{9,8},{10,11... | collective-permute-start | bytes 2555912 | tf_op jit(solution)/shard_map/ppermute | solution.py:786
  474.6 15.1 %collective-permute-start.46 = (bf16[4,208,512]{2,1,0:T(8,128)(2,1)}, bf16[4,208,512]{2,1,0:T(8,128)(2,1)}, u32[]{:S(2)}, u32[]{:S(2)}) collective-permute-start(bf16[4,208,512]{2,1,0:T(8,128)(2,1)} %get-tuple-element.409.refs_0_), channel_id=1, source_target_pairs={{0,1},{1,0},{2,3},{3,2},{4,5},{5,4},{6,7},{7,6},{8,9},{9,8},{10,11... | collective-permute-start | bytes 2555912 | tf_op jit(solution)/shard_map/ppermute | solution.py:786
  475.7 9.0 %collective-permute-start.52 = (bf16[2,32,1152]{2,1,0:T(8,128)(2,1)S(1)}, bf16[2,32,1152]{2,1,0:T(8,128)(2,1)S(1)}, u32[]{:S(2)}, u32[]{:S(2)}) collective-permute-start(bf16[2,32,1152]{2,1,0:T(8,128)(2,1)S(1)} %get-tuple-element.470), channel_id=1, source_target_pairs={{0,2},{2,0},{4,6},{6,4},{8,10},{10,8},{12,14},{14,12},{16,18},{18,... | collective-permute-start | bytes 442376 | tf_op jit(solution)/shard_map/ppermute | solution.py:585
  475.8 13.4 %collective-permute-start.50 = (bf16[2,32,1152]{2,1,0:T(8,128)(2,1)S(1)}, bf16[2,32,1152]{2,1,0:T(8,128)(2,1)S(1)}, u32[]{:S(2)}, u32[]{:S(2)}) collective-permute-start(bf16[2,32,1152]{2,1,0:T(8,128)(2,1)S(1)} %get-tuple-element.471), channel_id=1, source_target_pairs={{0,4},{2,6},{4,0},{6,2},{8,12},{10,14},{12,8},{14,10},{16,20},{18,... | collective-permute-start | bytes 442376 | tf_op jit(solution)/shard_map/ppermute | solution.py:585
  484.0 6.2 %collective-permute-start.44 = (bf16[2,208,512]{2,1,0:T(8,128)(2,1)S(1)}, bf16[2,208,512]{2,1,0:T(8,128)(2,1)S(1)}, u32[]{:S(2)}, u32[]{:S(2)}) collective-permute-start(bf16[2,208,512]{2,1,0:T(8,128)(2,1)S(1)} %copy-done.45), channel_id=1, source_target_pairs={{0,1},{1,0},{2,3},{3,2},{4,5},{5,4},{6,7},{7,6},{8,9},{9,8},{10,11... | collective-permute-start | bytes 1277960 | tf_op jit(solution)/shard_map/ppermute | solution.py:786
  484.7 23.1 %collective-permute-start.56 = (bf16[3,4,32,1024]{3,2,1,0:T(8,128)(2,1)}, bf16[3,4,32,1024]{3,2,1,0:T(8,128)(2,1)S(1)}, u32[]{:S(2)}, u32[]{:S(2)}) collective-permute-start(bf16[3,4,32,1024]{3,2,1,0:T(8,128)(2,1)} %get-tuple-element.430), channel_id=1, source_target_pairs={{0,8},{2,10},{8,16},{10,18},{16,24},{18,26},{24,28},{26,30},{28,20... | collective-permute-start | bytes 2359304 | tf_op jit(solution)/shard_map/ppermute | solution.py:642
  489.2 19.5 %collective-permute-start.57 = (bf16[3,4,32,1024]{3,2,1,0:T(8,128)(2,1)}, bf16[3,4,32,1024]{3,2,1,0:T(8,128)(2,1)S(1)}, u32[]{:S(2)}, u32[]{:S(2)}) collective-permute-start(bf16[3,4,32,1024]{3,2,1,0:T(8,128)(2,1)} %get-tuple-element.431), channel_id=1, source_target_pairs={{0,4},{2,6},{8,0},{10,2},{16,8},{18,10},{24,16},{26,18},{28,24},{3... | collective-permute-start | bytes 2359304 | tf_op jit(solution)/shard_map/ppermute | solution.py:642
  489.6 1.8 collective-permute-start.47
  489.7 2.5 collective-permute-start.45
  490.3 10.7 %collective-permute-start.48 = (bf16[2,208,512]{2,1,0:T(8,128)(2,1)S(1)}, bf16[2,208,512]{2,1,0:T(8,128)(2,1)S(1)}, u32[]{:S(2)}, u32[]{:S(2)}) collective-permute-start(bf16[2,208,512]{2,1,0:T(8,128)(2,1)S(1)} %copy-done.46), channel_id=1, source_target_pairs={{0,1},{1,0},{2,3},{3,2},{4,5},{5,4},{6,7},{7,6},{8,9},{9,8},{10,11... | collective-permute-start | bytes 1277960 | tf_op jit(solution)/shard_map/ppermute | solution.py:786
  491.4 25.7 %collective-permute-start.53 = (bf16[4,32,1152]{2,1,0:T(8,128)(2,1)}, bf16[4,32,1152]{2,1,0:T(8,128)(2,1)}, u32[]{:S(2)}, u32[]{:S(2)}) collective-permute-start(bf16[4,32,1152]{2,1,0:T(8,128)(2,1)} %pad_maximum_fusion.8), channel_id=1, source_target_pairs={{0,4},{2,6},{4,0},{6,2},{8,12},{10,14},{12,8},{14,10},{16,20},{18,... | collective-permute-start | bytes 884744 | tf_op jit(solution)/shard_map/ppermute | solution.py:585
  492.2 25.0 %collective-permute-start.51 = (bf16[4,32,1152]{2,1,0:T(8,128)(2,1)S(1)}, bf16[4,32,1152]{2,1,0:T(8,128)(2,1)S(1)}, u32[]{:S(2)}, u32[]{:S(2)}) collective-permute-start(bf16[4,32,1152]{2,1,0:T(8,128)(2,1)S(1)} %pad_maximum_fusion.7), channel_id=1, source_target_pairs={{0,2},{2,0},{4,6},{6,4},{8,10},{10,8},{12,14},{14,12},{16,18},{18,... | collective-permute-start | bytes 884744 | tf_op jit(solution)/shard_map/ppermute | solution.py:585
  513.5 8.2 %collective-permute-start.59 = (bf16[4,32,1024]{2,1,0:T(8,128)(2,1)}, bf16[4,32,1024]{2,1,0:T(8,128)(2,1)S(1)}, u32[]{:S(2)}, u32[]{:S(2)}) collective-permute-start(bf16[4,32,1024]{2,1,0:T(8,128)(2,1)} %get-tuple-element.436), channel_id=1, source_target_pairs={{0,2},{2,0},{4,6},{6,4},{8,10},{10,8},{12,14},{14,12},{16,18},{18,... | collective-permute-start | bytes 786440 | tf_op jit(solution)/shard_map/ppermute | solution.py:585
  518.3 5.2 collective-permute-start.54
  523.6 5.3 collective-permute-start.55
  (55 other events, 308.9 us)
